TPU v7x, 32 devices: a whole 2x2x4 slice. The times are simulated.
32 devices in a mesh: rep: 4 (over y, x), fsdp: 8 (over z, core).
Axes of the slice: x: 2, y: 2, z: 4, core: 2. Of those that a mesh axis runs over, the one named last changes fastest.
Arguments:
- tokens: bfloat16 [64, 128, 2048], P(('rep', 'fsdp')), may hold values from -6 to 6
- lengths: int32 [64], P(('rep', 'fsdp')), may hold values from 1 to 128, 6144 in all
- cotangent: bfloat16 [64, 128, 2048], P(('rep', 'fsdp')), may hold values from -6 to 6
- qkv_weight: bfloat16 [2048, 6144], P('fsdp'), may hold values from -0.125 to 0.125
- qv_bias: bfloat16 [4096], P('fsdp'), may hold values from -3 to 3
- out_weight: bfloat16 [2048, 2048], P('fsdp'), may hold values from -0.5 to 0.5
- out_bias: bfloat16 [2048], P('fsdp'), may hold values from -3 to 3
- attn_gain: bfloat16 [2048], P('fsdp'), may hold values from 0.5 to 1.5
- attn_shift: bfloat16 [2048], P('fsdp'), may hold values from -3 to 3
- up_weight: bfloat16 [2048, 8192], P('fsdp'), may hold values from -0.125 to 0.125
- up_bias: bfloat16 [8192], P('fsdp'), may hold values from -3 to 3
- down_weight: bfloat16 [8192, 2048], P('fsdp'), may hold values from -0.0625 to 0.0625
- down_bias: bfloat16 [2048], P('fsdp'), may hold values from -3 to 3
- ffn_gain: bfloat16 [2048], P('fsdp'), may hold values from 0.5 to 1.5
- ffn_shift: bfloat16 [2048], P('fsdp'), may hold values from -3 to 3
Outputs:
- output: bfloat16 [64, 128, 2048], P(('rep', 'fsdp'))
- input_grad: float32 [64, 128, 2048], P(('rep', 'fsdp'))
- qkv_weight_grad: float32 [2048, 6144], P('fsdp')
- qv_bias_grad: float32 [4096], P('fsdp')
- out_weight_grad: float32 [2048, 2048], P('fsdp')
- out_bias_grad: float32 [2048], P('fsdp')
- attn_gain_grad: float32 [2048], P('fsdp')
- attn_shift_grad: float32 [2048], P('fsdp')
- up_weight_grad: float32 [2048, 8192], P('fsdp')
- up_bias_grad: float32 [8192], P('fsdp')
- down_weight_grad: float32 [8192, 2048], P('fsdp')
- down_bias_grad: float32 [2048], P('fsdp')
- ffn_gain_grad: float32 [2048], P('fsdp')
- ffn_shift_grad: float32 [2048], P('fsdp')
Inputs may be any that keep to these rules, and one draw needn't show every extreme that they name: Slot i holds lengths[i] real tokens followed by padding; some slot is full.
All inputs are finite; a program needn't handle non-finite values. No bound on the sum of `lengths` on one device may be relied on, other than what follows from the above.
Results may differ from a plain program's by a relative error of at most 0.02.
Values may be sent and summed in bfloat16 or wider, within the bound.
No kernel may reach another device: no remote copies, remote signals or barrier semaphores. Data moves between devices by JAX's collectives and lax.ppermute only.
A program may use at most 576 MiB of HBM per device.

v0:
```python
from functools import partial

import jax
import jax.numpy as jnp
from jax import lax
from jax.sharding import PartitionSpec as P

D = 2048
HEADS = 16
HEAD_DIM = 128


eps_norm = 1e-05


def layer_norm(resid, gain, shift):
    center = resid - jnp.mean(resid, -1, keepdims=True)
    spread = jnp.mean(center * center, -1, keepdims=True)
    return center * lax.rsqrt(spread + eps_norm) * gain + shift


def contract_first(left, right):
    return lax.dot_general(
        left, right, (((0,), (0,)), ((), ())), preferred_element_type=jnp.float32
    )


def contract_last(left, right):
    return lax.dot_general(
        left, right, (((1,), (1,)), ((), ())), preferred_element_type=jnp.float32
    )


def column_sums(values):
    return jnp.sum(values.astype(jnp.float32), 0)


def join_rows(pieces):
    return jnp.concatenate(pieces, 0)


def per_device(
    tokens,
    lengths,
    cotangent,
    qkv_weight,
    qv_bias,
    out_weight,
    out_bias,
    attn_gain,
    attn_shift,
    up_weight,
    up_bias,
    down_weight,
    down_bias,
    ffn_gain,
    ffn_shift,
):
    micro_count = tokens.shape[0]
    seq_len = tokens.shape[1]
    factor = HEAD_DIM ** (-0.5)
    positions = jnp.arange(seq_len, dtype=jnp.int32)
    locals_all = (
        qkv_weight,
        qv_bias,
        out_weight,
        out_bias,
        attn_gain,
        attn_shift,
        up_weight,
        up_bias,
        down_weight,
        down_bias,
        ffn_gain,
        ffn_shift,
    )
    totals = [jnp.zeros(w.shape, jnp.float32) for w in locals_all]
    outputs = []
    input_grads = []
    keep_active, keep_branch, keep_first, keep_hidden = ([], [], [], [])
    keep_mixed, keep_attn, keep_inputs, keep_qkv = ([], [], [], [])
    norm_sums = [jnp.zeros((D,), jnp.float32) for _ in range(4)]
    for index in range(micro_count):
        attn_full = (
            lax.all_gather(qkv_weight, "fsdp", axis=0, tiled=True),
            lax.all_gather(qv_bias, "fsdp", axis=0, tiled=True),
            lax.all_gather(out_weight, "fsdp", axis=0, tiled=True),
            lax.all_gather(out_bias, "fsdp", axis=0, tiled=True),
            lax.all_gather(attn_gain, "fsdp", axis=0, tiled=True),
            lax.all_gather(attn_shift, "fsdp", axis=0, tiled=True),
        )
        ffn_full = (
            lax.all_gather(up_weight, "fsdp", axis=0, tiled=True),
            lax.all_gather(up_bias, "fsdp", axis=0, tiled=True),
            lax.all_gather(down_weight, "fsdp", axis=0, tiled=True),
            lax.all_gather(down_bias, "fsdp", axis=0, tiled=True),
            lax.all_gather(ffn_gain, "fsdp", axis=0, tiled=True),
            lax.all_gather(ffn_shift, "fsdp", axis=0, tiled=True),
        )
        w_qkv, b_qv, w_out, b_out, g_attn, s_attn = attn_full
        w_up, b_up, w_down, b_down, g_ffn, s_ffn = ffn_full
        b_qv = b_qv.astype(jnp.float32)
        inputs = tokens[index]
        valid = positions < lengths[index]
        qkv = jnp.dot(inputs, w_qkv, preferred_element_type=jnp.float32)
        query = (qkv[:, :D] + b_qv[:D]).astype(jnp.bfloat16).reshape(seq_len, HEADS, HEAD_DIM)
        keys = qkv[:, D : 2 * D].astype(jnp.bfloat16).reshape(seq_len, HEADS, HEAD_DIM)
        values = (qkv[:, 2 * D :] + b_qv[D:]).astype(jnp.bfloat16).reshape(seq_len, HEADS, HEAD_DIM)
        scores = (
            jnp.einsum("qhd,khd->hqk", query, keys, preferred_element_type=jnp.float32) * factor
        )
        scores = jnp.where(valid[None, None, :], scores, -1000000000.0)
        peak = jnp.max(scores, -1, keepdims=True)
        expo = jnp.exp(scores - peak)
        probs = expo / jnp.sum(expo, -1, keepdims=True)
        probs_low = probs.astype(jnp.bfloat16)
        mixed = jnp.einsum("hqk,khd->qhd", probs_low, values, preferred_element_type=jnp.float32)
        mixed = mixed.reshape(seq_len, D).astype(jnp.bfloat16)
        resid_one = (
            inputs.astype(jnp.float32)
            + jnp.dot(mixed, w_out, preferred_element_type=jnp.float32)
            + b_out.astype(jnp.float32)
        )
        first, norm_one_back = jax.vjp(
            layer_norm, resid_one, g_attn.astype(jnp.float32), s_attn.astype(jnp.float32)
        )
        first_low = first.astype(jnp.bfloat16)
        hidden = jnp.dot(first_low, w_up, preferred_element_type=jnp.float32) + b_up.astype(
            jnp.float32
        )
        active, gelu_back = jax.vjp(partial(jax.nn.gelu, approximate=True), hidden)
        active_low = active.astype(jnp.bfloat16)
        resid_two = (
            first
            + jnp.dot(active_low, w_down, preferred_element_type=jnp.float32)
            + b_down.astype(jnp.float32)
        )
        result, norm_two_back = jax.vjp(
            layer_norm, resid_two, g_ffn.astype(jnp.float32), s_ffn.astype(jnp.float32)
        )
        outputs.append(result.astype(jnp.bfloat16))
        grad_out = cotangent[index].astype(jnp.float32) * valid[:, None].astype(jnp.float32)
        grad_two, grad_gffn, grad_sffn = norm_two_back(grad_out)
        grad_branch = grad_two.astype(jnp.bfloat16)
        grad_active = contract_last(grad_branch, w_down)
        (grad_hidden,) = gelu_back(grad_active)
        grad_hidden = grad_hidden.astype(jnp.bfloat16)
        grad_first = grad_two + contract_last(grad_hidden, w_up)
        grad_one, grad_gattn, grad_sattn = norm_one_back(grad_first)
        grad_attn = grad_one.astype(jnp.bfloat16)
        grad_mixed = (
            contract_last(grad_attn, w_out).astype(jnp.bfloat16).reshape(seq_len, HEADS, HEAD_DIM)
        )
        grad_probs = jnp.einsum(
            "qhd,khd->hqk", grad_mixed, values, preferred_element_type=jnp.float32
        )
        grad_values = jnp.einsum(
            "hqk,qhd->khd", probs_low, grad_mixed, preferred_element_type=jnp.float32
        )
        row_dot = jnp.sum(probs * grad_probs, -1, keepdims=True)
        grad_scores = (probs * (grad_probs - row_dot)).astype(jnp.bfloat16)
        grad_query = (
            jnp.einsum("hqk,khd->qhd", grad_scores, keys, preferred_element_type=jnp.float32)
            * factor
        )
        grad_keys = (
            jnp.einsum("hqk,qhd->khd", grad_scores, query, preferred_element_type=jnp.float32)
            * factor
        )
        grad_query = grad_query.astype(jnp.bfloat16).reshape(seq_len, D)
        grad_keys = grad_keys.astype(jnp.bfloat16).reshape(seq_len, D)
        grad_values = grad_values.astype(jnp.bfloat16).reshape(seq_len, D)
        grad_qkv = jnp.concatenate([grad_query, grad_keys, grad_values], 1)
        input_grads.append(grad_one + contract_last(grad_qkv, w_qkv))
        keep_active.append(active_low)
        keep_branch.append(grad_branch)
        keep_first.append(first_low)
        keep_hidden.append(grad_hidden)
        keep_mixed.append(mixed)
        keep_attn.append(grad_attn)
        keep_inputs.append(inputs)
        keep_qkv.append(grad_qkv)
        norm_sums = [
            norm_sums[0] + grad_gffn,
            norm_sums[1] + grad_sffn,
            norm_sums[2] + grad_gattn,
            norm_sums[3] + grad_sattn,
        ]
    branch_all = join_rows(keep_branch)
    down_terms = (
        lax.psum_scatter(
            contract_first(join_rows(keep_active), branch_all).astype(jnp.bfloat16),
            "fsdp",
            scatter_dimension=0,
            tiled=True,
        ).astype(jnp.float32),
        lax.psum_scatter(
            column_sums(branch_all).astype(jnp.bfloat16), "fsdp", scatter_dimension=0, tiled=True
        ).astype(jnp.float32),
        lax.psum_scatter(
            norm_sums[0].astype(jnp.bfloat16), "fsdp", scatter_dimension=0, tiled=True
        ).astype(jnp.float32),
        lax.psum_scatter(
            norm_sums[1].astype(jnp.bfloat16), "fsdp", scatter_dimension=0, tiled=True
        ).astype(jnp.float32),
    )
    hidden_all = join_rows(keep_hidden)
    up_terms = (
        lax.psum_scatter(
            contract_first(join_rows(keep_first), hidden_all).astype(jnp.bfloat16),
            "fsdp",
            scatter_dimension=0,
            tiled=True,
        ).astype(jnp.float32),
        lax.psum_scatter(
            column_sums(hidden_all).astype(jnp.bfloat16), "fsdp", scatter_dimension=0, tiled=True
        ).astype(jnp.float32),
    )
    attn_all = join_rows(keep_attn)
    out_terms = (
        lax.psum_scatter(
            contract_first(join_rows(keep_mixed), attn_all).astype(jnp.bfloat16),
            "fsdp",
            scatter_dimension=0,
            tiled=True,
        ).astype(jnp.float32),
        lax.psum_scatter(
            column_sums(attn_all).astype(jnp.bfloat16), "fsdp", scatter_dimension=0, tiled=True
        ).astype(jnp.float32),
        lax.psum_scatter(
            norm_sums[2].astype(jnp.bfloat16), "fsdp", scatter_dimension=0, tiled=True
        ).astype(jnp.float32),
        lax.psum_scatter(
            norm_sums[3].astype(jnp.bfloat16), "fsdp", scatter_dimension=0, tiled=True
        ).astype(jnp.float32),
    )
    qkv_all = join_rows(keep_qkv)
    bias_terms = jnp.concatenate([column_sums(qkv_all[:, :D]), column_sums(qkv_all[:, 2 * D :])], 0)
    qkv_terms = (
        lax.psum_scatter(
            contract_first(join_rows(keep_inputs), qkv_all).astype(jnp.bfloat16),
            "fsdp",
            scatter_dimension=0,
            tiled=True,
        ).astype(jnp.float32),
        lax.psum_scatter(
            bias_terms.astype(jnp.bfloat16), "fsdp", scatter_dimension=0, tiled=True
        ).astype(jnp.float32),
    )
    totals = [
        qkv_terms[0],
        qkv_terms[1],
        out_terms[0],
        out_terms[1],
        out_terms[2],
        out_terms[3],
        up_terms[0],
        up_terms[1],
        down_terms[0],
        down_terms[1],
        down_terms[2],
        down_terms[3],
    ]
    summed = (
        lax.psum(totals[0].astype(jnp.bfloat16), "rep").astype(jnp.float32),
        lax.psum(totals[1].astype(jnp.bfloat16), "rep").astype(jnp.float32),
        lax.psum(totals[2].astype(jnp.bfloat16), "rep").astype(jnp.float32),
        lax.psum(totals[3].astype(jnp.bfloat16), "rep").astype(jnp.float32),
        lax.psum(totals[4].astype(jnp.bfloat16), "rep").astype(jnp.float32),
        lax.psum(totals[5].astype(jnp.bfloat16), "rep").astype(jnp.float32),
        lax.psum(totals[6].astype(jnp.bfloat16), "rep").astype(jnp.float32),
        lax.psum(totals[7].astype(jnp.bfloat16), "rep").astype(jnp.float32),
        lax.psum(totals[8].astype(jnp.bfloat16), "rep").astype(jnp.float32),
        lax.psum(totals[9].astype(jnp.bfloat16), "rep").astype(jnp.float32),
        lax.psum(totals[10].astype(jnp.bfloat16), "rep").astype(jnp.float32),
        lax.psum(totals[11].astype(jnp.bfloat16), "rep").astype(jnp.float32),
    )
    output = jnp.stack(outputs, 0)
    input_grad = jnp.stack(input_grads, 0)
    return (
        output,
        input_grad,
        summed[0],
        summed[1],
        summed[2],
        summed[3],
        summed[4],
        summed[5],
        summed[6],
        summed[7],
        summed[8],
        summed[9],
        summed[10],
        summed[11],
    )


def solution(mesh):
    return jax.shard_map(
        per_device,
        mesh=mesh,
        in_specs=(
            P(("rep", "fsdp"), None, None),
            P(("rep", "fsdp")),
            P(("rep", "fsdp"), None, None),
            P("fsdp", None),
            P("fsdp"),
            P("fsdp", None),
            P("fsdp"),
            P("fsdp"),
            P("fsdp"),
            P("fsdp", None),
            P("fsdp"),
            P("fsdp", None),
            P("fsdp"),
            P("fsdp"),
            P("fsdp"),
        ),
        out_specs=(
            P(("rep", "fsdp"), None, None),
            P(("rep", "fsdp"), None, None),
            P("fsdp", None),
            P("fsdp"),
            P("fsdp", None),
            P("fsdp"),
            P("fsdp"),
            P("fsdp"),
            P("fsdp", None),
            P("fsdp"),
            P("fsdp", None),
            P("fsdp"),
            P("fsdp"),
            P("fsdp"),
        ),
        check_vma=False,
    )
```

profile of v0, /device:TPU:0, one launch (start us, length us, event | category | flops | bytes accessed | tf_op | source)
XLA Modules:
  0.0 2282.0 jit_solution(7284855053095897092)
XLA Ops:
  23.6 20.8 all_gather.55
  54.3 16.9 all-gather.3
  83.8 18.9 all-gather.5
  115.1 31.8 %all-gather = bf16[8,1,512]{2,1,0:T(2,128)(2,1)S(1)} all-gather(bf16[1,1,512]{2,1,0:T(2,128)(2,1)S(1)} %reshape.249), channel_id=1, replica_groups=mesh['rep'=4,'fsdp'=8] {'fsdp'}, dimensions={0}, use_global_device_ids=true | all-gather | bytes 9216 | tf_op jit(solution)/shard_map/all_gather | solution.py:86
  150.2 82.6 %all-gather.12.cloned.1.call-done = bf16[2048,6144]{1,0:T(8,128)(2,1)} async-done(((bf16[256,6144]{1,0:T(8,128)(2,1)}), bf16[2048,6144]{1,0:T(8,128)(2,1)}) %all-gather.12.cloned.1.call-update) | async-done | bytes 25165840 | tf_op jit(solution)/shard_map/all_gather | solution.py:85
  264.4 50.3 %all-gather.14.cloned.1.call-done = bf16[2048,2048]{1,0:T(8,128)(2,1)} async-done(((bf16[256,2048]{1,0:T(8,128)(2,1)}), bf16[2048,2048]{1,0:T(8,128)(2,1)}) %all-gather.14.cloned.1.call-update) | async-done | bytes 8388624 | tf_op jit(solution)/shard_map/all_gather | solution.py:87
  323.9 279.6 %all-gather.16.cloned.1.call-done = bf16[2048,8192]{1,0:T(8,128)(2,1)} async-done(((bf16[256,8192]{1,0:T(8,128)(2,1)}), bf16[2048,8192]{1,0:T(8,128)(2,1)}) %all-gather.16.cloned.1.call-update) | async-done | bytes 33554448 | tf_op jit(solution)/shard_map/all_gather | solution.py:93
  603.5 19.3 multiply_convert_fusion.1
  622.8 269.0 %all-gather.18.cloned.1.call-done = bf16[8192,2048]{1,0:T(8,128)(2,1)} async-done(((bf16[1024,2048]{1,0:T(8,128)(2,1)}), bf16[8192,2048]{1,0:T(8,128)(2,1)}) %all-gather.18.cloned.1.call-update) | async-done | bytes 33554448 | tf_op jit(solution)/shard_map/all_gather | solution.py:95
  905.8 15.7 multiply_convert_fusion
  921.5 14.4 fusion.149
  941.3 19.1 fusion.132
  960.4 17.6 convolution_add_fusion.3
  978.0 19.0 fusion.134
  997.1 19.9 multiply_reduce_fusion.1
  1053.7 15.1 convolution_convert_fusion.2
  1070.7 15.4 convolution_convert_fusion.1
  1088.0 15.6 convolution_convert_fusion
  1114.3 247.7 %reduce-scatter.5.cloned.1.call-done = bf16[256,6144]{1,0:T(8,128)(2,1)} async-done(((bf16[2048,6144]{1,0:T(8,128)(2,1)}), bf16[256,6144]{1,0:T(8,128)(2,1)}) %reduce-scatter.5.cloned.1.call-update) | async-done | bytes 3145744 | tf_op jit(solution)/shard_map/reduce_scatter | solution.py:240
  1362.1 326.3 %reduce-scatter.9.cloned.1.call-done = bf16[256,8192]{1,0:T(8,128)(2,1)} async-done(((bf16[2048,8192]{1,0:T(8,128)(2,1)}), bf16[256,8192]{1,0:T(8,128)(2,1)}) %reduce-scatter.9.cloned.1.call-update) | async-done | bytes 4194320 | tf_op jit(solution)/shard_map/reduce_scatter | solution.py:209
  1688.4 326.4 %reduce-scatter.11.cloned.1.call-done = bf16[1024,2048]{1,0:T(8,128)(2,1)} async-done(((bf16[8192,2048]{1,0:T(8,128)(2,1)}), bf16[1024,2048]{1,0:T(8,128)(2,1)}) %reduce-scatter.11.cloned.1.call-update) | async-done | bytes 4194320 | tf_op jit(solution)/shard_map/reduce_scatter | solution.py:191
  2022.9 26.4 %all-reduce.8 = (bf16[4096]{0:T(1024)(128)(2,1)S(1)}, bf16[2048]{0:T(1024)(128)(2,1)S(1)}, bf16[2048]{0:T(1024)(128)(2,1)S(1)}, bf16[2048]{0:T(1024)(128)(2,1)S(...) all-reduce(bf16[4096]{0:T(1024)(128)(2,1)S(1)} %pad_maximum_fusion., ...), channel_id=3, replica_groups=mesh['rep'=4,'fsdp'=8] {'fsdp'}, use_global_device_ids=true, to_apply=%region_26.27.clone | all-reduce | flops 24576 | bytes 98304
  2066.2 14.6 fusion.33
  2096.1 163.0 %all-reduce.13.cloned.1.call-done = (bf16[256,6144]{1,0:T(8,128)(2,1)}, bf16[256,2048]{1,0:T(8,128)(2,1)}, bf16[256,8192]{1,0:T(8,128)(2,1)}, bf16[1024,2048]{1,0:T(8,128)(2,1)}) async-done(((bf16[256,6144]{1,0:T(8,128)(2,1)}, bf16[256,2048]{1,0:T(8,128)(2,1)}, bf16[256,8192]{1,0:T(8,128)(2,1)}, bf16[1024,2048]{1,0:T(8,128)(2,1)}), (bf16[256,6144]{1,0:T(8,128)(2,1)}, bf16[256,2048]{1,0:T(8,128)(2,1)}, ...) | async-done | bytes 12582928 | tf_op jit(solution)/shard_map/psum | solution.py:265
  (265 shorter events, 219.2 us)
Async XLA Ops:
  7.2 225.6 %all-gather.12.cloned.1.call-start = ((), (), s32[]{:S(2)}) async-start(), calls=%async_computation.4 | async-start | bytes 28311552 | tf_op jit(solution)/shard_map/all_gather | solution.py:85
  7.9 306.8 %all-gather.14.cloned.1.call-start = ((), (), s32[]{:S(2)}) async-start(), calls=%async_computation.5 | async-start | bytes 9437184 | tf_op jit(solution)/shard_map/all_gather | solution.py:87
  8.7 14.9 copy-start.53
  8.7 35.7 %copy-start.57 = (bf16[256]{0:T(256)(128)(2,1)S(1)}, bf16[256]{0:T(256)(128)(2,1)}, u32[]{:S(2)}) copy-start(bf16[256]{0:T(256)(128)(2,1)} %param.21) | copy-start | bytes 1540
  8.7 45.5 %copy-start.55 = (bf16[512]{0:T(512)(128)(2,1)S(1)}, bf16[512]{0:T(512)(128)(2,1)}, u32[]{:S(2)}) copy-start(bf16[512]{0:T(512)(128)(2,1)} %param.19) | copy-start | bytes 3076
  8.7 45.6 %copy-start.58 = (bf16[256]{0:T(256)(128)(2,1)S(1)}, bf16[256]{0:T(256)(128)(2,1)}, u32[]{:S(2)}) copy-start(bf16[256]{0:T(256)(128)(2,1)} %param.23) | copy-start | bytes 1540
  8.7 62.5 %copy-start.59 = (bf16[256]{0:T(256)(128)(2,1)S(1)}, bf16[256]{0:T(256)(128)(2,1)}, u32[]{:S(2)}) copy-start(bf16[256]{0:T(256)(128)(2,1)} %param.22) | copy-start | bytes 1540
  8.7 75.0 %copy-start.60 = (bf16[256]{0:T(256)(128)(2,1)S(1)}, bf16[256]{0:T(256)(128)(2,1)}, u32[]{:S(2)}) copy-start(bf16[256]{0:T(256)(128)(2,1)} %param.28) | copy-start | bytes 1540
  8.7 94.0 %copy-start.61 = (bf16[256]{0:T(256)(128)(2,1)S(1)}, bf16[256]{0:T(256)(128)(2,1)}, u32[]{:S(2)}) copy-start(bf16[256]{0:T(256)(128)(2,1)} %param.29) | copy-start | bytes 1540
  8.7 138.2 %copy-start.54 = (s32[2]{0:T(128)S(1)}, s32[2]{0:T(128)}, u32[]{:S(2)}) copy-start(s32[2]{0:T(128)} %param.16) | copy-start | bytes 28
  8.8 224.1 %copy-start.1 = (bf16[2,128,2048]{2,1,0:T(8,128)(2,1)S(1)}, bf16[2,128,2048]{2,1,0:T(8,128)(2,1)}, u32[]{:S(2)}) copy-start(bf16[2,128,2048]{2,1,0:T(8,128)(2,1)} %param.15) | copy-start | bytes 3145732
  8.8 594.7 %all-gather.16.cloned.1.call-start = ((), (), s32[]{:S(2)}) async-start(), calls=%async_computation.6 | async-start | bytes 37748736 | tf_op jit(solution)/shard_map/all_gather | solution.py:93
  9.5 882.3 %all-gather.18.cloned.1.call-start = ((), (), s32[]{:S(2)}) async-start(), calls=%async_computation.7 | async-start | bytes 37748736 | tf_op jit(solution)/shard_map/all_gather | solution.py:95
  10.1 1104.2 %reduce-scatter.7.cloned.1.call-start = ((), (), s32[]{:S(2)}) async-start(), calls=%async_computation.9 | async-start | bytes 9437184 | tf_op jit(solution)/shard_map/reduce_scatter | solution.py:221
  263.2 56.4 %copy-start.14 = (bf16[16,128,128]{2,1,0:T(8,128)(2,1)}, bf16[16,128,128]{2,1,0:T(8,128)(2,1)S(1)}, u32[]{:S(2)}) copy-start(bf16[16,128,128]{2,1,0:T(8,128)(2,1)S(1)} %convolution_convert_fusion.9) | copy-start | bytes 1572868
  921.5 14.7 copy-start.9
  1026.4 335.7 %reduce-scatter.5.cloned.1.call-start = ((), (), s32[]{:S(2)}) async-start(), calls=%async_computation.8 | async-start | bytes 28311552 | tf_op jit(solution)/shard_map/reduce_scatter | solution.py:240
  1037.4 15.5 copy-start.33
  1068.9 619.5 %reduce-scatter.9.cloned.1.call-start = ((), (), s32[]{:S(2)}) async-start(), calls=%async_computation.10 | async-start | bytes 37748736 | tf_op jit(solution)/shard_map/reduce_scatter | solution.py:209
  1086.2 928.6 %reduce-scatter.11.cloned.1.call-start = ((), (), s32[]{:S(2)}) async-start(), calls=%async_computation.11 | async-start | bytes 37748736 | tf_op jit(solution)/shard_map/reduce_scatter | solution.py:191
  1103.6 1155.5 %all-reduce.13.cloned.1.call-start = ((), (), s32[]{:S(2)}) async-start(), calls=%async_computation.12 | async-start | bytes 25165824 | tf_op jit(solution)/shard_map/psum | solution.py:265
  2014.8 50.4 %copy-start.31 = (bf16[1,128,2048]{2,1,0:T(8,128)(2,1)S(1)}, bf16[1,128,2048]{2,1,0:T(8,128)(2,1)}, u32[]{:S(2)}) copy-start(bf16[1,128,2048]{2,1,0:T(8,128)(2,1)} %get-tuple-element.75) | copy-start | bytes 1572868
  2014.8 50.4 %copy-start.32 = (bf16[1,128,2048]{2,1,0:T(8,128)(2,1)S(1)}, bf16[1,128,2048]{2,1,0:T(8,128)(2,1)}, u32[]{:S(2)}) copy-start(bf16[1,128,2048]{2,1,0:T(8,128)(2,1)} %get-tuple-element.76) | copy-start | bytes 1572868
  2014.8 51.4 %copy-start.13 = (f32[128,2048]{1,0:T(8,128)S(1)}, f32[128,2048]{1,0:T(8,128)}, u32[]{:S(2)}) copy-start(f32[128,2048]{1,0:T(8,128)} %copy-done.12) | copy-start | bytes 3145732
  (48 other events, 207.5 us)
Sparse Core Ops, SparseCore 0:
  9.7 223.1 all-gather.11
  234.4 80.2 all-gather.13
  316.3 287.1 all-gather.15
  604.9 286.8 all-gather.17
  1026.5 87.8 reduce-scatter.6
  1116.5 245.4 reduce-scatter.4
  1364.4 323.8 reduce-scatter.8
  1690.8 323.8 reduce-scatter.10
  2018.7 240.3 all-reduce.12
where the time goes:
time: 2290 us; the launch traced here: 2280 us
  waiting for transfers between devices  1760 us (77%)
  matrix products  273 us (12%)
  blocking collectives  174 us (8%)
  other arithmetic  42.6 us (2%)
    reduce_scatter x1, waiting for transfers between devices, per_device(): lax.psum_scatter(contract_first(join_rows(keep_active), branch_all).astyp...  326 us
    reduce_scatter x1, waiting for transfers between devices, per_device(): lax.psum_scatter(contract_first(join_rows(keep_first), hidden_all).astype...  326 us
    all_gather x1, waiting for transfers between devices, per_device(): lax.all_gather(up_weight, 'fsdp', axis=0, tiled=True)  280 us
    all_gather x1, waiting for transfers between devices, per_device(): lax.all_gather(down_weight, 'fsdp', axis=0, tiled=True)  269 us
    reduce_scatter x1, waiting for transfers between devices, per_device(): lax.psum_scatter(contract_first(join_rows(keep_inputs), qkv_all).astype(j...  248 us
    psum x1, waiting for transfers between devices, per_device(): lax.psum(totals[0].astype(jnp.bfloat16), 'rep').astype(jnp.float32)  163 us
    dot_general x8, matrix products, contract_last(): lax.dot_general(left, right, (((1,), (1,)), ((), ())), preferred_element_...  117 us
    all_gather x1, waiting for transfers between devices, per_device(): lax.all_gather(qkv_weight, 'fsdp', axis=0, tiled=True)  82.6 us
  transfers between devices with their start and end apart: 9, of which 9 were waited for; matrix products, arithmetic and copies ran while one was open for 8% of the time, Pallas kernels for 0%

commit v1 on v0

v1 whole, which is shorter than its diff:
```python
import jax
import jax.numpy as jnp
from jax import lax
from jax.experimental import pallas as pl
from jax.experimental.pallas import tpu as pltpu
from jax.sharding import PartitionSpec as P

D = 2048
HEADS = 16
HEAD_DIM = 128
EPS = 1e-05
BF = jnp.bfloat16
F32 = jnp.float32


def mm(a, b):
    return jnp.dot(a, b, preferred_element_type=F32)


def mm_nt(a, b):
    return lax.dot_general(a, b, (((1,), (1,)), ((), ())), preferred_element_type=F32)


def mm_tn(a, b):
    return lax.dot_general(a, b, (((0,), (0,)), ((), ())), preferred_element_type=F32)


def head_probs(q, k, length, factor):
    s = mm_nt(q, k) * factor
    cols = lax.broadcasted_iota(jnp.int32, s.shape, 1)
    s = jnp.where(cols < length, s, -1000000000.0)
    e = jnp.exp(s - jnp.max(s, -1, keepdims=True))
    return e / jnp.sum(e, -1, keepdims=True)


def attn_fwd_kernel(len_ref, qkv_ref, o_ref):
    width = o_ref.shape[1]
    length = len_ref[pl.program_id(0)]
    for h in range(width // HEAD_DIM):
        at = h * HEAD_DIM
        q = qkv_ref[:, at : at + HEAD_DIM]
        k = qkv_ref[:, width + at : width + at + HEAD_DIM]
        v = qkv_ref[:, 2 * width + at : 2 * width + at + HEAD_DIM]
        p = head_probs(q, k, length, HEAD_DIM**-0.5).astype(BF)
        o_ref[:, at : at + HEAD_DIM] = mm(p, v).astype(BF)


def attn_bwd_kernel(len_ref, qkv_ref, do_ref, dqkv_ref, sums_ref):
    width = do_ref.shape[1]
    factor = HEAD_DIM**-0.5
    length = len_ref[pl.program_id(0)]

    @pl.when(pl.program_id(0) == 0)
    def _():
        sums_ref[...] = jnp.zeros_like(sums_ref)

    for h in range(width // HEAD_DIM):
        at = h * HEAD_DIM
        q = qkv_ref[:, at : at + HEAD_DIM]
        k = qkv_ref[:, width + at : width + at + HEAD_DIM]
        v = qkv_ref[:, 2 * width + at : 2 * width + at + HEAD_DIM]
        do = do_ref[:, at : at + HEAD_DIM]
        p = head_probs(q, k, length, factor)
        dp = mm_nt(do, v)
        dv = mm_tn(p.astype(BF), do).astype(BF)
        ds = (p * (dp - jnp.sum(p * dp, -1, keepdims=True))).astype(BF)
        dq = (mm(ds, k) * factor).astype(BF)
        dk = (mm_tn(ds, q) * factor).astype(BF)
        for part, grad in ((0, dq), (1, dk), (2, dv)):
            cols = slice(part * width + at, part * width + at + HEAD_DIM)
            dqkv_ref[:, cols] = grad
            sums_ref[:, cols] += jnp.sum(grad.astype(F32), 0, keepdims=True)


def attn_fwd(lengths, qkv, seq):
    rows, wide = qkv.shape
    width = wide // 3
    return pl.pallas_call(
        attn_fwd_kernel,
        grid_spec=pltpu.PrefetchScalarGridSpec(
            num_scalar_prefetch=1,
            grid=(rows // seq,),
            in_specs=[pl.BlockSpec((seq, wide), lambda i, n: (i, 0))],
            out_specs=pl.BlockSpec((seq, width), lambda i, n: (i, 0)),
        ),
        out_shape=jax.ShapeDtypeStruct((rows, width), BF),
        cost_estimate=pl.CostEstimate(
            flops=4 * rows * seq * width, bytes_accessed=8 * rows * width, transcendentals=rows * seq * width // HEAD_DIM
        ),
    )(lengths, qkv)


def attn_bwd(lengths, qkv, do, seq):
    rows, wide = qkv.shape
    width = wide // 3
    return pl.pallas_call(
        attn_bwd_kernel,
        grid_spec=pltpu.PrefetchScalarGridSpec(
            num_scalar_prefetch=1,
            grid=(rows // seq,),
            in_specs=[
                pl.BlockSpec((seq, wide), lambda i, n: (i, 0)),
                pl.BlockSpec((seq, width), lambda i, n: (i, 0)),
            ],
            out_specs=[
                pl.BlockSpec((seq, wide), lambda i, n: (i, 0)),
                pl.BlockSpec((1, wide), lambda i, n: (0, 0)),
            ],
        ),
        out_shape=[jax.ShapeDtypeStruct((rows, wide), BF), jax.ShapeDtypeStruct((1, wide), F32)],
        cost_estimate=pl.CostEstimate(
            flops=10 * rows * seq * width, bytes_accessed=14 * rows * width, transcendentals=rows * seq * width // HEAD_DIM
        ),
    )(lengths, qkv, do)


def norm_forward(resid, gain, shift):
    center = resid - jnp.mean(resid, -1, keepdims=True)
    inv = lax.rsqrt(jnp.mean(center * center, -1, keepdims=True) + EPS)
    n = center * inv
    return n * gain + shift, n, inv


def norm_backward(g, gain, n, inv):
    dn = g * gain
    d = inv * (dn - jnp.mean(dn, -1, keepdims=True) - n * jnp.mean(dn * n, -1, keepdims=True))
    return d, jnp.sum(g * n, 0), jnp.sum(g, 0)


class Moves:
    def __init__(self, reps, shards):
        self.reps, self.shards = reps, shards
        self.square = reps == 4
        self.me = lax.axis_index("rep")
        self.xs = [(r, r ^ 1) for r in range(reps)]
        self.ys = [(r, r ^ 2) for r in range(reps)]
        self.ds = [(r, r ^ 3) for r in range(reps)]

    def over_x(self, a):
        return lax.ppermute(a, "rep", self.xs)

    def over_y(self, a):
        return lax.ppermute(a, "rep", self.ys)

    def owner(self, k):
        return self.me ^ k if self.square else k

    def gather_blocks(self, a):
        if not self.square:
            whole = lax.all_gather(a, "rep", axis=0, tiled=False)
            return [whole[k] for k in range(self.reps)]
        half = a.shape[0] // 2
        ax, ay = self.over_x(a), self.over_y(a)
        low, high = self.over_x(ay[:half]), self.over_y(ax[half:])
        return [a, ax, ay, jnp.concatenate([low, high], 0)]

    def gather_small(self, a):
        if not self.square:
            return lax.all_gather(a, "rep", axis=0, tiled=True)
        return jnp.concatenate([a, self.over_x(a), self.over_y(a), lax.ppermute(a, "rep", self.ds)], 0)

    def scatter_sum(self, part):
        if not self.square:
            whole = jnp.concatenate([part(k).astype(BF) for k in range(self.reps)], 0)
            return lax.psum_scatter(whole, "rep", scatter_dimension=0, tiled=True).astype(F32)
        d = part(3).astype(BF)
        half = d.shape[0] // 2
        for_y, for_x = self.over_x(d[:half]), self.over_y(d[half:])
        px, py = part(1), part(2)
        px = jnp.concatenate([px[:half], px[half:] + for_x.astype(F32)], 0).astype(BF)
        py = jnp.concatenate([py[:half] + for_y.astype(F32), py[half:]], 0).astype(BF)
        got_x, got_y = self.over_x(px), self.over_y(py)
        return part(0) + got_x.astype(F32) + got_y.astype(F32)

    def swap(self, a):
        return lax.all_to_all(a, "rep", 0, 0, tiled=True)

    def gather_weight(self, w):
        return lax.all_gather(w, "fsdp", axis=0, tiled=True)

    def scatter_weight(self, g):
        return lax.psum_scatter(g, "fsdp", scatter_dimension=0, tiled=True)


def per_device(
    tokens,
    lengths,
    cotangent,
    qkv_weight,
    qv_bias,
    out_weight,
    out_bias,
    attn_gain,
    attn_shift,
    up_weight,
    up_bias,
    down_weight,
    down_bias,
    ffn_gain,
    ffn_shift,
    reps,
    shards,
):
    mv = Moves(reps, shards)
    r = mv.me
    slots, seq, _ = tokens.shape
    rows = slots * seq
    ff = up_weight.shape[1]
    dr, fr = D // reps, ff // reps
    fpart = ff // (shards * reps)
    wrows = qkv_weight.shape[0]

    small = [qv_bias, out_bias, attn_gain, attn_shift, up_bias, down_bias, ffn_gain, ffn_shift]
    sizes = [s.shape[0] for s in small]
    packed = lax.all_gather(jnp.concatenate(small, 0), "fsdp", axis=0, tiled=False).astype(F32)
    full, at = [], 0
    for size in sizes:
        full.append(packed[:, at : at + size].reshape(-1))
        at += size
    b_qv, b_out, g_attn, s_attn, b_up, b_down, g_ffn, s_ffn = full
    bias_q = lax.dynamic_slice(b_qv, (r * dr,), (dr,))
    bias_v = lax.dynamic_slice(b_qv, (D + r * dr,), (dr,))
    bias_qkv = jnp.concatenate([bias_q, jnp.zeros_like(bias_q), bias_v], 0)
    bias_up = lax.dynamic_index_in_dim(b_up.reshape(shards, reps, fpart), r, 1, False).reshape(-1)

    qkv_own = lax.dynamic_index_in_dim(qkv_weight.reshape(wrows, 3, reps, dr), r, 2, False).reshape(wrows, 3 * dr)
    out_own = lax.dynamic_slice(out_weight, (0, r * dr), (wrows, dr))
    up_own = lax.dynamic_index_in_dim(up_weight.reshape(wrows, shards, reps, fpart), r, 2, False).reshape(wrows, fr)
    down_own = lax.dynamic_slice(down_weight, (r * fpart, 0), (fpart, D))
    w_qkv = mv.gather_weight(qkv_own)
    w_out_cols = mv.gather_weight(out_own)
    w_out = mv.swap(w_out_cols)
    w_out = w_out.reshape(reps, dr, dr).transpose(1, 0, 2).reshape(dr, D)
    w_up = mv.gather_weight(up_own)
    w_down = mv.gather_weight(down_own)

    x = tokens.reshape(rows, D)
    lens = mv.gather_small(lengths)
    x_all = jnp.concatenate(mv.gather_blocks(x), 0)
    qkv = (mm(x_all, w_qkv) + bias_qkv).astype(BF)
    o = attn_fwd(lens, qkv, seq)
    block = lambda a, k: a[k * rows : (k + 1) * rows]
    attn = mv.scatter_sum(lambda k: mm(block(o, k), w_out))
    x1, n1, inv1 = norm_forward(x.astype(F32) + attn + b_out, g_attn, s_attn)

    x1_all = jnp.concatenate(mv.gather_blocks(x1.astype(BF)), 0)
    hidden = mm(x1_all, w_up) + bias_up
    act, gelu_back = jax.vjp(lambda h: jax.nn.gelu(h, approximate=True), hidden)
    act = act.astype(BF)
    branch = mv.scatter_sum(lambda k: mm(block(act, k), w_down))
    result, n2, inv2 = norm_forward(x1 + branch + b_down, g_ffn, s_ffn)
    output = result.astype(BF).reshape(slots, seq, D)

    valid = (jnp.arange(seq, dtype=jnp.int32)[None, :] < lengths[:, None]).astype(F32)
    g = cotangent.reshape(rows, D).astype(F32) * valid.reshape(rows, 1)
    dr2, d_gffn, d_sffn = norm_backward(g, g_ffn, n2, inv2)
    df = dr2.astype(BF)
    df_all = jnp.concatenate(mv.gather_blocks(df), 0)
    d_wdown = mv.scatter_weight(mm_tn(act, df_all).astype(BF))
    d_bdown = jnp.sum(df.astype(F32), 0)
    (dh,) = gelu_back(mm_nt(df_all, w_down))
    dh = dh.astype(BF)
    d_wup = mv.scatter_weight(mm_tn(x1_all, dh).astype(BF))
    d_bup = jnp.sum(dh.astype(F32), 0)
    dx1 = dr2 + mv.scatter_sum(lambda k: mm_nt(block(dh, k), w_up))

    dr1, d_gattn, d_sattn = norm_backward(dx1, g_attn, n1, inv1)
    dt = dr1.astype(BF)
    dt_all = jnp.concatenate(mv.gather_blocks(dt), 0)
    d_bout = jnp.sum(dt.astype(F32), 0)
    d_wout = mm_tn(o, dt_all).astype(BF)
    d_wout = mv.swap(d_wout.reshape(dr, reps, dr).transpose(1, 0, 2).reshape(reps * dr, dr))
    d_wout = mv.scatter_weight(d_wout)
    do = mm_nt(dt_all, w_out).astype(BF)
    dqkv, sums = attn_bwd(lens, qkv, do, seq)
    d_wqkv = mv.scatter_weight(mm_tn(x_all, dqkv).astype(BF))
    input_grad = dr1 + mv.scatter_sum(lambda k: mm_nt(block(dqkv, k), w_qkv))
    input_grad = input_grad.reshape(slots, seq, D)

    def spread(shard, shape, at):
        total = jnp.zeros(shape, F32)
        for k, piece in enumerate(mv.gather_blocks(shard)):
            start = [0] * len(shape)
            start[at] = mv.owner(k)
            kept = list(shape)
            kept[at] = 1
            total = lax.dynamic_update_slice(total, piece.astype(F32).reshape(kept), start)
        return total

    d_wdown = spread(d_wdown, (reps, fpart, D), 0).reshape(down_weight.shape)
    d_wup = spread(d_wup, (wrows, shards, reps, fpart), 2).reshape(up_weight.shape)
    d_wout = spread(d_wout, (wrows, reps, dr), 1).reshape(out_weight.shape)
    d_wqkv = spread(d_wqkv, (wrows, 3, reps, dr), 2).reshape(qkv_weight.shape)

    zero = jnp.zeros((2, D), F32)
    d_qv = lax.dynamic_update_slice(zero, jnp.stack([sums[0, :dr], sums[0, 2 * dr :]]), (0, r * dr)).reshape(-1)
    d_bup = lax.dynamic_update_slice(
        jnp.zeros((shards, reps, fpart), F32), d_bup.reshape(shards, 1, fpart), (0, r, 0)
    ).reshape(-1)
    grads = [d_qv, d_bout, d_gattn, d_sattn, d_bup, d_bdown, d_gffn, d_sffn]
    packed = jnp.concatenate([v.reshape(shards, -1) for v in grads], 1)
    packed = lax.psum(packed, ("rep", "fsdp"))
    packed = lax.dynamic_index_in_dim(packed, lax.axis_index("fsdp"), 0, False)
    pieces, at = [], 0
    for size in sizes:
        pieces.append(packed[at : at + size])
        at += size
    d_qv, d_bout, d_gattn, d_sattn, d_bup, d_bdown, d_gffn, d_sffn = pieces
    return (
        output,
        input_grad,
        d_wqkv,
        d_qv,
        d_wout,
        d_bout,
        d_gattn,
        d_sattn,
        d_wup,
        d_bup,
        d_wdown,
        d_bdown,
        d_gffn,
        d_sffn,
    )


def solution(mesh):
    reps, shards = mesh.shape["rep"], mesh.shape["fsdp"]
    seqs = P(("rep", "fsdp"), None, None)
    mat, vec = P("fsdp", None), P("fsdp")

    def program(*args):
        return per_device(*args, reps=reps, shards=shards)

    params = (mat, vec, mat, vec, vec, vec, mat, vec, mat, vec, vec, vec)
    return jax.shard_map(
        program,
        mesh=mesh,
        in_specs=(seqs, P(("rep", "fsdp")), seqs) + params,
        out_specs=(seqs, seqs) + params,
        check_vma=False,
    )
```

time: 2290 us -> 1340 us (0.59)
  waiting for transfers between devices: 1760 us -> 574 us
  local copies, waits for them, and re-layouts: 16.2 us -> 436 us
  blocking collectives: 174 us -> 14.2 us
  matrix products: 273 us -> 149 us
  starting transfers between devices: 0.57 us -> 73.5 us
  Pallas kernels: 0 us -> 30.7 us
    reduce_scatter x4, waiting for transfers between devices: 911 us -> 260 us  [scatter_weight(): return lax.psum_scatter(g, 'fsdp', scatter_dimension=0, tiled=True)]
    all_gather x4, waiting for transfers between devices: 682 us -> 51.1 us  [gather_weight(): return lax.all_gather(w, 'fsdp', axis=0, tiled=True)]
    dynamic_update_slice x0 -> x11, local copies, waits for them, and re-layouts: none -> 303 us  [the longest x10 303 us: spread(): lax.dynamic_update_slice(total, piece.astype(F32).reshape(kept), start)]
    ppermute x0 -> x51, waiting for transfers between devices: none -> 214 us  [the longest x25 123 us: over_y(): return lax.ppermute(a, 'rep', self.ys)]
    all_gather x8 -> x1, blocking collectives: 137 us -> 14.2 us  [per_device(): lax.all_gather(jnp.concatenate(small, 0), 'fsdp', axis=0, tiled=False)]
    dot_general x30 -> x24, matrix products: 270 us -> 149 us  [the longest x10 58.7 us: mm_nt(): lax.dot_general(a, b, (((1,), (1,)), ((), ())), preferred_element_type=F32)]
    psum x1, waiting for transfers between devices: 163 us -> 48.3 us  [per_device(): packed = lax.psum(packed, ('rep', 'fsdp'))]
    ppermute x0 -> x51, starting transfers between devices: none -> 64.3 us  [the longest x25 35.2 us: over_y(): return lax.ppermute(a, 'rep', self.ys)]
  transfers between devices with their start and end apart: 9 -> 62, of which waited for: 9 -> 30; matrix products, arithmetic and copies ran while one was open for 8% -> 42% of each run, Pallas kernels for 0% -> 2%
where the time goes in v1:
time: 1340 us; the launch traced here: 1320 us
  waiting for transfers between devices  574 us (43%)
  local copies, waits for them, and re-layouts  436 us (33%)
  matrix products  149 us (11%)
  starting transfers between devices  73.5 us (5%)
  other arithmetic  31.9 us (2%)
  Pallas kernels  30.7 us (2%)
  between operations  15.2 us (1%)
  blocking collectives  14.2 us (1%)
    dynamic_update_slice x10, local copies, waits for them, and re-layouts, spread(): lax.dynamic_update_slice(total, piece.astype(F32).reshape(kept), start)  303 us
    reduce_scatter x4, waiting for transfers between devices, scatter_weight(): return lax.psum_scatter(g, 'fsdp', scatter_dimension=0, tiled=True)  260 us
    ppermute x25, waiting for transfers between devices, over_y(): return lax.ppermute(a, 'rep', self.ys)  123 us
    ppermute x25, waiting for transfers between devices, over_x(): return lax.ppermute(a, 'rep', self.xs)  90.8 us
    dot_general x10, matrix products, mm_nt(): lax.dot_general(a, b, (((1,), (1,)), ((), ())), preferred_element_type=F32)  58.7 us
    all_gather x4, waiting for transfers between devices, gather_weight(): return lax.all_gather(w, 'fsdp', axis=0, tiled=True)  51.1 us
    psum x1, waiting for transfers between devices, per_device(): packed = lax.psum(packed, ('rep', 'fsdp'))  48.3 us
    dot_general x10, matrix products, mm(): return jnp.dot(a, b, preferred_element_type=F32)  46.3 us
  transfers between devices with their start and end apart: 62, of which 30 were waited for; matrix products, arithmetic and copies ran while one was open for 42% of the time, Pallas kernels for 2%

profile of v1, /device:TPU:0, one launch (start us, length us, event | category | flops | bytes accessed | tf_op | source)
XLA Modules:
  0.0 1324.4 jit_solution(11437734474764561783)
XLA Ops:
  67.2 24.6 %collective-permute-done.5 = bf16[128,2048]{1,0:T(8,128)(2,1)S(1)} collective-permute-done((bf16[128,2048]{1,0:T(8,128)(2,1)S(1)}, bf16[128,2048]{1,0:T(8,128)(2,1)S(1)}, u32[]{:S(2)}, u32[]{:S(2)}) %collective-permute-start.5) | collective-permute-done | bytes 524320 | tf_op jit(solution)/shard_map/ppermute | solution.py:140
  153.6 21.3 %collective-permute-done.10 = bf16[256,2048]{1,0:T(8,128)(2,1)S(1)} collective-permute-done((bf16[256,2048]{1,0:T(8,128)(2,1)S(1)}, bf16[256,2048]{1,0:T(8,128)(2,1)S(1)}, u32[]{:S(2)}, u32[]{:S(2)}) %collective-permute-start.10) | collective-permute-done | bytes 1048608 | tf_op jit(solution)/shard_map/ppermute | solution.py:143
  181.7 21.3 %collective-permute-done.12 = bf16[256,2048]{1,0:T(8,128)(2,1)S(1)} collective-permute-done((bf16[256,2048]{1,0:T(8,128)(2,1)S(1)}, bf16[256,2048]{1,0:T(8,128)(2,1)S(1)}, u32[]{:S(2)}, u32[]{:S(2)}) %collective-permute-start.12) | collective-permute-done | bytes 1048608 | tf_op jit(solution)/shard_map/ppermute | solution.py:143
  217.2 17.4 %multiply_convert_fusion = (bf16[1024,2048]{1,0:T(8,128)(2,1)}, f32[1024,2048]{1,0:T(8,128)}) fusion(f32[2048]{0:T(1024)S(1)} %bitcast.192, bf16[1024,2048]{1,0:T(8,128)(2,1)} %constant_dynamic-update-slice_fusion.5, bf16[2048,2048]{0,1:T(8,128)(2,1)} %all-gather.10.cloned.1.call-done), kind=kOutput, calls=%fused_computation.10 | convolution fusion | flops 8610906112 | bytes 25174016 | tf_op jit(solution)/shard_map/dot_general | solution.py:17
  234.5 39.7 %all-gather.12.cloned.1.call-done = bf16[2048,2048]{1,0:T(8,128)(2,1)} async-done(((bf16[256,2048]{1,0:T(8,128)(2,1)}), bf16[2048,2048]{1,0:T(8,128)(2,1)}) %all-gather.12.cloned.1.call-update) | async-done | bytes 8388624 | tf_op jit(solution)/shard_map/all_gather | solution.py:179
  304.6 18.3 %collective-permute-done.18 = bf16[256,2048]{1,0:T(8,128)(2,1)S(1)} collective-permute-done((bf16[256,2048]{1,0:T(8,128)(2,1)S(1)}, bf16[256,2048]{1,0:T(8,128)(2,1)S(1)}, u32[]{:S(2)}, u32[]{:S(2)}) %collective-permute-start.18) | collective-permute-done | bytes 1048608 | tf_op jit(solution)/shard_map/ppermute | solution.py:143
  329.6 21.3 %collective-permute-done.20 = bf16[256,2048]{1,0:T(8,128)(2,1)S(1)} collective-permute-done((bf16[256,2048]{1,0:T(8,128)(2,1)S(1)}, bf16[256,2048]{1,0:T(8,128)(2,1)S(1)}, u32[]{:S(2)}, u32[]{:S(2)}) %collective-permute-start.20) | collective-permute-done | bytes 1048608 | tf_op jit(solution)/shard_map/ppermute | solution.py:143
  363.6 21.5 %convert_reduce_fusion = (f32[2048]{0:T(1024)S(1)}, bf16[1024,2048]{1,0:T(8,128)(2,1)}) fusion(f32[1024,2048]{1,0:T(8,128)} %get-tuple-element.68, f32[2048]{0:T(1024)S(1)} %bitcast.193, bf16[1024,2048]{1,0:T(8,128)(2,1)S(1)} %constant_dynamic-update-slice_fusion.10, bf16[2048,2048]{1,0:T(8,128)(2,1)} %all-gather.12.cloned.1.call-done), kind=kOutput, calls=%fused_computation.9 | convolution fusion | flops 8638167040 | bytes 25182208 | tf_op jit(solution)/shard_map/dot_general | solution.py:21
  413.8 17.4 %collective-permute-done.26 = bf16[256,2048]{1,0:T(8,128)(2,1)S(1)} collective-permute-done((bf16[256,2048]{1,0:T(8,128)(2,1)S(1)}, bf16[256,2048]{1,0:T(8,128)(2,1)S(1)}, u32[]{:S(2)}, u32[]{:S(2)}) %collective-permute-start.26) | collective-permute-done | bytes 1048608 | tf_op jit(solution)/shard_map/ppermute | solution.py:143
  438.9 20.3 %collective-permute-done.28 = bf16[256,2048]{1,0:T(8,128)(2,1)S(1)} collective-permute-done((bf16[256,2048]{1,0:T(8,128)(2,1)S(1)}, bf16[256,2048]{1,0:T(8,128)(2,1)S(1)}, u32[]{:S(2)}, u32[]{:S(2)}) %collective-permute-start.28) | collective-permute-done | bytes 1048608 | tf_op jit(solution)/shard_map/ppermute | solution.py:143
  490.8 17.0 %shard_map.255 = (bf16[1024,1536]{1,0:T(8,128)(2,1)}, f32[1,1536]{1,0:T(1,128)}) custom-call(s32[8]{0:T(128)} %pad_add_fusion.len_ref, bf16[1024,1536]{1,0:T(8,128)(2,1)} %add_convert_fusion.qkv_ref, bf16[1024,512]{1,0:T(8,128)(2,1)} %convolution_convert_fusion.8.do_ref), custom_call_target="tpu_custom_call" | custom-call | flops 671088640 | bytes 7340032 | tf_op jit(solution)/shard_map/pallas_call | solution.py:96
  580.7 48.3 %all-reduce.2.cloned.1.call-done = f32[8,3072]{1,0:T(8,128)} async-done(((f32[8,3072]{1,0:T(8,128)}), f32[8,3072]{1,0:T(8,128)}) %all-reduce.2.cloned.1.call-update) | async-done | bytes 98320 | tf_op jit(solution)/shard_map/psum | solution.py:302
  633.2 34.7 %reduce-scatter.7.cloned.1.call-done = bf16[256,512]{1,0:T(8,128)(2,1)} async-done(((bf16[2048,512]{1,0:T(8,128)(2,1)}), bf16[256,512]{1,0:T(8,128)(2,1)}) %reduce-scatter.7.cloned.1.call-update) | async-done | bytes 262160 | tf_op jit(solution)/shard_map/reduce_scatter | solution.py:182
  670.9 68.5 %reduce-scatter.5.cloned.1.call-done = bf16[256,1536]{1,0:T(8,128)(2,1)} async-done(((bf16[2048,1536]{1,0:T(8,128)(2,1)}), bf16[256,1536]{1,0:T(8,128)(2,1)}) %reduce-scatter.5.cloned.1.call-update) | async-done | bytes 786448 | tf_op jit(solution)/shard_map/reduce_scatter | solution.py:182
  761.2 69.0 %reduce-scatter.9.cloned.1.call-done = bf16[256,2048]{1,0:T(8,128)(2,1)} async-done(((bf16[2048,2048]{1,0:T(8,128)(2,1)}), bf16[256,2048]{1,0:T(8,128)(2,1)}) %reduce-scatter.9.cloned.1.call-update) | async-done | bytes 1048592 | tf_op jit(solution)/shard_map/reduce_scatter | solution.py:182
  833.2 87.9 %reduce-scatter.11.cloned.1.call-done = bf16[256,2048]{1,0:T(8,128)(2,1)} async-done(((bf16[2048,2048]{1,0:T(8,128)(2,1)}), bf16[256,2048]{1,0:T(8,128)(2,1)}) %reduce-scatter.11.cloned.1.call-update) | async-done | bytes 1048592 | tf_op jit(solution)/shard_map/reduce_scatter | solution.py:182
  948.1 28.5 %dynamic_update_slice.54 = f32[256,3,4,512]{3,2,1,0:T(4,128)} dynamic-update-slice(f32[256,3,4,512]{3,2,1,0:T(4,128)} %broadcast_in_dim.15, f32[256,3,1,512]{3,2,1,0:T(1,128)S(1)} %copy-done.9, s32[]{:T(128)} %constant.23.clone.1, s32[]{:T(128)} %constant.23.clone.1, s32[]{:T(128)S(6)} %select_n.25, s32[]{:T(128)} %constant.23.clone.1) | dynamic-update-slice | bytes 3145732 | tf_op jit(solution)/shard_map/dynamic_update_slice | solution.py:287
  983.8 28.7 %dynamic_update_slice.55 = f32[256,3,4,512]{3,2,1,0:T(4,128)} dynamic-update-slice(f32[256,3,4,512]{3,2,1,0:T(4,128)} %dynamic_update_slice.54, f32[256,3,1,512]{3,2,1,0:T(1,128)} %copy.82, s32[]{:T(128)} %constant.23.clone.1, s32[]{:T(128)} %constant.23.clone.1, s32[]{:T(128)S(6)} %select_n.53, s32[]{:T(128)} %constant.23.clone.1) | dynamic-update-slice | bytes 3145732 | tf_op jit(solution)/shard_map/dynamic_update_slice | solution.py:287
  1012.5 28.5 %dynamic_update_slice.56 = f32[256,3,4,512]{3,2,1,0:T(4,128)} dynamic-update-slice(f32[256,3,4,512]{3,2,1,0:T(4,128)} %dynamic_update_slice.55, f32[256,3,1,512]{3,2,1,0:T(1,128)S(1)} %copy-done.8, s32[]{:T(128)} %constant.23.clone.1, s32[]{:T(128)} %constant.23.clone.1, s32[]{:T(128)S(6)} %select_n.54, s32[]{:T(128)} %constant.23.clone.1) | dynamic-update-slice | bytes 3145732 | tf_op jit(solution)/shard_map/dynamic_update_slice | solution.py:287
  1051.4 44.2 %dynamic_update_slice.64 = f32[256,8,4,256]{3,2,1,0:T(4,128)} dynamic-update-slice(f32[256,8,4,256]{3,2,1,0:T(4,128)} %broadcast_in_dim.37, f32[256,8,1,256]{3,2,1,0:T(1,128)S(1)} %reshape.466, s32[]{:T(128)} %constant.23.clone.1, s32[]{:T(128)} %constant.23.clone.1, s32[]{:T(128)S(6)} %select_n.25, s32[]{:T(128)} %constant.23.clone.1) | dynamic-update-slice | bytes 4194308 | tf_op jit(solution)/shard_map/dynamic_update_slice | solution.py:287
  1106.8 28.6 %dynamic_update_slice.57 = f32[256,3,4,512]{3,2,1,0:T(4,128)} dynamic-update-slice(f32[256,3,4,512]{3,2,1,0:T(4,128)} %dynamic_update_slice.56, f32[256,3,1,512]{3,2,1,0:T(1,128)} %copy.87, s32[]{:T(128)} %constant.23.clone.1, s32[]{:T(128)} %constant.23.clone.1, s32[]{:T(128)S(6)} %select_n.55, s32[]{:T(128)} %constant.23.clone.1) | dynamic-update-slice | bytes 3145732 | tf_op jit(solution)/shard_map/dynamic_update_slice | solution.py:287
  1157.2 44.2 %dynamic_update_slice.65 = f32[256,8,4,256]{3,2,1,0:T(4,128)} dynamic-update-slice(f32[256,8,4,256]{3,2,1,0:T(4,128)} %dynamic_update_slice.64, f32[256,8,1,256]{3,2,1,0:T(1,128)S(1)} %reshape.467, s32[]{:T(128)} %constant.23.clone.1, s32[]{:T(128)} %constant.23.clone.1, s32[]{:T(128)S(6)} %select_n.53, s32[]{:T(128)} %constant.23.clone.1) | dynamic-update-slice | bytes 4194308 | tf_op jit(solution)/shard_map/dynamic_update_slice | solution.py:287
  1205.2 44.4 %dynamic_update_slice.66 = f32[256,8,4,256]{3,2,1,0:T(4,128)} dynamic-update-slice(f32[256,8,4,256]{3,2,1,0:T(4,128)} %dynamic_update_slice.65, f32[256,8,1,256]{3,2,1,0:T(1,128)S(1)} %reshape.468, s32[]{:T(128)} %constant.23.clone.1, s32[]{:T(128)} %constant.23.clone.1, s32[]{:T(128)S(6)} %select_n.54, s32[]{:T(128)} %constant.23.clone.1) | dynamic-update-slice | bytes 4194308 | tf_op jit(solution)/shard_map/dynamic_update_slice | solution.py:287
  1259.9 44.2 %dynamic_update_slice.67 = f32[256,8,4,256]{3,2,1,0:T(4,128)} dynamic-update-slice(f32[256,8,4,256]{3,2,1,0:T(4,128)} %dynamic_update_slice.66, f32[256,8,1,256]{3,2,1,0:T(1,128)S(1)} %copy.94, s32[]{:T(128)} %constant.23.clone.1, s32[]{:T(128)} %constant.23.clone.1, s32[]{:T(128)S(6)} %select_n.55, s32[]{:T(128)} %constant.23.clone.1) | dynamic-update-slice | bytes 4194308 | tf_op jit(solution)/shard_map/dynamic_update_slice | solution.py:287
  (396 shorter events, 469.4 us)
Async XLA Ops:
  9.2 99.9 %all-gather.6.cloned.1.call-start = ((), (), s32[]{:S(2)}) async-start(), calls=%async_computation.6 | async-start | bytes 7077888 | tf_op jit(solution)/shard_map/all_gather | solution.py:179
  15.9 201.2 %all-gather.10.cloned.1.call-start = ((), (), s32[]{:S(2)}) async-start(), calls=%async_computation.8 | async-start | bytes 9437184 | tf_op jit(solution)/shard_map/all_gather | solution.py:179
  24.8 249.4 %all-gather.12.cloned.1.call-start = ((), (), s32[]{:S(2)}) async-start(), calls=%async_computation.9 | async-start | bytes 9437184 | tf_op jit(solution)/shard_map/all_gather | solution.py:179
  485.3 143.8 %all-reduce.2.cloned.1.call-start = ((), (), s32[]{:S(2)}) async-start(), calls=%async_computation.11 | async-start | bytes 196608 | tf_op jit(solution)/shard_map/psum | solution.py:302
  509.3 158.6 %reduce-scatter.7.cloned.1.call-start = ((), (), s32[]{:S(2)}) async-start(), calls=%async_computation.12 | async-start | bytes 2359296 | tf_op jit(solution)/shard_map/reduce_scatter | solution.py:182
  509.9 229.5 %reduce-scatter.5.cloned.1.call-start = ((), (), s32[]{:S(2)}) async-start(), calls=%async_computation.10 | async-start | bytes 7077888 | tf_op jit(solution)/shard_map/reduce_scatter | solution.py:182
  521.4 308.8 %reduce-scatter.9.cloned.1.call-start = ((), (), s32[]{:S(2)}) async-start(), calls=%async_computation.13 | async-start | bytes 9437184 | tf_op jit(solution)/shard_map/reduce_scatter | solution.py:182
  535.9 385.2 %reduce-scatter.11.cloned.1.call-start = ((), (), s32[]{:S(2)}) async-start(), calls=%async_computation.14 | async-start | bytes 9437184 | tf_op jit(solution)/shard_map/reduce_scatter | solution.py:182
  570.2 170.6 %collective-permute-start.34 = (bf16[256,2048]{1,0:T(8,128)(2,1)}, bf16[256,2048]{1,0:T(8,128)(2,1)}, u32[]{:S(2)}, u32[]{:S(2)}) collective-permute-start(bf16[256,2048]{1,0:T(8,128)(2,1)} %pad_maximum_fusion.7), channel_id=1, source_target_pairs={{0,16},{8,24},{16,0},{24,8},{1,17},{9,25},{17,1},{25,9},{2,18},{10... | collective-permute-start | bytes 3145736 | tf_op jit(solution)/shard_map/ppermute | solution.py:143
  573.1 169.2 %collective-permute-start.32 = (bf16[256,2048]{1,0:T(8,128)(2,1)}, bf16[256,2048]{1,0:T(8,128)(2,1)}, u32[]{:S(2)}, u32[]{:S(2)}) collective-permute-start(bf16[256,2048]{1,0:T(8,128)(2,1)} %pad_maximum_fusion.6), channel_id=1, source_target_pairs={{0,8},{8,0},{16,24},{24,16},{1,9},{9,1},{17,25},{25,17},{2,10},{10... | collective-permute-start | bytes 3145736 | tf_op jit(solution)/shard_map/ppermute | solution.py:140
  667.9 81.0 %collective-permute-start.39 = (bf16[256,512]{1,0:T(8,128)(2,1)}, bf16[256,512]{1,0:T(8,128)(2,1)S(1)}, u32[]{:S(2)}, u32[]{:S(2)}) collective-permute-start(bf16[256,512]{1,0:T(8,128)(2,1)} %reduce-scatter.7.cloned.1.call-done), channel_id=1, source_target_pairs={{0,8},{8,0},{16,24},{24,16},{1,9},{9,1},{17,25},{25,17},{2,10},{10... | collective-permute-start | bytes 786440 | tf_op jit(solution)/shard_map/ppermute | solution.py:140
  669.3 80.2 %collective-permute-start.40 = (bf16[256,512]{1,0:T(8,128)(2,1)}, bf16[256,512]{1,0:T(8,128)(2,1)S(1)}, u32[]{:S(2)}, u32[]{:S(2)}) collective-permute-start(bf16[256,512]{1,0:T(8,128)(2,1)} %reduce-scatter.7.cloned.1.call-done), channel_id=1, source_target_pairs={{0,16},{8,24},{16,0},{24,8},{1,17},{9,25},{17,1},{25,9},{2,18},{10... | collective-permute-start | bytes 786440 | tf_op jit(solution)/shard_map/ppermute | solution.py:143
  740.8 181.7 %collective-permute-start.36 = (bf16[256,1536]{1,0:T(8,128)(2,1)}, bf16[256,1536]{1,0:T(8,128)(2,1)}, u32[]{:S(2)}, u32[]{:S(2)}) collective-permute-start(bf16[256,1536]{1,0:T(8,128)(2,1)} %reduce-scatter.5.cloned.1.call-done), channel_id=1, source_target_pairs={{0,16},{8,24},{16,0},{24,8},{1,17},{9,25},{17,1},{25,9},{2,18},{10... | collective-permute-start | bytes 2359304 | tf_op jit(solution)/shard_map/ppermute | solution.py:143
  748.9 82.8 %collective-permute-start.42 = (bf16[128,512]{1,0:T(8,128)(2,1)S(1)}, bf16[128,512]{1,0:T(8,128)(2,1)S(1)}, u32[]{:S(2)}, u32[]{:S(2)}) collective-permute-start(bf16[128,512]{1,0:T(8,128)(2,1)S(1)} %slice.391), channel_id=1, source_target_pairs={{0,16},{8,24},{16,0},{24,8},{1,17},{9,25},{17,1},{25,9},{2,18},{10... | collective-permute-start | bytes 393224 | tf_op jit(solution)/shard_map/ppermute | solution.py:143
  749.5 83.7 %collective-permute-start.41 = (bf16[128,512]{1,0:T(8,128)(2,1)S(1)}, bf16[128,512]{1,0:T(8,128)(2,1)S(1)}, u32[]{:S(2)}, u32[]{:S(2)}) collective-permute-start(bf16[128,512]{1,0:T(8,128)(2,1)S(1)} %slice.390), channel_id=1, source_target_pairs={{0,8},{8,0},{16,24},{24,16},{1,9},{9,1},{17,25},{25,17},{2,10},{10... | collective-permute-start | bytes 393224 | tf_op jit(solution)/shard_map/ppermute | solution.py:140
  758.9 336.7 %collective-permute-start.38 = (bf16[128,1536]{1,0:T(8,128)(2,1)}, bf16[128,1536]{1,0:T(8,128)(2,1)}, u32[]{:S(2)}, u32[]{:S(2)}) collective-permute-start(bf16[128,1536]{1,0:T(8,128)(2,1)} %slice.389), channel_id=1, source_target_pairs={{0,16},{8,24},{16,0},{24,8},{1,17},{9,25},{17,1},{25,9},{2,18},{10... | collective-permute-start | bytes 1179656 | tf_op jit(solution)/shard_map/ppermute | solution.py:143
  830.2 313.5 %collective-permute-start.43 = (bf16[256,2048]{1,0:T(8,128)(2,1)}, bf16[256,2048]{1,0:T(8,128)(2,1)S(1)}, u32[]{:S(2)}, u32[]{:S(2)}) collective-permute-start(bf16[256,2048]{1,0:T(8,128)(2,1)} %reduce-scatter.9.cloned.1.call-done), channel_id=1, source_target_pairs={{0,8},{8,0},{16,24},{24,16},{1,9},{9,1},{17,25},{25,17},{2,10},{10... | collective-permute-start | bytes 3145736 | tf_op jit(solution)/shard_map/ppermute | solution.py:140
  831.7 313.5 %collective-permute-start.44 = (bf16[256,2048]{1,0:T(8,128)(2,1)}, bf16[256,2048]{1,0:T(8,128)(2,1)}, u32[]{:S(2)}, u32[]{:S(2)}) collective-permute-start(bf16[256,2048]{1,0:T(8,128)(2,1)} %reduce-scatter.9.cloned.1.call-done), channel_id=1, source_target_pairs={{0,16},{8,24},{16,0},{24,8},{1,17},{9,25},{17,1},{25,9},{2,18},{10... | collective-permute-start | bytes 3145736 | tf_op jit(solution)/shard_map/ppermute | solution.py:143
  921.1 227.1 %collective-permute-start.47 = (bf16[256,2048]{1,0:T(8,128)(2,1)}, bf16[256,2048]{1,0:T(8,128)(2,1)}, u32[]{:S(2)}, u32[]{:S(2)}) collective-permute-start(bf16[256,2048]{1,0:T(8,128)(2,1)} %reduce-scatter.11.cloned.1.call-done), channel_id=1, source_target_pairs={{0,8},{8,0},{16,24},{24,16},{1,9},{9,1},{17,25},{25,17},{2,10},{10... | collective-permute-start | bytes 3145736 | tf_op jit(solution)/shard_map/ppermute | solution.py:140
  922.5 229.0 %collective-permute-start.48 = (bf16[256,2048]{1,0:T(8,128)(2,1)}, bf16[256,2048]{1,0:T(8,128)(2,1)}, u32[]{:S(2)}, u32[]{:S(2)}) collective-permute-start(bf16[256,2048]{1,0:T(8,128)(2,1)} %reduce-scatter.11.cloned.1.call-done), channel_id=1, source_target_pairs={{0,16},{8,24},{16,0},{24,8},{1,17},{9,25},{17,1},{25,9},{2,18},{10... | collective-permute-start | bytes 3145736 | tf_op jit(solution)/shard_map/ppermute | solution.py:143
  1144.6 110.7 %collective-permute-start.46 = (bf16[128,2048]{1,0:T(8,128)(2,1)}, bf16[128,2048]{1,0:T(8,128)(2,1)}, u32[]{:S(2)}, u32[]{:S(2)}) collective-permute-start(bf16[128,2048]{1,0:T(8,128)(2,1)} %slice.393), channel_id=1, source_target_pairs={{0,16},{8,24},{16,0},{24,8},{1,17},{9,25},{17,1},{25,9},{2,18},{10... | collective-permute-start | bytes 1572872 | tf_op jit(solution)/shard_map/ppermute | solution.py:143
  1147.0 109.4 %collective-permute-start.45 = (bf16[128,2048]{1,0:T(8,128)(2,1)}, bf16[128,2048]{1,0:T(8,128)(2,1)}, u32[]{:S(2)}, u32[]{:S(2)}) collective-permute-start(bf16[128,2048]{1,0:T(8,128)(2,1)} %slice.392), channel_id=1, source_target_pairs={{0,8},{8,0},{16,24},{24,16},{1,9},{9,1},{17,25},{25,17},{2,10},{10... | collective-permute-start | bytes 1572872 | tf_op jit(solution)/shard_map/ppermute | solution.py:140
  1150.0 164.8 %collective-permute-start.50 = (bf16[128,2048]{1,0:T(8,128)(2,1)}, bf16[128,2048]{1,0:T(8,128)(2,1)}, u32[]{:S(2)}, u32[]{:S(2)}) collective-permute-start(bf16[128,2048]{1,0:T(8,128)(2,1)} %slice.395), channel_id=1, source_target_pairs={{0,16},{8,24},{16,0},{24,8},{1,17},{9,25},{17,1},{25,9},{2,18},{10... | collective-permute-start | bytes 1572872 | tf_op jit(solution)/shard_map/ppermute | solution.py:143
  1153.4 161.5 %collective-permute-start.49 = (bf16[128,2048]{1,0:T(8,128)(2,1)}, bf16[128,2048]{1,0:T(8,128)(2,1)}, u32[]{:S(2)}, u32[]{:S(2)}) collective-permute-start(bf16[128,2048]{1,0:T(8,128)(2,1)} %slice.394), channel_id=1, source_target_pairs={{0,8},{8,0},{16,24},{24,16},{1,9},{9,1},{17,25},{25,17},{2,10},{10... | collective-permute-start | bytes 1572872 | tf_op jit(solution)/shard_map/ppermute | solution.py:140
  (76 other events, 1451.5 us)
Sparse Core Ops, SparseCore 0:
  10.2 31.8 all-gather.7
  44.2 64.7 all-gather.5
  111.2 80.6 all-gather.9
  193.9 80.2 all-gather.11
  509.4 119.5 all-reduce.1
  631.2 36.6 reduce-scatter.6
  670.8 68.5 reduce-scatter.4
  742.2 87.9 reduce-scatter.8
  833.1 87.9 reduce-scatter.10

commit v2 on v1

--- a/solution.py
+++ b/solution.py
@@ -114,6 +114,241 @@
     )(lengths, qkv, do)
 
 
+def pick_attn_kernel(me_ref, qkv, out, kept):
+    p = pl.program_id(0)
+
+    @pl.when(p < 3)
+    def _():
+        kept[...] = qkv[...]
+
+    @pl.when(p == 3)
+    def _():
+        kept[...] = out[...]
+
+
+def pick_attn(me, qkv_weight, out_weight, reps):
+    rows, width = out_weight.shape[0], out_weight.shape[1] // reps
+    return pl.pallas_call(
+        pick_attn_kernel,
+        grid_spec=pltpu.PrefetchScalarGridSpec(
+            num_scalar_prefetch=1,
+            grid=(4,),
+            in_specs=[
+                pl.BlockSpec((rows, width), lambda p, m: (0, jnp.minimum(p, 2) * reps + m[0])),
+                pl.BlockSpec((rows, width), lambda p, m: (0, m[0])),
+            ],
+            out_specs=pl.BlockSpec((rows, width), lambda p, m: (0, p)),
+        ),
+        out_shape=jax.ShapeDtypeStruct((rows, 4 * width), BF),
+        cost_estimate=pl.CostEstimate(flops=0, bytes_accessed=16 * rows * width, transcendentals=0),
+    )(me.reshape(1), qkv_weight, out_weight)
+
+
+def pick_ffn_kernel(me_ref, up, down, up_kept, down_kept):
+    up_kept[...] = up[...]
+    down_kept[...] = down[...]
+
+
+def pick_ffn(me, up_weight, down_weight, reps, shards):
+    rows, ff = up_weight.shape
+    width = ff // (reps * shards)
+    tall, dim = down_weight.shape[0] // reps, down_weight.shape[1]
+    tile = dim // shards
+    return pl.pallas_call(
+        pick_ffn_kernel,
+        grid_spec=pltpu.PrefetchScalarGridSpec(
+            num_scalar_prefetch=1,
+            grid=(shards,),
+            in_specs=[
+                pl.BlockSpec((rows, width), lambda p, m: (0, p * reps + m[0])),
+                pl.BlockSpec((tall, tile), lambda p, m: (m[0], p)),
+            ],
+            out_specs=[
+                pl.BlockSpec((rows, width), lambda p, m: (0, p)),
+                pl.BlockSpec((tall, tile), lambda p, m: (0, p)),
+            ],
+        ),
+        out_shape=[jax.ShapeDtypeStruct((rows, ff // reps), BF), jax.ShapeDtypeStruct((tall, dim), BF)],
+        cost_estimate=pl.CostEstimate(flops=0, bytes_accessed=8 * rows * width * shards, transcendentals=0),
+    )(me.reshape(1), up_weight, down_weight)
+
+
+def place_cols_kernel(me_ref, own, ax, ay, low, high, out):
+    width = own.shape[1]
+    me = me_ref[0]
+
+    def put(k, value):
+        out[:, pl.ds(pl.multiple_of((me ^ k) * width, width), width)] = value.astype(out.dtype)
+
+    put(0, own[...])
+    put(1, ax[...])
+    put(2, ay[...])
+
+    @pl.when(pl.program_id(1) == 0)
+    def _():
+        put(3, low[...])
+
+    @pl.when(pl.program_id(1) == 1)
+    def _():
+        put(3, high[...])
+
+
+def place_cols(me, pieces, parts, dtype=F32):
+    own, low = pieces[0], pieces[3]
+    rows, cols = own.shape
+    width, half = cols // parts, rows // 2
+    tile = pl.BlockSpec((half, width), lambda p, t, m: (t, p))
+    part = pl.BlockSpec((half, width), lambda p, t, m: (0, p))
+    return pl.pallas_call(
+        place_cols_kernel,
+        grid_spec=pltpu.PrefetchScalarGridSpec(
+            num_scalar_prefetch=1,
+            grid=(parts, 2),
+            in_specs=[tile, tile, tile, part, part],
+            out_specs=pl.BlockSpec((half, 4 * width), lambda p, t, m: (t, p)),
+        ),
+        out_shape=jax.ShapeDtypeStruct((rows, 4 * cols), dtype),
+        cost_estimate=pl.CostEstimate(flops=0, bytes_accessed=24 * rows * cols, transcendentals=0),
+    )(me.reshape(1), *pieces)
+
+
+def join_attn_kernel(me_ref, qkv, own, ax, ay, low, high, joined):
+    k = pl.program_id(0)
+    wide, half = qkv.shape[1], low.shape[0]
+    joined[:, :wide] = qkv[...]
+
+    @pl.when(k == 0)
+    def _():
+        joined[:, wide:] = own[...]
+
+    @pl.when(k == 1)
+    def _():
+        joined[:, wide:] = ax[...]
+
+    @pl.when(k == 2)
+    def _():
+        joined[:, wide:] = ay[...]
+
+    @pl.when(k == 3)
+    def _():
+        joined[:half, wide:] = low[...]
+        joined[half:, wide:] = high[...]
+
+
+def join_attn(me, qkv, pieces):
+    own, low = pieces[0], pieces[3]
+    rows, cols = own.shape
+    wide = qkv.shape[1]
+    full = pl.BlockSpec((rows, cols), lambda k, m: (0, 0))
+    part = pl.BlockSpec((low.shape[0], cols), lambda k, m: (0, 0))
+    return pl.pallas_call(
+        join_attn_kernel,
+        grid_spec=pltpu.PrefetchScalarGridSpec(
+            num_scalar_prefetch=1,
+            grid=(4,),
+            in_specs=[pl.BlockSpec((rows, wide), lambda k, m: (m[0] ^ k, 0)), full, full, full, part, part],
+            out_specs=pl.BlockSpec((rows, wide + cols), lambda k, m: (m[0] ^ k, 0)),
+        ),
+        out_shape=jax.ShapeDtypeStruct((4 * rows, wide + cols), BF),
+        cost_estimate=pl.CostEstimate(flops=0, bytes_accessed=16 * rows * (wide + cols), transcendentals=0),
+    )(me.reshape(1), qkv, *pieces)
+
+
+def place_attn_kernel(me_ref, own, ax, ay, low, high, qkv, out):
+    width = own.shape[1]
+    me = me_ref[0]
+    p, t = pl.program_id(0), pl.program_id(1)
+
+    def put(k, value):
+        at = pl.ds(pl.multiple_of((me ^ k) * width, width), width)
+
+        @pl.when(p < 3)
+        def _():
+            qkv[:, at] = value.astype(F32)
+
+        @pl.when(p == 3)
+        def _():
+            out[:, at] = value.astype(F32)
+
+    put(0, own[...])
+    put(1, ax[...])
+    put(2, ay[...])
+
+    @pl.when(t == 0)
+    def _():
+        put(3, low[...])
+
+    @pl.when(t == 1)
+    def _():
+        put(3, high[...])
+
+
+def place_attn(me, pieces):
+    own, low = pieces[0], pieces[3]
+    rows, cols = own.shape
+    width, half = cols // 4, rows // 2
+    tile = pl.BlockSpec((half, width), lambda p, t, m: (t, p))
+    part = pl.BlockSpec((half, width), lambda p, t, m: (0, p))
+    return pl.pallas_call(
+        place_attn_kernel,
+        grid_spec=pltpu.PrefetchScalarGridSpec(
+            num_scalar_prefetch=1,
+            grid=(4, 2),
+            in_specs=[tile, tile, tile, part, part],
+            out_specs=[
+                pl.BlockSpec((half, cols), lambda p, t, m: (jnp.where(p < 3, t, 1), jnp.minimum(p, 2))),
+                pl.BlockSpec((half, cols), lambda p, t, m: (jnp.where(p < 3, 0, t), 0)),
+            ],
+        ),
+        out_shape=[jax.ShapeDtypeStruct((rows, 3 * cols), F32), jax.ShapeDtypeStruct((rows, cols), F32)],
+        cost_estimate=pl.CostEstimate(flops=0, bytes_accessed=24 * rows * cols, transcendentals=0),
+    )(me.reshape(1), *pieces)
+
+
+def place_rows_kernel(me_ref, own, ax, ay, low, high, out):
+    k = pl.program_id(0)
+    half = low.shape[0]
+
+    @pl.when(k == 0)
+    def _():
+        out[...] = own[...].astype(out.dtype)
+
+    @pl.when(k == 1)
+    def _():
+        out[...] = ax[...].astype(out.dtype)
+
+    @pl.when(k == 2)
+    def _():
+        out[...] = ay[...].astype(out.dtype)
+
+    @pl.when(k == 3)
+    def _():
+        out[:half] = low[...].astype(out.dtype)
+        out[half:] = high[...].astype(out.dtype)
+
+
+def place_rows(me, pieces, dtype=F32):
+    own, low = pieces[0], pieces[3]
+    rows, cols = own.shape
+    full = pl.BlockSpec((rows, cols), lambda k, m: (0, 0))
+    part = pl.BlockSpec((low.shape[0], cols), lambda k, m: (0, 0))
+    return pl.pallas_call(
+        place_rows_kernel,
+        grid_spec=pltpu.PrefetchScalarGridSpec(
+            num_scalar_prefetch=1,
+            grid=(4,),
+            in_specs=[full, full, full, part, part],
+            out_specs=pl.BlockSpec((rows, cols), lambda k, m: (m[0] ^ k, 0)),
+        ),
+        out_shape=jax.ShapeDtypeStruct((4 * rows, cols), dtype),
+        cost_estimate=pl.CostEstimate(flops=0, bytes_accessed=24 * rows * cols, transcendentals=0),
+    )(me.reshape(1), *pieces)
+
+
+def after(value, *deps):
+    return lax.optimization_barrier((value,) + deps)[0]
+
+
 def norm_forward(resid, gain, shift):
     center = resid - jnp.mean(resid, -1, keepdims=True)
     inv = lax.rsqrt(jnp.mean(center * center, -1, keepdims=True) + EPS)
@@ -142,41 +377,68 @@
     def over_y(self, a):
         return lax.ppermute(a, "rep", self.ys)
 
-    def owner(self, k):
-        return self.me ^ k if self.square else k
-
-    def gather_blocks(self, a):
+    def gather_near(self, a):
+        return a, self.over_x(a), self.over_y(a)
+
+    def gather_far(self, near):
+        own, ax, ay = near
+        half = own.shape[0] // 2
+        return [own, ax, ay, self.over_x(ay[:half]), self.over_y(ax[half:])]
+
+    def gather_pieces(self, a, *meanwhile):
+        near = self.gather_near(a)
+        if meanwhile:
+            near = lax.optimization_barrier(near + meanwhile)[:3]
+        return self.gather_far(near)
+
+    def gather_rows(self, a):
         if not self.square:
-            whole = lax.all_gather(a, "rep", axis=0, tiled=False)
-            return [whole[k] for k in range(self.reps)]
-        half = a.shape[0] // 2
-        ax, ay = self.over_x(a), self.over_y(a)
-        low, high = self.over_x(ay[:half]), self.over_y(ax[half:])
-        return [a, ax, ay, jnp.concatenate([low, high], 0)]
+            return lax.all_gather(a, "rep", axis=0, tiled=True)
+        return jnp.concatenate(self.gather_pieces(a), 0)
 
     def gather_small(self, a):
         if not self.square:
             return lax.all_gather(a, "rep", axis=0, tiled=True)
         return jnp.concatenate([a, self.over_x(a), self.over_y(a), lax.ppermute(a, "rep", self.ds)], 0)
 
-    def scatter_sum(self, part):
+    def far_term(self, left, right, product):
+        rows = left.shape[0] // self.reps
+        return product(left[3 * rows : 4 * rows], right).astype(BF) if self.square else None
+
+    def scatter_sum(self, left, right, product, far, late=()):
+        rows = left.shape[0] // self.reps
+        block = lambda a, k: product(a[k * rows : (k + 1) * rows], right)
         if not self.square:
-            whole = jnp.concatenate([part(k).astype(BF) for k in range(self.reps)], 0)
+            whole = jnp.concatenate([block(left, k).astype(BF) for k in range(self.reps)], 0)
             return lax.psum_scatter(whole, "rep", scatter_dimension=0, tiled=True).astype(F32)
-        d = part(3).astype(BF)
-        half = d.shape[0] // 2
-        for_y, for_x = self.over_x(d[:half]), self.over_y(d[half:])
-        px, py = part(1), part(2)
+        half = rows // 2
+        for_y, for_x = self.over_x(far[:half]), self.over_y(far[half:])
+        left = after(left, far)
+        px, py = block(left, 1), block(left, 2)
         px = jnp.concatenate([px[:half], px[half:] + for_x.astype(F32)], 0).astype(BF)
         py = jnp.concatenate([py[:half] + for_y.astype(F32), py[half:]], 0).astype(BF)
         got_x, got_y = self.over_x(px), self.over_y(py)
-        return part(0) + got_x.astype(F32) + got_y.astype(F32)
+        return block(after(left, *late), 0) + got_x.astype(F32) + got_y.astype(F32)
+
+    def over_both(self, a):
+        return lax.ppermute(a, "rep", self.ds)
+
+    def swap_pieces(self, take):
+        got = self.over_both(take(self.me ^ 3))
+        half = got.shape[0] // 2
+        return [take(self.me), self.over_x(take(self.me ^ 1)), self.over_y(take(self.me ^ 2)), got[:half], got[half:]]
 
     def swap(self, a):
         return lax.all_to_all(a, "rep", 0, 0, tiled=True)
 
     def gather_weight(self, w):
         return lax.all_gather(w, "fsdp", axis=0, tiled=True)
+
+    def own_total(self, a):
+        if not self.square:
+            return lax.dynamic_index_in_dim(lax.psum(a, ("rep", "fsdp")), lax.axis_index("fsdp"), 0, False)
+        a = jnp.sum(lax.all_to_all(a, "fsdp", 0, 0, tiled=True), 0)
+        return a + self.over_x(a) + self.over_y(a) + self.over_both(a)
 
     def scatter_weight(self, g):
         return lax.psum_scatter(g, "fsdp", scatter_dimension=0, tiled=True)
@@ -223,31 +485,41 @@
     bias_qkv = jnp.concatenate([bias_q, jnp.zeros_like(bias_q), bias_v], 0)
     bias_up = lax.dynamic_index_in_dim(b_up.reshape(shards, reps, fpart), r, 1, False).reshape(-1)
 
-    qkv_own = lax.dynamic_index_in_dim(qkv_weight.reshape(wrows, 3, reps, dr), r, 2, False).reshape(wrows, 3 * dr)
-    out_own = lax.dynamic_slice(out_weight, (0, r * dr), (wrows, dr))
-    up_own = lax.dynamic_index_in_dim(up_weight.reshape(wrows, shards, reps, fpart), r, 2, False).reshape(wrows, fr)
-    down_own = lax.dynamic_slice(down_weight, (r * fpart, 0), (fpart, D))
-    w_qkv = mv.gather_weight(qkv_own)
-    w_out_cols = mv.gather_weight(out_own)
-    w_out = mv.swap(w_out_cols)
-    w_out = w_out.reshape(reps, dr, dr).transpose(1, 0, 2).reshape(dr, D)
+    fast = mv.square and fpart % 128 == 0
+    if fast:
+        attn_own = pick_attn(r, qkv_weight, out_weight, reps)
+        up_own, down_own = pick_ffn(r, up_weight, down_weight, reps, shards)
+        w_attn = mv.gather_weight(attn_own)
+        w_qkv = w_attn[:, : 3 * dr]
+        w_out = place_cols(r, mv.swap_pieces(lambda q: lax.dynamic_slice(w_attn, (q * dr, 3 * dr), (dr, dr))), 1, BF)
+    else:
+        pick_cols = lambda w, parts: lax.dynamic_index_in_dim(w.reshape(wrows, parts, reps, -1), r, 2, False).reshape(wrows, -1)
+        up_own = pick_cols(up_weight, shards)
+        down_own = lax.dynamic_slice(down_weight, (r * fpart, 0), (fpart, D))
+        w_qkv = mv.gather_weight(pick_cols(qkv_weight, 3))
+        w_out = mv.swap(mv.gather_weight(pick_cols(out_weight, 1)))
+        w_out = w_out.reshape(reps, dr, dr).transpose(1, 0, 2).reshape(dr, D)
     w_up = mv.gather_weight(up_own)
     w_down = mv.gather_weight(down_own)
 
     x = tokens.reshape(rows, D)
     lens = mv.gather_small(lengths)
-    x_all = jnp.concatenate(mv.gather_blocks(x), 0)
+    x_all = mv.gather_rows(x)
     qkv = (mm(x_all, w_qkv) + bias_qkv).astype(BF)
     o = attn_fwd(lens, qkv, seq)
-    block = lambda a, k: a[k * rows : (k + 1) * rows]
-    attn = mv.scatter_sum(lambda k: mm(block(o, k), w_out))
+    attn = mv.scatter_sum(o, w_out, mm, mv.far_term(o, w_out, mm))
     x1, n1, inv1 = norm_forward(x.astype(F32) + attn + b_out, g_attn, s_attn)
 
-    x1_all = jnp.concatenate(mv.gather_blocks(x1.astype(BF)), 0)
+    x1_all = mv.gather_rows(x1.astype(BF))
     hidden = mm(x1_all, w_up) + bias_up
-    act, gelu_back = jax.vjp(lambda h: jax.nn.gelu(h, approximate=True), hidden)
-    act = act.astype(BF)
-    branch = mv.scatter_sum(lambda k: mm(block(act, k), w_down))
+    inner = 0.7978845608028654 * (hidden + 0.044715 * hidden * hidden * hidden)
+    t = jnp.tanh(inner)
+    act = (0.5 * hidden * (1.0 + t)).astype(BF)
+    slope = 0.5 * (1.0 + t) + 0.5 * hidden * (1.0 - t * t) * (
+        0.7978845608028654 * (1.0 + 3 * 0.044715 * hidden * hidden)
+    )
+    slope = slope.astype(BF)
+    branch = mv.scatter_sum(act, w_down, mm, mv.far_term(act, w_down, mm))
     result, n2, inv2 = norm_forward(x1 + branch + b_down, g_ffn, s_ffn)
     output = result.astype(BF).reshape(slots, seq, D)
 
@@ -255,42 +527,38 @@
     g = cotangent.reshape(rows, D).astype(F32) * valid.reshape(rows, 1)
     dr2, d_gffn, d_sffn = norm_backward(g, g_ffn, n2, inv2)
     df = dr2.astype(BF)
-    df_all = jnp.concatenate(mv.gather_blocks(df), 0)
-    d_wdown = mv.scatter_weight(mm_tn(act, df_all).astype(BF))
+    df_all = mv.gather_rows(df)
+    d_wdown = mm_tn(act, df_all).astype(BF)
+    df_all = after(df_all, d_wdown)
+    d_wdown = mv.scatter_weight(d_wdown)
     d_bdown = jnp.sum(df.astype(F32), 0)
-    (dh,) = gelu_back(mm_nt(df_all, w_down))
-    dh = dh.astype(BF)
-    d_wup = mv.scatter_weight(mm_tn(x1_all, dh).astype(BF))
+    dh = (mm_nt(df_all, w_down) * slope.astype(F32)).astype(BF)
     d_bup = jnp.sum(dh.astype(F32), 0)
-    dx1 = dr2 + mv.scatter_sum(lambda k: mm_nt(block(dh, k), w_up))
+    far = mv.far_term(dh, w_up, mm_nt)
+    d_wup = mm_tn(x1_all, after(dh, far) if fast else dh).astype(BF)
+    dx1 = dr2 + mv.scatter_sum(dh, w_up, mm_nt, far, (d_wup,))
+    d_wup = mv.scatter_weight(d_wup)
 
     dr1, d_gattn, d_sattn = norm_backward(dx1, g_attn, n1, inv1)
     dt = dr1.astype(BF)
-    dt_all = jnp.concatenate(mv.gather_blocks(dt), 0)
+    dt_all = after(mv.gather_rows(dt), d_wdown)
     d_bout = jnp.sum(dt.astype(F32), 0)
     d_wout = mm_tn(o, dt_all).astype(BF)
-    d_wout = mv.swap(d_wout.reshape(dr, reps, dr).transpose(1, 0, 2).reshape(reps * dr, dr))
-    d_wout = mv.scatter_weight(d_wout)
+    if fast:
+        out_pieces = mv.swap_pieces(lambda q: lax.dynamic_slice(d_wout, (0, q * dr), (dr, dr)))
     do = mm_nt(dt_all, w_out).astype(BF)
     dqkv, sums = attn_bwd(lens, qkv, do, seq)
-    d_wqkv = mv.scatter_weight(mm_tn(x_all, dqkv).astype(BF))
-    input_grad = dr1 + mv.scatter_sum(lambda k: mm_nt(block(dqkv, k), w_qkv))
-    input_grad = input_grad.reshape(slots, seq, D)
-
-    def spread(shard, shape, at):
-        total = jnp.zeros(shape, F32)
-        for k, piece in enumerate(mv.gather_blocks(shard)):
-            start = [0] * len(shape)
-            start[at] = mv.owner(k)
-            kept = list(shape)
-            kept[at] = 1
-            total = lax.dynamic_update_slice(total, piece.astype(F32).reshape(kept), start)
-        return total
-
-    d_wdown = spread(d_wdown, (reps, fpart, D), 0).reshape(down_weight.shape)
-    d_wup = spread(d_wup, (wrows, shards, reps, fpart), 2).reshape(up_weight.shape)
-    d_wout = spread(d_wout, (wrows, reps, dr), 1).reshape(out_weight.shape)
-    d_wqkv = spread(d_wqkv, (wrows, 3, reps, dr), 2).reshape(qkv_weight.shape)
+    d_wqkv = mm_tn(x_all, dqkv).astype(BF)
+    if fast:
+        down_near = mv.gather_near(after(d_wdown, dt_all))
+        d_wattn = join_attn(r, after(d_wqkv, *down_near), out_pieces)
+        dqkv = after(dqkv, d_wattn)
+        d_wattn = mv.scatter_weight(d_wattn)
+        down_pieces = mv.gather_far(down_near)
+    else:
+        d_wqkv = mv.scatter_weight(d_wqkv)
+        d_wout = mv.swap(d_wout.reshape(dr, reps, dr).transpose(1, 0, 2).reshape(reps * dr, dr))
+        d_wout = mv.scatter_weight(d_wout)
 
     zero = jnp.zeros((2, D), F32)
     d_qv = lax.dynamic_update_slice(zero, jnp.stack([sums[0, :dr], sums[0, 2 * dr :]]), (0, r * dr)).reshape(-1)
@@ -299,8 +567,28 @@
     ).reshape(-1)
     grads = [d_qv, d_bout, d_gattn, d_sattn, d_bup, d_bdown, d_gffn, d_sffn]
     packed = jnp.concatenate([v.reshape(shards, -1) for v in grads], 1)
-    packed = lax.psum(packed, ("rep", "fsdp"))
-    packed = lax.dynamic_index_in_dim(packed, lax.axis_index("fsdp"), 0, False)
+    packed = mv.own_total(packed)
+
+    late = (packed, d_wup, *down_pieces) if fast else ()
+    input_grad = dr1 + mv.scatter_sum(dqkv, w_qkv, mm_nt, mv.far_term(dqkv, w_qkv, mm_nt), late)
+    input_grad = input_grad.reshape(slots, seq, D)
+
+    if fast:
+        up_pieces = mv.gather_pieces(d_wup)
+        d_wdown = place_rows(r, down_pieces)
+        d_wup = place_cols(r, up_pieces, shards)
+        attn_pieces = mv.gather_pieces(after(d_wattn, input_grad, *up_pieces), d_wdown, d_wup)
+        d_wqkv, d_wout = place_attn(r, attn_pieces)
+    else:
+
+        def spread(shard, parts):
+            whole = lax.all_gather(shard, "rep", axis=0, tiled=False).astype(F32)
+            whole = whole.reshape(reps, wrows, parts, -1).transpose(1, 2, 0, 3)
+            return whole.reshape(wrows, -1)
+
+        d_wdown = mv.gather_rows(d_wdown).astype(F32)
+        d_wup, d_wout, d_wqkv = spread(d_wup, shards), spread(d_wout, 1), spread(d_wqkv, 3)
+
     pieces, at = [], 0
     for size in sizes:
         pieces.append(packed[at : at + size])

time: 1340 us -> 689 us (0.51)
  local copies, waits for them, and re-layouts: 436 us -> 37.8 us
  waiting for transfers between devices: 574 us -> 293 us
  Pallas kernels: 30.7 us -> 75.4 us
  other arithmetic: 31.9 us -> 15.5 us
    dynamic_update_slice x10 -> x0, local copies, waits for them, and re-layouts: 303 us -> none  [spread(): lax.dynamic_update_slice(total, piece.astype(F32).reshape(kept), start)]
    reduce_scatter x4 -> x3, waiting for transfers between devices: 260 us -> 1.82 us  [scatter_weight(): return lax.psum_scatter(g, 'fsdp', scatter_dimension=0, tiled=True)]
    psum x1 -> x0, waiting for transfers between devices: 48.3 us -> none  [per_device(): packed = lax.psum(packed, ('rep', 'fsdp'))]
    pallas_call x0 -> x7, Pallas kernels: none -> 44.7 us  [the longest x2 14 us: place_cols(): pl.pallas_call(place_cols_kernel, grid_spec=pltpu.PrefetchScalarGridSpec(...]
    reshape x12 -> x1, local copies, waits for them, and re-layouts: 42.7 us -> 0.01 us  [per_device(): d_bup.reshape(shards, 1, fpart)]
    ppermute x25 -> x26, waiting for transfers between devices: 90.8 us -> 121 us  [over_x(): return lax.ppermute(a, 'rep', self.xs)]
    ppermute x25 -> x26, waiting for transfers between devices: 123 us -> 102 us  [over_y(): return lax.ppermute(a, 'rep', self.ys)]
    unnamed x122 -> x124, local copies, waits for them, and re-layouts: 36.9 us -> 20.2 us
  transfers between devices with their start and end apart: 62 -> 62, of which waited for: 30 -> 39; matrix products, arithmetic and copies ran while one was open for 42% -> 26% of each run, Pallas kernels for 2% -> 9%
where the time goes in v2:
time: 689 us; the launch traced here: 684 us
  waiting for transfers between devices  293 us (43%)
  matrix products  151 us (22%)
  Pallas kernels  75.4 us (11%)
  starting transfers between devices  69.9 us (10%)
  local copies, waits for them, and re-layouts  37.8 us (5%)
  blocking collectives  26.5 us (4%)
  other arithmetic  15.5 us (2%)
  between operations  15.4 us (2%)
    ppermute x26, waiting for transfers between devices, over_x(): return lax.ppermute(a, 'rep', self.xs)  121 us
    ppermute x26, waiting for transfers between devices, over_y(): return lax.ppermute(a, 'rep', self.ys)  102 us
    all_gather x3, waiting for transfers between devices, gather_weight(): return lax.all_gather(w, 'fsdp', axis=0, tiled=True)  64.8 us
    dot_general x10, matrix products, mm_nt(): lax.dot_general(a, b, (((1,), (1,)), ((), ())), preferred_element_type=F32)  63 us
    dot_general x10, matrix products, mm(): return jnp.dot(a, b, preferred_element_type=F32)  48.5 us
    dot_general x4, matrix products, mm_tn(): lax.dot_general(a, b, (((0,), (0,)), ((), ())), preferred_element_type=F32)  39 us
    ppermute x26, starting transfers between devices, over_x(): return lax.ppermute(a, 'rep', self.xs)  31 us
    ppermute x26, starting transfers between devices, over_y(): return lax.ppermute(a, 'rep', self.ys)  29.7 us
  transfers between devices with their start and end apart: 62, of which 39 were waited for; matrix products, arithmetic and copies ran while one was open for 26% of the time, Pallas kernels for 9%

profile of v2, /device:TPU:0, one launch (start us, length us, event | category | flops | bytes accessed | tf_op | source)
XLA Modules:
  0.0 683.6 jit_solution(9069045517009311555)
XLA Ops:
  26.3 14.7 %all-gather = bf16[24576]{0:T(1024)(128)(2,1)S(1)} all-gather(bf16[3072]{0:T(1024)(128)(2,1)S(1)} %dynamic-update-slice.30), channel_id=2, replica_groups=mesh['rep'=4,'fsdp'=8] {'fsdp'}, dimensions={0}, use_global_device_ids=true | all-gather | bytes 55296 | tf_op jit(solution)/shard_map/all_gather | solution.py:477
  59.0 36.5 %all-gather.5.cloned.1.call-done = bf16[2048,2048]{1,0:T(8,128)(2,1)} async-done(((bf16[256,2048]{1,0:T(8,128)(2,1)}), bf16[2048,2048]{1,0:T(8,128)(2,1)}) %all-gather.5.cloned.1.call-update) | async-done | bytes 8388624 | tf_op jit(solution)/shard_map/all_gather | solution.py:435
  101.9 11.9 %add_convert_fusion.qkv_ref = bf16[1024,1536]{1,0:T(8,128)(2,1)} fusion(bf16[1024,2048]{1,0:T(8,128)(2,1)} %constant_dynamic-update-slice_fusion, bf16[2048,2048]{1,0:T(8,128)(2,1)} %all-gather.5.cloned.1.call-done, f32[1536]{0:T(1024)S(1)} %pad_maximum_fusion.8), kind=kOutput, calls=%fused_computation.15 | convolution fusion | flops 6445596672 | bytes 13637632 | tf_op jit(solution)/shard_map/dot_general | solution.py:17
  113.8 13.7 %shard_map.255 = bf16[1024,512]{1,0:T(8,128)(2,1)} custom-call(s32[8]{0:T(128)} %pad_add_fusion.len_ref, bf16[1024,1536]{1,0:T(8,128)(2,1)} %add_convert_fusion.qkv_ref), custom_call_target="tpu_custom_call" | custom-call | flops 268435456 | bytes 4194304 | tf_op jit(solution)/shard_map/pallas_call | solution.py:78
  152.4 21.0 %collective-permute-done.11 = bf16[256,2048]{1,0:T(8,128)(2,1)S(1)} collective-permute-done((bf16[256,2048]{1,0:T(8,128)(2,1)S(1)}, bf16[256,2048]{1,0:T(8,128)(2,1)S(1)}, u32[]{:S(2)}, u32[]{:S(2)}) %collective-permute-start.11) | collective-permute-done | bytes 1048608 | tf_op jit(solution)/shard_map/ppermute | solution.py:375
  180.9 20.6 %collective-permute-done.15 = bf16[256,2048]{1,0:T(8,128)(2,1)S(1)} collective-permute-done((bf16[256,2048]{1,0:T(8,128)(2,1)}, bf16[256,2048]{1,0:T(8,128)(2,1)S(1)}, u32[]{:S(2)}, u32[]{:S(2)}) %collective-permute-start.15) | collective-permute-done | bytes 1048608 | tf_op jit(solution)/shard_map/ppermute | solution.py:378
  215.1 17.2 %multiply_convert_fusion.1 = (bf16[1024,2048]{1,0:T(8,128)(2,1)}, f32[1024,2048]{1,0:T(8,128)}) fusion(f32[2048]{0:T(1024)S(1)} %bitcast.101, bf16[1024,2048]{1,0:T(8,128)(2,1)} %constant_dynamic-update-slice_fusion.5, bf16[2048,2048]{1,0:T(8,128)(2,1)} %all-gather.7.cloned.1.call-done), kind=kOutput, calls=%fused_computation.11 | convolution fusion | flops 8610906112 | bytes 25174016 | tf_op jit(solution)/shard_map/dot_general | solution.py:17
  232.4 28.3 %all-gather.9.cloned.1.call-done = bf16[2048,2048]{1,0:T(8,128)(2,1)} async-done(((bf16[256,2048]{1,0:T(8,128)(2,1)}), bf16[2048,2048]{1,0:T(8,128)(2,1)}) %all-gather.9.cloned.1.call-update) | async-done | bytes 8388624 | tf_op jit(solution)/shard_map/all_gather | solution.py:435
  289.7 17.5 %collective-permute-done.19 = bf16[256,2048]{1,0:T(8,128)(2,1)S(1)} collective-permute-done((bf16[256,2048]{1,0:T(8,128)(2,1)S(1)}, bf16[256,2048]{1,0:T(8,128)(2,1)S(1)}, u32[]{:S(2)}, u32[]{:S(2)}) %collective-permute-start.19) | collective-permute-done | bytes 1048608 | tf_op jit(solution)/shard_map/ppermute | solution.py:375
  315.2 19.7 %collective-permute-done.23 = bf16[256,2048]{1,0:T(8,128)(2,1)S(1)} collective-permute-done((bf16[256,2048]{1,0:T(8,128)(2,1)S(1)}, bf16[256,2048]{1,0:T(8,128)(2,1)S(1)}, u32[]{:S(2)}, u32[]{:S(2)}) %collective-permute-start.23) | collective-permute-done | bytes 1048608 | tf_op jit(solution)/shard_map/ppermute | solution.py:378
  338.7 9.0 %collective-permute-done.24 = bf16[128,2048]{1,0:T(8,128)(2,1)S(1)} collective-permute-done((bf16[128,2048]{1,0:T(8,128)(2,1)S(1)}, bf16[128,2048]{1,0:T(8,128)(2,1)S(1)}, u32[]{:S(2)}, u32[]{:S(2)}) %collective-permute-start.24) | collective-permute-done | bytes 524320 | tf_op jit(solution)/shard_map/ppermute | solution.py:375
  349.7 11.4 %convolution_convert_fusion.2 = bf16[2048,2048]{1,0:T(8,128)(2,1)} fusion(bf16[1024,2048]{1,0:T(8,128)(2,1)S(1)} %copy-done.37, bf16[1024,2048]{1,0:T(8,128)(2,1)S(1)} %constant_dynamic-update-slice_fusion.10), kind=kOutput, calls=%fused_computation.14 | convolution fusion | flops 8594128896 | bytes 16777216 | tf_op jit(solution)/shard_map/dot_general | solution.py:25
  361.2 18.9 %convert_reduce_fusion = (f32[2048]{0:T(1024)S(1)}, bf16[1024,2048]{1,0:T(8,128)(2,1)S(1)}) fusion(f32[1024,2048]{1,0:T(8,128)} %get-tuple-element.116, f32[2048]{0:T(1024)S(1)} %bitcast.102, bf16[1024,2048]{1,0:T(8,128)(2,1)} %copy-done.21, bf16[2048,2048]{1,0:T(8,128)(2,1)} %all-gather.9.cloned.1.call-done), kind=kOutput, calls=%fused_computation.9 | convolution fusion | flops 8640264192 | bytes 25182208 | tf_op jit(solution)/shard_map/dot_general | solution.py:21
  388.6 11.4 %convolution_convert_fusion.1 = bf16[2048,2048]{1,0:T(8,128)(2,1)} fusion(bf16[1024,2048]{1,0:T(8,128)(2,1)S(1)} %copy-done.22, bf16[1024,2048]{1,0:T(8,128)(2,1)S(1)} %get-tuple-element.41), kind=kOutput, calls=%fused_computation.13 | convolution fusion | flops 8594128896 | bytes 16777216 | tf_op jit(solution)/shard_map/dot_general | solution.py:25
  414.2 10.0 %collective-permute-done.28 = bf16[128,2048]{1,0:T(8,128)(2,1)S(1)} collective-permute-done((bf16[128,2048]{1,0:T(8,128)(2,1)S(1)}, bf16[128,2048]{1,0:T(8,128)(2,1)S(1)}, u32[]{:S(2)}, u32[]{:S(2)}) %collective-permute-start.28) | collective-permute-done | bytes 524320 | tf_op jit(solution)/shard_map/ppermute | solution.py:375
  428.0 13.3 %collective-permute-done.27 = bf16[256,2048]{1,0:T(8,128)(2,1)S(1)} collective-permute-done((bf16[256,2048]{1,0:T(8,128)(2,1)S(1)}, bf16[256,2048]{1,0:T(8,128)(2,1)S(1)}, u32[]{:S(2)}, u32[]{:S(2)}) %collective-permute-start.27) | collective-permute-done | bytes 1048608 | tf_op jit(solution)/shard_map/ppermute | solution.py:375
  450.8 18.0 %collective-permute-done.31 = bf16[256,2048]{1,0:T(8,128)(2,1)S(1)} collective-permute-done((bf16[256,2048]{1,0:T(8,128)(2,1)S(1)}, bf16[256,2048]{1,0:T(8,128)(2,1)S(1)}, u32[]{:S(2)}, u32[]{:S(2)}) %collective-permute-start.31) | collective-permute-done | bytes 1048608 | tf_op jit(solution)/shard_map/ppermute | solution.py:378
  500.1 17.0 %shard_map.258 = (bf16[1024,1536]{1,0:T(8,128)(2,1)}, f32[1,1536]{1,0:T(1,128)}) custom-call(s32[8]{0:T(128)} %pad_add_fusion.len_ref, bf16[1024,1536]{1,0:T(8,128)(2,1)} %add_convert_fusion.qkv_ref, bf16[1024,512]{1,0:T(8,128)(2,1)} %convolution_convert_fusion.7.do_ref), custom_call_target="tpu_custom_call" | custom-call | flops 671088640 | bytes 7340032 | tf_op jit(solution)/shard_map/pallas_call | solution.py:96
  517.1 11.6 %convolution_convert_fusion.qkv = bf16[2048,1536]{1,0:T(8,128)(2,1)} fusion(bf16[1024,2048]{1,0:T(8,128)(2,1)} %constant_dynamic-update-slice_fusion, bf16[1024,1536]{1,0:T(8,128)(2,1)} %get-tuple-element.49), kind=kOutput, calls=%fused_computation.12 | convolution fusion | flops 6445596672 | bytes 13631488 | tf_op jit(solution)/shard_map/dot_general | solution.py:25
  555.7 17.7 %collective-permute-done.44 = bf16[128,2048]{1,0:T(8,128)(2,1)S(1)} collective-permute-done((bf16[128,2048]{1,0:T(8,128)(2,1)S(1)}, bf16[128,2048]{1,0:T(8,128)(2,1)S(1)}, u32[]{:S(2)}, u32[]{:S(2)}) %collective-permute-start.44) | collective-permute-done | bytes 524320 | tf_op jit(solution)/shard_map/ppermute | solution.py:378
  578.8 11.8 %all_to_all.9 = f32[8,1,3072]{2,1,0:T(1,128)S(1)} all-to-all(f32[8,1,3072]{2,1,0:T(1,128)S(1)} %all_to_all.6), channel_id=1, replica_groups=mesh['rep'=4,'fsdp'=8] {'fsdp'}, dimensions={0} | all-to-all | bytes 196608 | tf_op jit(solution)/shard_map/all_to_all | solution.py:440
  610.0 10.5 %collective-permute-done.42.low = bf16[128,2048]{1,0:T(8,128)(2,1)} collective-permute-done((bf16[128,2048]{1,0:T(8,128)(2,1)S(1)}, bf16[128,2048]{1,0:T(8,128)(2,1)}, u32[]{:S(2)}, u32[]{:S(2)}) %collective-permute-start.42) | collective-permute-done | bytes 524320 | tf_op jit(solution)/shard_map/ppermute | solution.py:375
  634.4 11.2 %shard_map.261 = f32[256,8192]{1,0:T(8,128)} custom-call(s32[1]{0:T(128)} %bitcast.1.me_ref, bf16[256,2048]{1,0:T(8,128)(2,1)} %reduce-scatter.6.cloned.1.call-done.own, bf16[256,2048]{1,0:T(8,128)(2,1)} %collective-permute-done.48.ax, bf16[256,2048]{1,0:T(8,128)(2,1)} %copy-done.10, bf16[128,2048]{1,0:T(8,128)(2,1)} %copy-done.14, ...), custom_call_target="tpu_custom_call" | custom-call | bytes 12582912 | tf_op jit(solution)/shard_map/pallas_call | solution.py:202
  667.7 8.9 %shard_map.262 = (f32[256,6144]{1,0:T(8,128)}, f32[256,2048]{1,0:T(8,128)}) custom-call(s32[1]{0:T(128)} %bitcast.1.me_ref, bf16[256,2048]{1,0:T(8,128)(2,1)} %reduce-scatter.8.cloned.1.call-done.own, bf16[256,2048]{1,0:T(8,128)(2,1)} %copy-done.11, bf16[256,2048]{1,0:T(8,128)(2,1)} %copy-done.12, bf16[128,2048]{1,0:T(8,128)(2,1)} %copy-done.17, ...), custom_call_target="tpu_custom_call" | custom-call | bytes 12582912 | tf_op jit(solution)/shard_map/pallas_call | solution.py:292
  (362 shorter events, 286.4 us)
Async XLA Ops:
  7.2 88.3 %all-gather.5.cloned.1.call-start = ((), (), s32[]{:S(2)}) async-start(), calls=%async_computation.4 | async-start | bytes 9437184 | tf_op jit(solution)/shard_map/all_gather | solution.py:435
  10.4 204.7 %all-gather.7.cloned.1.call-start = ((), (), s32[]{:S(2)}) async-start(), calls=%async_computation.5 | async-start | bytes 9437184 | tf_op jit(solution)/shard_map/all_gather | solution.py:435
  16.4 244.2 %all-gather.9.cloned.1.call-start = ((), (), s32[]{:S(2)}) async-start(), calls=%async_computation.6 | async-start | bytes 9437184 | tf_op jit(solution)/shard_map/all_gather | solution.py:435
  16.5 26.2 %collective-permute-start.4 = (bf16[256,2048]{1,0:T(8,128)(2,1)S(1)}, bf16[256,2048]{1,0:T(8,128)(2,1)S(1)}, u32[]{:S(2)}, u32[]{:S(2)}) collective-permute-start(bf16[256,2048]{1,0:T(8,128)(2,1)S(1)} %bitcast.78), channel_id=1, source_target_pairs={{0,16},{8,24},{16,0},{24,8},{1,17},{9,25},{17,1},{25,9},{2,18},{10... | collective-permute-start | bytes 3145736 | tf_op jit(solution)/shard_map/ppermute | solution.py:378
  19.5 463.9 %reduce-scatter.4.cloned.1.call-start = ((), (), s32[]{:S(2)}) async-start(), calls=%async_computation.7 | async-start | bytes 9437184 | tf_op jit(solution)/shard_map/reduce_scatter | solution.py:444
  19.6 25.6 %collective-permute-start.3 = (bf16[256,2048]{1,0:T(8,128)(2,1)S(1)}, bf16[256,2048]{1,0:T(8,128)(2,1)S(1)}, u32[]{:S(2)}, u32[]{:S(2)}) collective-permute-start(bf16[256,2048]{1,0:T(8,128)(2,1)S(1)} %bitcast.79), channel_id=1, source_target_pairs={{0,8},{8,0},{16,24},{24,16},{1,9},{9,1},{17,25},{25,17},{2,10},{10... | collective-permute-start | bytes 3145736 | tf_op jit(solution)/shard_map/ppermute | solution.py:375
  98.4 29.1 %collective-permute-start.9 = (bf16[512,512]{1,0:T(8,128)(2,1)}, bf16[512,512]{1,0:T(8,128)(2,1)}, u32[]{:S(2)}, u32[]{:S(2)}) collective-permute-start(bf16[512,512]{1,0:T(8,128)(2,1)} %get-tuple-element.74), channel_id=1, source_target_pairs={{0,24},{8,16},{16,8},{24,0},{1,25},{9,17},{17,9},{25,1},{2,26},{10... | collective-permute-start | bytes 1572872 | tf_op jit(solution)/shard_map/ppermute | solution.py:424
  100.9 28.6 %collective-permute-start.7 = (bf16[512,512]{1,0:T(8,128)(2,1)}, bf16[512,512]{1,0:T(8,128)(2,1)S(1)}, u32[]{:S(2)}, u32[]{:S(2)}) collective-permute-start(bf16[512,512]{1,0:T(8,128)(2,1)} %get-tuple-element.76), channel_id=1, source_target_pairs={{0,8},{8,0},{16,24},{24,16},{1,9},{9,1},{17,25},{25,17},{2,10},{10... | collective-permute-start | bytes 1572872 | tf_op jit(solution)/shard_map/ppermute | solution.py:375
  101.4 28.1 %collective-permute-start.8 = (bf16[512,512]{1,0:T(8,128)(2,1)}, bf16[512,512]{1,0:T(8,128)(2,1)S(1)}, u32[]{:S(2)}, u32[]{:S(2)}) collective-permute-start(bf16[512,512]{1,0:T(8,128)(2,1)} %get-tuple-element.75), channel_id=1, source_target_pairs={{0,16},{8,24},{16,0},{24,8},{1,17},{9,25},{17,1},{25,9},{2,18},{10... | collective-permute-start | bytes 1572872 | tf_op jit(solution)/shard_map/ppermute | solution.py:378
  281.2 26.0 %collective-permute-start.19 = (bf16[256,2048]{1,0:T(8,128)(2,1)S(1)}, bf16[256,2048]{1,0:T(8,128)(2,1)S(1)}, u32[]{:S(2)}, u32[]{:S(2)}) collective-permute-start(bf16[256,2048]{1,0:T(8,128)(2,1)S(1)} %pad_maximum_fusion.2), channel_id=1, source_target_pairs={{0,8},{8,0},{16,24},{24,16},{1,9},{9,1},{17,25},{25,17},{2,10},{10... | collective-permute-start | bytes 3145736 | tf_op jit(solution)/shard_map/ppermute | solution.py:375
  313.8 24.6 %collective-permute-start.22 = (bf16[256,2048]{1,0:T(8,128)(2,1)S(1)}, bf16[256,2048]{1,0:T(8,128)(2,1)S(1)}, u32[]{:S(2)}, u32[]{:S(2)}) collective-permute-start(bf16[256,2048]{1,0:T(8,128)(2,1)S(1)} %get-tuple-element.65), channel_id=1, source_target_pairs={{0,8},{8,0},{16,24},{24,16},{1,9},{9,1},{17,25},{25,17},{2,10},{10... | collective-permute-start | bytes 3145736 | tf_op jit(solution)/shard_map/ppermute | solution.py:375
  361.1 178.3 %reduce-scatter.6.cloned.1.call-start = ((), (), s32[]{:S(2)}) async-start(), calls=%async_computation.8 | async-start | bytes 9437184 | tf_op jit(solution)/shard_map/reduce_scatter | solution.py:444
  400.1 231.4 %reduce-scatter.8.cloned.1.call-start = ((), (), s32[]{:S(2)}) async-start(), calls=%async_computation.9 | async-start | bytes 9437184 | tf_op jit(solution)/shard_map/reduce_scatter | solution.py:444
  412.6 28.7 %collective-permute-start.27 = (bf16[256,2048]{1,0:T(8,128)(2,1)S(1)}, bf16[256,2048]{1,0:T(8,128)(2,1)S(1)}, u32[]{:S(2)}, u32[]{:S(2)}) collective-permute-start(bf16[256,2048]{1,0:T(8,128)(2,1)S(1)} %pad_maximum_fusion.4), channel_id=1, source_target_pairs={{0,8},{8,0},{16,24},{24,16},{1,9},{9,1},{17,25},{25,17},{2,10},{10... | collective-permute-start | bytes 3145736 | tf_op jit(solution)/shard_map/ppermute | solution.py:375
  483.5 47.0 %collective-permute-start.35 = (bf16[256,2048]{1,0:T(8,128)(2,1)}, bf16[256,2048]{1,0:T(8,128)(2,1)S(1)}, u32[]{:S(2)}, u32[]{:S(2)}) collective-permute-start(bf16[256,2048]{1,0:T(8,128)(2,1)} %reduce-scatter.4.cloned.1.call-done.own), channel_id=1, source_target_pairs={{0,16},{8,24},{16,0},{24,8},{1,17},{9,25},{17,1},{25,9},{2,18},{10... | collective-permute-start | bytes 3145736 | tf_op jit(solution)/shard_map/ppermute | solution.py:378
  483.5 47.0 %collective-permute-start.34 = (bf16[256,2048]{1,0:T(8,128)(2,1)}, bf16[256,2048]{1,0:T(8,128)(2,1)S(1)}, u32[]{:S(2)}, u32[]{:S(2)}) collective-permute-start(bf16[256,2048]{1,0:T(8,128)(2,1)} %reduce-scatter.4.cloned.1.call-done.own), channel_id=1, source_target_pairs={{0,8},{8,0},{16,24},{24,16},{1,9},{9,1},{17,25},{25,17},{2,10},{10... | collective-permute-start | bytes 3145736 | tf_op jit(solution)/shard_map/ppermute | solution.py:375
  491.0 37.6 %collective-permute-start.38 = (bf16[512,512]{1,0:T(8,128)(2,1)}, bf16[512,512]{1,0:T(8,128)(2,1)}, u32[]{:S(2)}, u32[]{:S(2)}) collective-permute-start(bf16[512,512]{1,0:T(8,128)(2,1)} %get-tuple-element.79), channel_id=1, source_target_pairs={{0,24},{8,16},{16,8},{24,0},{1,25},{9,17},{17,9},{25,1},{2,26},{10... | collective-permute-start | bytes 1572872 | tf_op jit(solution)/shard_map/ppermute | solution.py:424
  493.0 37.5 %collective-permute-start.36 = (bf16[512,512]{1,0:T(8,128)(2,1)}, bf16[512,512]{1,0:T(8,128)(2,1)S(1)}, u32[]{:S(2)}, u32[]{:S(2)}) collective-permute-start(bf16[512,512]{1,0:T(8,128)(2,1)} %get-tuple-element.81), channel_id=1, source_target_pairs={{0,8},{8,0},{16,24},{24,16},{1,9},{9,1},{17,25},{25,17},{2,10},{10... | collective-permute-start | bytes 1572872 | tf_op jit(solution)/shard_map/ppermute | solution.py:375
  494.5 36.1 %collective-permute-start.37 = (bf16[512,512]{1,0:T(8,128)(2,1)}, bf16[512,512]{1,0:T(8,128)(2,1)S(1)}, u32[]{:S(2)}, u32[]{:S(2)}) collective-permute-start(bf16[512,512]{1,0:T(8,128)(2,1)} %get-tuple-element.80), channel_id=1, source_target_pairs={{0,16},{8,24},{16,0},{24,8},{1,17},{9,25},{17,1},{25,9},{2,18},{10... | collective-permute-start | bytes 1572872 | tf_op jit(solution)/shard_map/ppermute | solution.py:378
  539.4 67.9 %collective-permute-start.49 = (bf16[256,2048]{1,0:T(8,128)(2,1)}, bf16[256,2048]{1,0:T(8,128)(2,1)S(1)}, u32[]{:S(2)}, u32[]{:S(2)}) collective-permute-start(bf16[256,2048]{1,0:T(8,128)(2,1)} %reduce-scatter.6.cloned.1.call-done.own), channel_id=1, source_target_pairs={{0,16},{8,24},{16,0},{24,8},{1,17},{9,25},{17,1},{25,9},{2,18},{10... | collective-permute-start | bytes 3145736 | tf_op jit(solution)/shard_map/ppermute | solution.py:378
  541.6 66.9 %collective-permute-start.48 = (bf16[256,2048]{1,0:T(8,128)(2,1)}, bf16[256,2048]{1,0:T(8,128)(2,1)}, u32[]{:S(2)}, u32[]{:S(2)}) collective-permute-start(bf16[256,2048]{1,0:T(8,128)(2,1)} %reduce-scatter.6.cloned.1.call-done.own), channel_id=1, source_target_pairs={{0,8},{8,0},{16,24},{24,16},{1,9},{9,1},{17,25},{25,17},{2,10},{10... | collective-permute-start | bytes 3145736 | tf_op jit(solution)/shard_map/ppermute | solution.py:375
  547.3 26.1 %collective-permute-start.44 = (bf16[128,2048]{1,0:T(8,128)(2,1)S(1)}, bf16[128,2048]{1,0:T(8,128)(2,1)S(1)}, u32[]{:S(2)}, u32[]{:S(2)}) collective-permute-start(bf16[128,2048]{1,0:T(8,128)(2,1)S(1)} %get-tuple-element.83), channel_id=1, source_target_pairs={{0,16},{8,24},{16,0},{24,8},{1,17},{9,25},{17,1},{25,9},{2,18},{10... | collective-permute-start | bytes 1572872 | tf_op jit(solution)/shard_map/ppermute | solution.py:378
  574.6 46.6 %collective-permute-start.45 = (bf16[256,2048]{1,0:T(8,128)(2,1)}, bf16[256,2048]{1,0:T(8,128)(2,1)}, u32[]{:S(2)}, u32[]{:S(2)}) collective-permute-start(bf16[256,2048]{1,0:T(8,128)(2,1)} %pad_maximum_fusion.6), channel_id=1, source_target_pairs={{0,8},{8,0},{16,24},{24,16},{1,9},{9,1},{17,25},{25,17},{2,10},{10... | collective-permute-start | bytes 3145736 | tf_op jit(solution)/shard_map/ppermute | solution.py:375
  577.3 43.9 %collective-permute-start.47 = (bf16[256,2048]{1,0:T(8,128)(2,1)}, bf16[256,2048]{1,0:T(8,128)(2,1)}, u32[]{:S(2)}, u32[]{:S(2)}) collective-permute-start(bf16[256,2048]{1,0:T(8,128)(2,1)} %pad_maximum_fusion.7), channel_id=1, source_target_pairs={{0,16},{8,24},{16,0},{24,8},{1,17},{9,25},{17,1},{25,9},{2,18},{10... | collective-permute-start | bytes 3145736 | tf_op jit(solution)/shard_map/ppermute | solution.py:378
  (80 other events, 1110.1 us)
Sparse Core Ops, SparseCore 0:
  10.4 85.0 all-gather.4
  97.7 80.6 all-gather.6
  180.0 80.5 all-gather.8
  361.3 87.1 reduce-scatter.3
  451.2 87.9 reduce-scatter.5
  541.9 89.5 reduce-scatter.7

commit v3 on v2

--- a/solution.py
+++ b/solution.py
@@ -9,6 +9,7 @@
 HEADS = 16
 HEAD_DIM = 128
 EPS = 1e-05
+PAD = 16
 BF = jnp.bfloat16
 F32 = jnp.float32
 
@@ -25,63 +26,77 @@
     return lax.dot_general(a, b, (((0,), (0,)), ((), ())), preferred_element_type=F32)
 
 
-def head_probs(q, k, length, factor):
-    s = mm_nt(q, k) * factor
-    cols = lax.broadcasted_iota(jnp.int32, s.shape, 1)
-    s = jnp.where(cols < length, s, -1000000000.0)
-    e = jnp.exp(s - jnp.max(s, -1, keepdims=True))
-    return e / jnp.sum(e, -1, keepdims=True)
-
-
-def attn_fwd_kernel(len_ref, qkv_ref, o_ref):
-    width = o_ref.shape[1]
-    length = len_ref[pl.program_id(0)]
-    for h in range(width // HEAD_DIM):
-        at = h * HEAD_DIM
-        q = qkv_ref[:, at : at + HEAD_DIM]
-        k = qkv_ref[:, width + at : width + at + HEAD_DIM]
-        v = qkv_ref[:, 2 * width + at : 2 * width + at + HEAD_DIM]
-        p = head_probs(q, k, length, HEAD_DIM**-0.5).astype(BF)
-        o_ref[:, at : at + HEAD_DIM] = mm(p, v).astype(BF)
-
-
-def attn_bwd_kernel(len_ref, qkv_ref, do_ref, dqkv_ref, sums_ref):
+SLOTS = 2
+
+
+def heads_of(qkv_ref, width, seq):
+    return [
+        (slot, slice(slot * seq, (slot + 1) * seq), [part * width + at for part in range(3)])
+        for slot in range(SLOTS)
+        for at in range(0, width, HEAD_DIM)
+    ]
+
+
+def cut(ref, rows, at):
+    return ref[rows, at : at + HEAD_DIM]
+
+
+def all_probs(len_ref, qkv_ref, heads):
+    scores = [mm_nt(cut(qkv_ref, rows, at[0]), cut(qkv_ref, rows, at[1])) * HEAD_DIM**-0.5 for _, rows, at in heads]
+    cols = lax.broadcasted_iota(jnp.int32, scores[0].shape, 1)
+    first = pl.program_id(0) * SLOTS
+    valid = [cols < len_ref[first + slot] for slot in range(SLOTS)]
+    scores = [jnp.where(valid[slot], s, -1000000000.0) for s, (slot, _, _) in zip(scores, heads)]
+    expo = [jnp.exp(s - jnp.max(s, -1, keepdims=True)) for s in scores]
+    return [e / jnp.sum(e, -1, keepdims=True) for e in expo]
+
+
+def attn_fwd_kernel(len_ref, qkv_ref, o_ref, seq):
+    heads = heads_of(qkv_ref, o_ref.shape[1], seq)
+    probs = all_probs(len_ref, qkv_ref, heads)
+    for p, (_, rows, at) in zip(probs, heads):
+        o_ref[rows, at[0] : at[0] + HEAD_DIM] = mm(p.astype(BF), cut(qkv_ref, rows, at[2])).astype(BF)
+
+
+def attn_bwd_kernel(len_ref, qkv_ref, do_ref, dqkv_ref, sums_ref, seq):
     width = do_ref.shape[1]
     factor = HEAD_DIM**-0.5
-    length = len_ref[pl.program_id(0)]
+    heads = heads_of(qkv_ref, width, seq)
+    dps = [mm_nt(cut(do_ref, rows, at[0]), cut(qkv_ref, rows, at[2])) for _, rows, at in heads]
+    probs = all_probs(len_ref, qkv_ref, heads)
+    lows = [p.astype(BF) for p in probs]
+    dss = [(p * (dp - jnp.sum(p * dp, -1, keepdims=True))).astype(BF) for p, dp in zip(probs, dps)]
+    totals = {}
+    for p, ds, (_, rows, at) in zip(lows, dss, heads):
+        grads = (
+            (mm(ds, cut(qkv_ref, rows, at[1])) * factor).astype(BF),
+            (mm_tn(ds, cut(qkv_ref, rows, at[0])) * factor).astype(BF),
+            mm_tn(p, cut(do_ref, rows, at[0])).astype(BF),
+        )
+        for part, grad in enumerate(grads):
+            dqkv_ref[rows, at[part] : at[part] + HEAD_DIM] = grad
+            if part != 1:
+                total = jnp.sum(grad.astype(F32), 0, keepdims=True)
+                totals[at[part]] = totals[at[part]] + total if at[part] in totals else total
 
     @pl.when(pl.program_id(0) == 0)
     def _():
         sums_ref[...] = jnp.zeros_like(sums_ref)
 
-    for h in range(width // HEAD_DIM):
-        at = h * HEAD_DIM
-        q = qkv_ref[:, at : at + HEAD_DIM]
-        k = qkv_ref[:, width + at : width + at + HEAD_DIM]
-        v = qkv_ref[:, 2 * width + at : 2 * width + at + HEAD_DIM]
-        do = do_ref[:, at : at + HEAD_DIM]
-        p = head_probs(q, k, length, factor)
-        dp = mm_nt(do, v)
-        dv = mm_tn(p.astype(BF), do).astype(BF)
-        ds = (p * (dp - jnp.sum(p * dp, -1, keepdims=True))).astype(BF)
-        dq = (mm(ds, k) * factor).astype(BF)
-        dk = (mm_tn(ds, q) * factor).astype(BF)
-        for part, grad in ((0, dq), (1, dk), (2, dv)):
-            cols = slice(part * width + at, part * width + at + HEAD_DIM)
-            dqkv_ref[:, cols] = grad
-            sums_ref[:, cols] += jnp.sum(grad.astype(F32), 0, keepdims=True)
+    for start, total in totals.items():
+        sums_ref[:, start : start + HEAD_DIM] += total
 
 
 def attn_fwd(lengths, qkv, seq):
     rows, wide = qkv.shape
     width = wide // 3
     return pl.pallas_call(
-        attn_fwd_kernel,
+        lambda *refs: attn_fwd_kernel(*refs, seq=seq),
         grid_spec=pltpu.PrefetchScalarGridSpec(
             num_scalar_prefetch=1,
-            grid=(rows // seq,),
-            in_specs=[pl.BlockSpec((seq, wide), lambda i, n: (i, 0))],
-            out_specs=pl.BlockSpec((seq, width), lambda i, n: (i, 0)),
+            grid=(rows // (SLOTS * seq),),
+            in_specs=[pl.BlockSpec((SLOTS * seq, wide), lambda i, n: (i, 0))],
+            out_specs=pl.BlockSpec((SLOTS * seq, width), lambda i, n: (i, 0)),
         ),
         out_shape=jax.ShapeDtypeStruct((rows, width), BF),
         cost_estimate=pl.CostEstimate(
@@ -94,16 +109,16 @@
     rows, wide = qkv.shape
     width = wide // 3
     return pl.pallas_call(
-        attn_bwd_kernel,
+        lambda *refs: attn_bwd_kernel(*refs, seq=seq),
         grid_spec=pltpu.PrefetchScalarGridSpec(
             num_scalar_prefetch=1,
-            grid=(rows // seq,),
+            grid=(rows // (SLOTS * seq),),
             in_specs=[
-                pl.BlockSpec((seq, wide), lambda i, n: (i, 0)),
-                pl.BlockSpec((seq, width), lambda i, n: (i, 0)),
+                pl.BlockSpec((SLOTS * seq, wide), lambda i, n: (i, 0)),
+                pl.BlockSpec((SLOTS * seq, width), lambda i, n: (i, 0)),
             ],
             out_specs=[
-                pl.BlockSpec((seq, wide), lambda i, n: (i, 0)),
+                pl.BlockSpec((SLOTS * seq, wide), lambda i, n: (i, 0)),
                 pl.BlockSpec((1, wide), lambda i, n: (0, 0)),
             ],
         ),
@@ -112,6 +127,33 @@
             flops=10 * rows * seq * width, bytes_accessed=14 * rows * width, transcendentals=rows * seq * width // HEAD_DIM
         ),
     )(lengths, qkv, do)
+
+
+def hidden_grad_kernel(df_ref, w_ref, slope_ref, dh_ref, sums_ref):
+    dh = (mm_nt(df_ref[...], w_ref[...]) * slope_ref[...].astype(F32)).astype(BF)
+    dh_ref[...] = dh
+    sums_ref[...] = jnp.sum(dh.astype(F32), 0, keepdims=True)
+
+
+def hidden_grad(df, w_down, slope):
+    rows, dim = df.shape
+    units = w_down.shape[0]
+    tile = 256
+    return pl.pallas_call(
+        hidden_grad_kernel,
+        grid=(units // tile,),
+        in_specs=[
+            pl.BlockSpec((rows, dim), lambda i: (0, 0)),
+            pl.BlockSpec((tile, dim), lambda i: (i, 0)),
+            pl.BlockSpec((rows, tile), lambda i: (0, i)),
+        ],
+        out_specs=[pl.BlockSpec((rows, tile), lambda i: (0, i)), pl.BlockSpec((1, tile), lambda i: (0, i))],
+        out_shape=[jax.ShapeDtypeStruct((rows, units), BF), jax.ShapeDtypeStruct((1, units), F32)],
+        compiler_params=pltpu.CompilerParams(vmem_limit_bytes=56 * 2**20),
+        cost_estimate=pl.CostEstimate(
+            flops=2 * rows * dim * units, bytes_accessed=2 * (rows * dim + units * dim + 2 * rows * units), transcendentals=0
+        ),
+    )(df, w_down, slope)
 
 
 def pick_attn_kernel(me_ref, qkv, out, kept):
@@ -173,136 +215,99 @@
     )(me.reshape(1), up_weight, down_weight)
 
 
-def place_cols_kernel(me_ref, own, ax, ay, low, high, out):
-    width = own.shape[1]
+def place_cols_kernel(me_ref, own, ax, ay, low, high, out, parts):
+    width = own.shape[1] // parts
     me = me_ref[0]
-
-    def put(k, value):
-        out[:, pl.ds(pl.multiple_of((me ^ k) * width, width), width)] = value.astype(out.dtype)
-
-    put(0, own[...])
-    put(1, ax[...])
-    put(2, ay[...])
-
-    @pl.when(pl.program_id(1) == 0)
-    def _():
-        put(3, low[...])
-
-    @pl.when(pl.program_id(1) == 1)
-    def _():
-        put(3, high[...])
+    t, tiles = pl.program_id(0), pl.num_programs(0)
+
+    def put(k, piece):
+        for p in range(parts):
+            at = pl.multiple_of((p * 4 + (me ^ k)) * width, width)
+            out[:, pl.ds(at, width)] = piece[:, p * width : (p + 1) * width].astype(out.dtype)
+
+    put(0, own)
+    put(1, ax)
+    put(2, ay)
+
+    @pl.when(t < tiles // 2)
+    def _():
+        put(3, low)
+
+    @pl.when(t >= tiles // 2)
+    def _():
+        put(3, high)
 
 
 def place_cols(me, pieces, parts, dtype=F32):
-    own, low = pieces[0], pieces[3]
-    rows, cols = own.shape
-    width, half = cols // parts, rows // 2
-    tile = pl.BlockSpec((half, width), lambda p, t, m: (t, p))
-    part = pl.BlockSpec((half, width), lambda p, t, m: (0, p))
-    return pl.pallas_call(
-        place_cols_kernel,
+    cols = pieces[0].shape[1]
+    rows = 2 * pieces[3].shape[0]
+    tile = 64 if parts > 1 else 128
+    half = rows // (2 * tile)
+    full = pl.BlockSpec((tile, cols), lambda t, m: (t, 0))
+    return pl.pallas_call(
+        lambda *refs: place_cols_kernel(*refs, parts=parts),
         grid_spec=pltpu.PrefetchScalarGridSpec(
             num_scalar_prefetch=1,
-            grid=(parts, 2),
-            in_specs=[tile, tile, tile, part, part],
-            out_specs=pl.BlockSpec((half, 4 * width), lambda p, t, m: (t, p)),
+            grid=(rows // tile,),
+            in_specs=[
+                full,
+                full,
+                full,
+                pl.BlockSpec((tile, cols), lambda t, m: (jnp.minimum(t, half - 1), 0)),
+                pl.BlockSpec((tile, cols), lambda t, m: (jnp.maximum(t - half, 0), 0)),
+            ],
+            out_specs=pl.BlockSpec((tile, 4 * cols), lambda t, m: (t, 0)),
         ),
         out_shape=jax.ShapeDtypeStruct((rows, 4 * cols), dtype),
         cost_estimate=pl.CostEstimate(flops=0, bytes_accessed=24 * rows * cols, transcendentals=0),
     )(me.reshape(1), *pieces)
 
 
-def join_attn_kernel(me_ref, qkv, own, ax, ay, low, high, joined):
+def out_grad_kernel(me_ref, own, ax, ay, low, high, dt, small, joined):
     k = pl.program_id(0)
-    wide, half = qkv.shape[1], low.shape[0]
-    joined[:, :wide] = qkv[...]
-
-    @pl.when(k == 0)
-    def _():
-        joined[:, wide:] = own[...]
-
-    @pl.when(k == 1)
-    def _():
-        joined[:, wide:] = ax[...]
-
-    @pl.when(k == 2)
-    def _():
-        joined[:, wide:] = ay[...]
-
-    @pl.when(k == 3)
-    def _():
-        joined[:half, wide:] = low[...]
-        joined[half:, wide:] = high[...]
-
-
-def join_attn(me, qkv, pieces):
+    per, tall, _ = joined.shape
+    kept, rows, half = tall - PAD, dt.shape[0] // 4, low.shape[0]
+    joined[:, kept:, :] = small[...]
+
+    def heads(of, block):
+        if of < 3:
+            return (own, ax, ay)[of][block * rows : (block + 1) * rows, :]
+        ref, at = (low, block * rows) if block * rows < half else (high, block * rows - half)
+        return ref[at : at + rows, :]
+
+    def put(of):
+        grad = sum(mm_tn(heads(of, n ^ of), dt[n * rows : (n + 1) * rows, :]) for n in range(4)).astype(BF)
+        for i in range(per):
+            joined[i, :kept, :] = grad[i * kept : (i + 1) * kept, :]
+
+    for of in range(4):
+        pl.when(k == of)(lambda of=of: put(of))
+
+
+def out_grad(me, pieces, dt, small):
     own, low = pieces[0], pieces[3]
     rows, cols = own.shape
-    wide = qkv.shape[1]
+    shards = small.shape[0]
+    per = shards // 4
+    tall = cols // per + PAD
     full = pl.BlockSpec((rows, cols), lambda k, m: (0, 0))
     part = pl.BlockSpec((low.shape[0], cols), lambda k, m: (0, 0))
     return pl.pallas_call(
-        join_attn_kernel,
+        out_grad_kernel,
         grid_spec=pltpu.PrefetchScalarGridSpec(
             num_scalar_prefetch=1,
             grid=(4,),
-            in_specs=[pl.BlockSpec((rows, wide), lambda k, m: (m[0] ^ k, 0)), full, full, full, part, part],
-            out_specs=pl.BlockSpec((rows, wide + cols), lambda k, m: (m[0] ^ k, 0)),
-        ),
-        out_shape=jax.ShapeDtypeStruct((4 * rows, wide + cols), BF),
-        cost_estimate=pl.CostEstimate(flops=0, bytes_accessed=16 * rows * (wide + cols), transcendentals=0),
-    )(me.reshape(1), qkv, *pieces)
-
-
-def place_attn_kernel(me_ref, own, ax, ay, low, high, qkv, out):
-    width = own.shape[1]
-    me = me_ref[0]
-    p, t = pl.program_id(0), pl.program_id(1)
-
-    def put(k, value):
-        at = pl.ds(pl.multiple_of((me ^ k) * width, width), width)
-
-        @pl.when(p < 3)
-        def _():
-            qkv[:, at] = value.astype(F32)
-
-        @pl.when(p == 3)
-        def _():
-            out[:, at] = value.astype(F32)
-
-    put(0, own[...])
-    put(1, ax[...])
-    put(2, ay[...])
-
-    @pl.when(t == 0)
-    def _():
-        put(3, low[...])
-
-    @pl.when(t == 1)
-    def _():
-        put(3, high[...])
-
-
-def place_attn(me, pieces):
-    own, low = pieces[0], pieces[3]
-    rows, cols = own.shape
-    width, half = cols // 4, rows // 2
-    tile = pl.BlockSpec((half, width), lambda p, t, m: (t, p))
-    part = pl.BlockSpec((half, width), lambda p, t, m: (0, p))
-    return pl.pallas_call(
-        place_attn_kernel,
-        grid_spec=pltpu.PrefetchScalarGridSpec(
-            num_scalar_prefetch=1,
-            grid=(4, 2),
-            in_specs=[tile, tile, tile, part, part],
-            out_specs=[
-                pl.BlockSpec((half, cols), lambda p, t, m: (jnp.where(p < 3, t, 1), jnp.minimum(p, 2))),
-                pl.BlockSpec((half, cols), lambda p, t, m: (jnp.where(p < 3, 0, t), 0)),
+            in_specs=[full, full, full, part, part]
+            + [
+                pl.BlockSpec((rows, cols), lambda k, m: (0, m[0])),
+                pl.BlockSpec((per, PAD, cols), lambda k, m: (m[0] ^ k, 0, 0)),
             ],
-        ),
-        out_shape=[jax.ShapeDtypeStruct((rows, 3 * cols), F32), jax.ShapeDtypeStruct((rows, cols), F32)],
-        cost_estimate=pl.CostEstimate(flops=0, bytes_accessed=24 * rows * cols, transcendentals=0),
-    )(me.reshape(1), *pieces)
+            out_specs=pl.BlockSpec((per, tall, cols), lambda k, m: (m[0] ^ k, 0, 0)),
+        ),
+        out_shape=jax.ShapeDtypeStruct((shards, tall, cols), BF),
+        compiler_params=pltpu.CompilerParams(vmem_limit_bytes=40 * 2**20),
+        cost_estimate=pl.CostEstimate(flops=8 * rows * cols * cols, bytes_accessed=14 * rows * cols, transcendentals=0),
+    )(me.reshape(1), *pieces, dt, small)
 
 
 def place_rows_kernel(me_ref, own, ax, ay, low, high, out):
@@ -382,7 +387,7 @@
 
     def gather_far(self, near):
         own, ax, ay = near
-        half = own.shape[0] // 2
+        half = own.shape[0] // 32 * 16
         return [own, ax, ay, self.over_x(ay[:half]), self.over_y(ax[half:])]
 
     def gather_pieces(self, a, *meanwhile):
@@ -391,6 +396,11 @@
             near = lax.optimization_barrier(near + meanwhile)[:3]
         return self.gather_far(near)
 
+    def gather_direct(self, a):
+        half = a.shape[0] // 32 * 16
+        both = self.over_both(a)
+        return [a, self.over_x(a), self.over_y(a), both[:half], both[half:]]
+
     def gather_rows(self, a):
         if not self.square:
             return lax.all_gather(a, "rep", axis=0, tiled=True)
@@ -401,24 +411,27 @@
             return lax.all_gather(a, "rep", axis=0, tiled=True)
         return jnp.concatenate([a, self.over_x(a), self.over_y(a), lax.ppermute(a, "rep", self.ds)], 0)
 
-    def far_term(self, left, right, product):
+    def scatter_sum(self, left, right, product, whole=False, between=None, first=()):
         rows = left.shape[0] // self.reps
-        return product(left[3 * rows : 4 * rows], right).astype(BF) if self.square else None
-
-    def scatter_sum(self, left, right, product, far, late=()):
-        rows = left.shape[0] // self.reps
-        block = lambda a, k: product(a[k * rows : (k + 1) * rows], right)
+        full = product(left, right) if whole or not self.square else None
         if not self.square:
-            whole = jnp.concatenate([block(left, k).astype(BF) for k in range(self.reps)], 0)
-            return lax.psum_scatter(whole, "rep", scatter_dimension=0, tiled=True).astype(F32)
+            return lax.psum_scatter(full.astype(BF), "rep", scatter_dimension=0, tiled=True).astype(F32)
+        cut = lambda a, k: a[k * rows : (k + 1) * rows]
+        block = lambda a, k: cut(full, k) if whole else product(cut(a, k), right)
         half = rows // 2
+        if whole:
+            full = after(full, *first)
+        far = block(left, 3).astype(BF)
         for_y, for_x = self.over_x(far[:half]), self.over_y(far[half:])
         left = after(left, far)
         px, py = block(left, 1), block(left, 2)
         px = jnp.concatenate([px[:half], px[half:] + for_x.astype(F32)], 0).astype(BF)
         py = jnp.concatenate([py[:half] + for_y.astype(F32), py[half:]], 0).astype(BF)
         got_x, got_y = self.over_x(px), self.over_y(py)
-        return block(after(left, *late), 0) + got_x.astype(F32) + got_y.astype(F32)
+        own = block(left, 0)
+        if between is not None:
+            own = after(own, *between(px, py))
+        return own + got_x.astype(F32) + got_y.astype(F32)
 
     def over_both(self, a):
         return lax.ppermute(a, "rep", self.ds)
@@ -435,10 +448,7 @@
         return lax.all_gather(w, "fsdp", axis=0, tiled=True)
 
     def own_total(self, a):
-        if not self.square:
-            return lax.dynamic_index_in_dim(lax.psum(a, ("rep", "fsdp")), lax.axis_index("fsdp"), 0, False)
-        a = jnp.sum(lax.all_to_all(a, "fsdp", 0, 0, tiled=True), 0)
-        return a + self.over_x(a) + self.over_y(a) + self.over_both(a)
+        return lax.dynamic_index_in_dim(lax.psum(a, ("rep", "fsdp")), lax.axis_index("fsdp"), 0, False)
 
     def scatter_weight(self, g):
         return lax.psum_scatter(g, "fsdp", scatter_dimension=0, tiled=True)
@@ -507,7 +517,7 @@
     x_all = mv.gather_rows(x)
     qkv = (mm(x_all, w_qkv) + bias_qkv).astype(BF)
     o = attn_fwd(lens, qkv, seq)
-    attn = mv.scatter_sum(o, w_out, mm, mv.far_term(o, w_out, mm))
+    attn = mv.scatter_sum(o, w_out, mm)
     x1, n1, inv1 = norm_forward(x.astype(F32) + attn + b_out, g_attn, s_attn)
 
     x1_all = mv.gather_rows(x1.astype(BF))
@@ -519,7 +529,10 @@
         0.7978845608028654 * (1.0 + 3 * 0.044715 * hidden * hidden)
     )
     slope = slope.astype(BF)
-    branch = mv.scatter_sum(act, w_down, mm, mv.far_term(act, w_down, mm))
+    if fast:
+        o_pieces = mv.gather_pieces(after(o, x1_all))
+        act = after(act, *o_pieces)
+    branch = mv.scatter_sum(act, w_down, mm)
     result, n2, inv2 = norm_forward(x1 + branch + b_down, g_ffn, s_ffn)
     output = result.astype(BF).reshape(slots, seq, D)
 
@@ -532,33 +545,33 @@
     df_all = after(df_all, d_wdown)
     d_wdown = mv.scatter_weight(d_wdown)
     d_bdown = jnp.sum(df.astype(F32), 0)
-    dh = (mm_nt(df_all, w_down) * slope.astype(F32)).astype(BF)
-    d_bup = jnp.sum(dh.astype(F32), 0)
-    far = mv.far_term(dh, w_up, mm_nt)
-    d_wup = mm_tn(x1_all, after(dh, far) if fast else dh).astype(BF)
-    dx1 = dr2 + mv.scatter_sum(dh, w_up, mm_nt, far, (d_wup,))
-    d_wup = mv.scatter_weight(d_wup)
+    dh, d_bup = hidden_grad(df_all, w_down, slope)
+    def up_grad(*sent):
+        return [mm_tn(x1_all, after(dh, *sent)).astype(BF)]
+
+    kept = []
+
+    def keep_up_grad(*sent):
+        kept.extend(up_grad(*sent))
+        return kept
+
+    dx1 = dr2 + mv.scatter_sum(dh, w_up, mm_nt, True, keep_up_grad)
+    d_wup = mv.scatter_weight((kept or up_grad())[0])
 
     dr1, d_gattn, d_sattn = norm_backward(dx1, g_attn, n1, inv1)
     dt = dr1.astype(BF)
     dt_all = after(mv.gather_rows(dt), d_wdown)
     d_bout = jnp.sum(dt.astype(F32), 0)
-    d_wout = mm_tn(o, dt_all).astype(BF)
-    if fast:
-        out_pieces = mv.swap_pieces(lambda q: lax.dynamic_slice(d_wout, (0, q * dr), (dr, dr)))
     do = mm_nt(dt_all, w_out).astype(BF)
     dqkv, sums = attn_bwd(lens, qkv, do, seq)
+    if fast:
+        down_near = mv.gather_near(after(d_wdown, dt_all))
+        x_all = after(x_all, *down_near)
     d_wqkv = mm_tn(x_all, dqkv).astype(BF)
     if fast:
-        down_near = mv.gather_near(after(d_wdown, dt_all))
-        d_wattn = join_attn(r, after(d_wqkv, *down_near), out_pieces)
-        dqkv = after(dqkv, d_wattn)
-        d_wattn = mv.scatter_weight(d_wattn)
+        dqkv = after(dqkv, d_wqkv)
         down_pieces = mv.gather_far(down_near)
-    else:
-        d_wqkv = mv.scatter_weight(d_wqkv)
-        d_wout = mv.swap(d_wout.reshape(dr, reps, dr).transpose(1, 0, 2).reshape(reps * dr, dr))
-        d_wout = mv.scatter_weight(d_wout)
+    d_wqkv = mv.scatter_weight(d_wqkv)
 
     zero = jnp.zeros((2, D), F32)
     d_qv = lax.dynamic_update_slice(zero, jnp.stack([sums[0, :dr], sums[0, 2 * dr :]]), (0, r * dr)).reshape(-1)
@@ -567,18 +580,38 @@
     ).reshape(-1)
     grads = [d_qv, d_bout, d_gattn, d_sattn, d_bup, d_bdown, d_gffn, d_sffn]
     packed = jnp.concatenate([v.reshape(shards, -1) for v in grads], 1)
-    packed = mv.own_total(packed)
-
-    late = (packed, d_wup, *down_pieces) if fast else ()
-    input_grad = dr1 + mv.scatter_sum(dqkv, w_qkv, mm_nt, mv.far_term(dqkv, w_qkv, mm_nt), late)
+    if fast:
+        small = packed.astype(BF).reshape(shards, -1, dr)
+        small = jnp.pad(small, ((0, 0), (0, PAD - small.shape[1]), (0, 0)))
+    else:
+        packed = mv.own_total(packed)
+
+    def late_grads(*sent):
+        if fast:
+            up_near = mv.gather_near(after(d_wup, *sent))
+            placed = place_rows(r, after(down_pieces, *up_near))
+            d_wout = out_grad(r, o_pieces, after(dt_all, *sent), small)
+            kept.extend([d_wout.reshape(-1, dr), placed, up_near])
+            return kept[:1]
+        grad = mm_tn(after(o, *sent), dt_all).astype(BF)
+        return [mv.swap(grad.reshape(dr, reps, dr).transpose(1, 0, 2).reshape(reps * dr, dr))]
+
+    kept = []
+    input_grad = dr1 + mv.scatter_sum(dqkv, w_qkv, mm_nt, True, late_grads, down_pieces if fast else ())
+    d_wout = mv.scatter_weight((kept or late_grads())[0])
     input_grad = input_grad.reshape(slots, seq, D)
 
     if fast:
-        up_pieces = mv.gather_pieces(d_wup)
-        d_wdown = place_rows(r, down_pieces)
+        d_wdown = kept[1]
+        up_pieces = mv.gather_far(kept[2])
         d_wup = place_cols(r, up_pieces, shards)
-        attn_pieces = mv.gather_pieces(after(d_wattn, input_grad, *up_pieces), d_wdown, d_wup)
-        d_wqkv, d_wout = place_attn(r, attn_pieces)
+        qkv_near = mv.gather_near(after(d_wqkv, *up_pieces))
+        qkv_pieces = mv.gather_far(after(qkv_near, d_wup))
+        d_wqkv = place_cols(r, qkv_pieces, 3)
+        out_pieces = mv.gather_direct(after(d_wout, input_grad, d_wdown, d_wqkv))
+        d_wout = place_cols(r, out_pieces, 1)
+        below = [p[wrows:] for p in out_pieces[:3]] + [out_pieces[4][wrows - out_pieces[3].shape[0] :]]
+        packed = sum(p.astype(F32) for p in below).reshape(-1)[: sum(sizes)]
     else:
 
         def spread(shard, parts):

time: 689 us -> 680 us (0.987)
  waiting for transfers between devices: 293 us -> 333 us
  matrix products: 151 us -> 113 us
  blocking collectives: 26.5 us -> 14.7 us
  Pallas kernels: 75.4 us -> 67.5 us
  other arithmetic: 15.5 us -> 23.3 us
    ppermute x26 -> x27, waiting for transfers between devices: 102 us -> 147 us  [over_y(): return lax.ppermute(a, 'rep', self.ys)]
    dot_general x10 -> x3, matrix products: 63 us -> 29 us  [mm_nt(): lax.dot_general(a, b, (((1,), (1,)), ((), ())), preferred_element_type=F32)]
    all_gather x3, waiting for transfers between devices: 64.8 us -> 38.2 us  [gather_weight(): return lax.all_gather(w, 'fsdp', axis=0, tiled=True)]
    reduce_scatter x3 -> x4, waiting for transfers between devices: 1.82 us -> 18 us  [scatter_weight(): return lax.psum_scatter(g, 'fsdp', scatter_dimension=0, tiled=True)]
    all_to_all x1 -> x0, blocking collectives: 11.8 us -> none  [own_total(): a = jnp.sum(lax.all_to_all(a, 'fsdp', 0, 0, tiled=True), 0)]
    pallas_call x6 -> x8, Pallas kernels: 60.6 us -> 52.8 us  [the longest x4 18.1 us: place_cols(): pl.pallas_call(lambda *refs: place_cols_kernel(*refs, parts=parts), grid_...]
    dot_general x4 -> x3, matrix products: 39 us -> 34.3 us  [mm_tn(): lax.dot_general(a, b, (((0,), (0,)), ((), ())), preferred_element_type=F32)]
    ppermute x26 -> x27, waiting for transfers between devices: 121 us -> 123 us  [over_x(): return lax.ppermute(a, 'rep', self.xs)]
  transfers between devices with their start and end apart: 62 -> 64, of which waited for: 39 -> 46; matrix products, arithmetic and copies ran while one was open for 26% -> 21% of each run, Pallas kernels for 9% -> 9%
where the time goes in v3:
time: 680 us; the launch traced here: 674 us
  waiting for transfers between devices  333 us (49%)
  matrix products  113 us (17%)
  starting transfers between devices  68.1 us (10%)
  Pallas kernels  67.5 us (10%)
  local copies, waits for them, and re-layouts  38.7 us (6%)
  other arithmetic  23.3 us (3%)
  between operations  15.6 us (2%)
  blocking collectives  14.7 us (2%)
    ppermute x27, waiting for transfers between devices, over_y(): return lax.ppermute(a, 'rep', self.ys)  147 us
    ppermute x27, waiting for transfers between devices, over_x(): return lax.ppermute(a, 'rep', self.xs)  123 us
    dot_general x10, matrix products, mm(): return jnp.dot(a, b, preferred_element_type=F32)  49.6 us
    all_gather x3, waiting for transfers between devices, gather_weight(): return lax.all_gather(w, 'fsdp', axis=0, tiled=True)  38.2 us
    dot_general x3, matrix products, mm_tn(): lax.dot_general(a, b, (((0,), (0,)), ((), ())), preferred_element_type=F32)  34.3 us
    ppermute x27, starting transfers between devices, over_x(): return lax.ppermute(a, 'rep', self.xs)  30.1 us
    ppermute x27, starting transfers between devices, over_y(): return lax.ppermute(a, 'rep', self.ys)  30 us
    dot_general x3, matrix products, mm_nt(): lax.dot_general(a, b, (((1,), (1,)), ((), ())), preferred_element_type=F32)  29 us
  transfers between devices with their start and end apart: 64, of which 46 were waited for; matrix products, arithmetic and copies ran while one was open for 21% of the time, Pallas kernels for 9%

profile of v3, /device:TPU:0, one launch (start us, length us, event | category | flops | bytes accessed | tf_op | source)
XLA Modules:
  0.0 673.8 jit_solution(10309934054260628117)
XLA Ops:
  26.3 14.7 %all-gather = bf16[24576]{0:T(1024)(128)(2,1)S(1)} all-gather(bf16[3072]{0:T(1024)(128)(2,1)S(1)} %dynamic-update-slice.30), channel_id=2, replica_groups=mesh['rep'=4,'fsdp'=8] {'fsdp'}, dimensions={0}, use_global_device_ids=true | all-gather | bytes 55296 | tf_op jit(solution)/shard_map/all_gather | solution.py:487
  58.7 36.8 %all-gather.5.cloned.1.call-done = bf16[2048,2048]{1,0:T(8,128)(2,1)} async-done(((bf16[256,2048]{1,0:T(8,128)(2,1)}), bf16[2048,2048]{1,0:T(8,128)(2,1)}) %all-gather.5.cloned.1.call-update) | async-done | bytes 8388624 | tf_op jit(solution)/shard_map/all_gather | solution.py:448
  101.7 11.9 %add_convert_fusion.refs_1_ = bf16[1024,1536]{1,0:T(8,128)(2,1)} fusion(bf16[1024,2048]{1,0:T(8,128)(2,1)} %constant_dynamic-update-slice_fusion, bf16[2048,2048]{1,0:T(8,128)(2,1)} %all-gather.5.cloned.1.call-done, f32[1536]{0:T(1024)S(1)} %pad_maximum_fusion.8), kind=kOutput, calls=%fused_computation.13 | convolution fusion | flops 6445596672 | bytes 13637632 | tf_op jit(solution)/shard_map/dot_general | solution.py:18
  136.8 9.3 %collective-permute-done.10 = bf16[128,2048]{1,0:T(8,128)(2,1)S(1)} collective-permute-done((bf16[128,2048]{1,0:T(8,128)(2,1)S(1)}, bf16[128,2048]{1,0:T(8,128)(2,1)S(1)}, u32[]{:S(2)}, u32[]{:S(2)}) %collective-permute-start.10) | collective-permute-done | bytes 524320 | tf_op jit(solution)/shard_map/ppermute | solution.py:383
  149.7 21.0 %collective-permute-done.11 = bf16[256,2048]{1,0:T(8,128)(2,1)S(1)} collective-permute-done((bf16[256,2048]{1,0:T(8,128)(2,1)S(1)}, bf16[256,2048]{1,0:T(8,128)(2,1)S(1)}, u32[]{:S(2)}, u32[]{:S(2)}) %collective-permute-start.11) | collective-permute-done | bytes 1048608 | tf_op jit(solution)/shard_map/ppermute | solution.py:380
  177.1 21.4 %collective-permute-done.15 = bf16[256,2048]{1,0:T(8,128)(2,1)S(1)} collective-permute-done((bf16[256,2048]{1,0:T(8,128)(2,1)S(1)}, bf16[256,2048]{1,0:T(8,128)(2,1)S(1)}, u32[]{:S(2)}, u32[]{:S(2)}) %collective-permute-start.15) | collective-permute-done | bytes 1048608 | tf_op jit(solution)/shard_map/ppermute | solution.py:383
  201.0 9.8 %collective-permute-done.16 = bf16[128,2048]{1,0:T(8,128)(2,1)S(1)} collective-permute-done((bf16[128,2048]{1,0:T(8,128)(2,1)S(1)}, bf16[128,2048]{1,0:T(8,128)(2,1)S(1)}, u32[]{:S(2)}, u32[]{:S(2)}) %collective-permute-start.16) | collective-permute-done | bytes 524320 | tf_op jit(solution)/shard_map/ppermute | solution.py:380
  215.3 20.2 %collective-permute-done.19.ay = bf16[1024,512]{1,0:T(8,128)(2,1)S(1)} collective-permute-done((bf16[1024,512]{1,0:T(8,128)(2,1)S(1)}, bf16[1024,512]{1,0:T(8,128)(2,1)S(1)}, u32[]{:S(2)}, u32[]{:S(2)}) %collective-permute-start.19) | collective-permute-done | bytes 1048608 | tf_op jit(solution)/shard_map/ppermute | solution.py:383
  239.8 19.4 %fusion.6 = (bf16[1024,2048]{1,0:T(8,128)(2,1)}, bf16[1024,2048]{1,0:T(8,128)(2,1)}) fusion(f32[2048]{0:T(1024)S(1)} %bitcast.104, bf16[1024,2048]{1,0:T(8,128)(2,1)} %copy-done.21, bf16[2048,2048]{1,0:T(8,128)(2,1)} %all-gather.7.cloned.1.call-done), kind=kOutput, calls=%fused_computation.8 | convolution fusion | flops 8633974784 | bytes 20979712 | tf_op jit(solution)/shard_map/dot_general | solution.py:18
  289.7 17.5 %collective-permute-done.23 = bf16[256,2048]{1,0:T(8,128)(2,1)S(1)} collective-permute-done((bf16[256,2048]{1,0:T(8,128)(2,1)S(1)}, bf16[256,2048]{1,0:T(8,128)(2,1)S(1)}, u32[]{:S(2)}, u32[]{:S(2)}) %collective-permute-start.23) | collective-permute-done | bytes 1048608 | tf_op jit(solution)/shard_map/ppermute | solution.py:380
  315.3 19.7 %collective-permute-done.27 = bf16[256,2048]{1,0:T(8,128)(2,1)S(1)} collective-permute-done((bf16[256,2048]{1,0:T(8,128)(2,1)S(1)}, bf16[256,2048]{1,0:T(8,128)(2,1)S(1)}, u32[]{:S(2)}, u32[]{:S(2)}) %collective-permute-start.27) | collective-permute-done | bytes 1048608 | tf_op jit(solution)/shard_map/ppermute | solution.py:383
  338.8 9.0 %collective-permute-done.28 = bf16[128,2048]{1,0:T(8,128)(2,1)S(1)} collective-permute-done((bf16[128,2048]{1,0:T(8,128)(2,1)S(1)}, bf16[128,2048]{1,0:T(8,128)(2,1)S(1)}, u32[]{:S(2)}, u32[]{:S(2)}) %collective-permute-start.28) | collective-permute-done | bytes 524320 | tf_op jit(solution)/shard_map/ppermute | solution.py:380
  349.8 11.4 %convolution_convert_fusion.2 = bf16[2048,2048]{1,0:T(8,128)(2,1)} fusion(bf16[1024,2048]{1,0:T(8,128)(2,1)S(1)} %copy-done.35, bf16[1024,2048]{1,0:T(8,128)(2,1)S(1)} %constant_dynamic-update-slice_fusion.10.df_ref), kind=kOutput, calls=%fused_computation.12 | convolution fusion | flops 8594128896 | bytes 16777216 | tf_op jit(solution)/shard_map/dot_general | solution.py:26
  361.3 15.2 %shard_map.258 = (bf16[1024,2048]{1,0:T(8,128)(2,1)}, f32[1,2048]{1,0:T(1,128)}) custom-call(bf16[1024,2048]{1,0:T(8,128)(2,1)} %copy-done.20, bf16[2048,2048]{1,0:T(8,128)(2,1)} %all-gather.9.cloned.1.call-done.w_ref, bf16[1024,2048]{1,0:T(8,128)(2,1)} %get-tuple-element.94.slope_ref), custom_call_target="tpu_custom_call" | custom-call | flops 8589934592 | bytes 20971520 | tf_op jit(solution)/shard_map/pallas_call | solution.py:142
  376.5 12.6 %fusion.54 = f32[1024,2048]{1,0:T(8,128)S(1)} fusion(bf16[1024,2048]{1,0:T(8,128)(2,1)} %get-tuple-element.53, bf16[2048,2048]{1,0:T(8,128)(2,1)} %all-gather.7.cloned.1.call-done), kind=kOutput, calls=%fused_computation.154 | convolution fusion | flops 8589934592 | bytes 20971520 | tf_op jit(solution)/shard_map/dot_general | solution.py:22
  392.4 9.6 %collective-permute-done.30 = bf16[128,2048]{1,0:T(8,128)(2,1)S(1)} collective-permute-done((bf16[128,2048]{1,0:T(8,128)(2,1)S(1)}, bf16[128,2048]{1,0:T(8,128)(2,1)S(1)}, u32[]{:S(2)}, u32[]{:S(2)}) %collective-permute-start.30) | collective-permute-done | bytes 524320 | tf_op jit(solution)/shard_map/ppermute | solution.py:383
  406.4 11.4 %convolution_convert_fusion.1 = bf16[2048,2048]{1,0:T(8,128)(2,1)} fusion(bf16[1024,2048]{1,0:T(8,128)(2,1)S(1)} %copy-done.22, bf16[1024,2048]{1,0:T(8,128)(2,1)S(1)} %copy-done.36), kind=kOutput, calls=%fused_computation.11 | convolution fusion | flops 8594128896 | bytes 16777216 | tf_op jit(solution)/shard_map/dot_general | solution.py:26
  423.2 17.2 %collective-permute-done.32 = bf16[256,2048]{1,0:T(8,128)(2,1)S(1)} collective-permute-done((bf16[256,2048]{1,0:T(8,128)(2,1)}, bf16[256,2048]{1,0:T(8,128)(2,1)S(1)}, u32[]{:S(2)}, u32[]{:S(2)}) %collective-permute-start.32) | collective-permute-done | bytes 1048608 | tf_op jit(solution)/shard_map/ppermute | solution.py:380
  450.2 19.5 %collective-permute-done.35 = bf16[256,2048]{1,0:T(8,128)(2,1)S(1)} collective-permute-done((bf16[256,2048]{1,0:T(8,128)(2,1)S(1)}, bf16[256,2048]{1,0:T(8,128)(2,1)S(1)}, u32[]{:S(2)}, u32[]{:S(2)}) %collective-permute-start.35) | collective-permute-done | bytes 1048608 | tf_op jit(solution)/shard_map/ppermute | solution.py:383
  491.1 8.2 %shard_map.259 = (bf16[1024,1536]{1,0:T(8,128)(2,1)}, f32[1,1536]{1,0:T(1,128)}) custom-call(s32[8]{0:T(128)} %pad_add_fusion.refs_0_, bf16[1024,1536]{1,0:T(8,128)(2,1)} %add_convert_fusion.refs_1_, bf16[1024,512]{1,0:T(8,128)(2,1)} %convolution_convert_fusion.5.refs_2_), custom_call_target="tpu_custom_call" | custom-call | flops 671088640 | bytes 7340032 | tf_op jit(solution)/shard_map/pallas_call | solution.py:111
  506.6 11.5 %convolution_convert_fusion = bf16[2048,1536]{1,0:T(8,128)(2,1)} fusion(bf16[1024,2048]{1,0:T(8,128)(2,1)} %constant_dynamic-update-slice_fusion, bf16[1024,1536]{1,0:T(8,128)(2,1)} %get-tuple-element.59), kind=kOutput, calls=%fused_computation.10 | convolution fusion | flops 6445596672 | bytes 13631488 | tf_op jit(solution)/shard_map/dot_general | solution.py:26
  522.8 10.1 %fusion.7 = f32[1024,2048]{1,0:T(8,128)S(1)} fusion(bf16[1024,1536]{1,0:T(8,128)(2,1)} %get-tuple-element.59, bf16[2048,2048]{1,0:T(8,128)(2,1)} %all-gather.5.cloned.1.call-done), kind=kOutput, calls=%fused_computation.14 | convolution fusion | flops 6442450944 | bytes 17825792 | tf_op jit(solution)/shard_map/dot_general | solution.py:22
  555.0 19.9 %collective-permute-done.47.refs_3_ = bf16[256,2048]{1,0:T(8,128)(2,1)S(1)} collective-permute-done((bf16[256,2048]{1,0:T(8,128)(2,1)}, bf16[256,2048]{1,0:T(8,128)(2,1)S(1)}, u32[]{:S(2)}, u32[]{:S(2)}) %collective-permute-start.47) | collective-permute-done | bytes 1048608 | tf_op jit(solution)/shard_map/ppermute | solution.py:383
  594.0 16.3 %reduce-scatter.7.cloned.1.call-done.refs_1_ = bf16[256,1536]{1,0:T(8,128)(2,1)} async-done(((bf16[2048,1536]{1,0:T(8,128)(2,1)}), bf16[256,1536]{1,0:T(8,128)(2,1)}) %reduce-scatter.7.cloned.1.call-update) | async-done | bytes 786448 | tf_op jit(solution)/shard_map/reduce_scatter | solution.py:454
  (351 shorter events, 284.8 us)
Async XLA Ops:
  7.2 88.3 %all-gather.5.cloned.1.call-start = ((), (), s32[]{:S(2)}) async-start(), calls=%async_computation.4 | async-start | bytes 9437184 | tf_op jit(solution)/shard_map/all_gather | solution.py:448
  10.3 229.5 %all-gather.7.cloned.1.call-start = ((), (), s32[]{:S(2)}) async-start(), calls=%async_computation.5 | async-start | bytes 9437184 | tf_op jit(solution)/shard_map/all_gather | solution.py:448
  16.4 244.3 %all-gather.9.cloned.1.call-start = ((), (), s32[]{:S(2)}) async-start(), calls=%async_computation.6 | async-start | bytes 9437184 | tf_op jit(solution)/shard_map/all_gather | solution.py:448
  16.4 26.2 %collective-permute-start.4 = (bf16[256,2048]{1,0:T(8,128)(2,1)S(1)}, bf16[256,2048]{1,0:T(8,128)(2,1)S(1)}, u32[]{:S(2)}, u32[]{:S(2)}) collective-permute-start(bf16[256,2048]{1,0:T(8,128)(2,1)S(1)} %bitcast.80), channel_id=1, source_target_pairs={{0,16},{8,24},{16,0},{24,8},{1,17},{9,25},{17,1},{25,9},{2,18},{10... | collective-permute-start | bytes 3145736 | tf_op jit(solution)/shard_map/ppermute | solution.py:383
  19.5 25.6 %collective-permute-start.3 = (bf16[256,2048]{1,0:T(8,128)(2,1)S(1)}, bf16[256,2048]{1,0:T(8,128)(2,1)S(1)}, u32[]{:S(2)}, u32[]{:S(2)}) collective-permute-start(bf16[256,2048]{1,0:T(8,128)(2,1)S(1)} %bitcast.81), channel_id=1, source_target_pairs={{0,8},{8,0},{16,24},{24,16},{1,9},{9,1},{17,25},{25,17},{2,10},{10... | collective-permute-start | bytes 3145736 | tf_op jit(solution)/shard_map/ppermute | solution.py:380
  21.0 23.5 %collective-permute-start = (s32[2]{0:T(128)S(1)}, s32[2]{0:T(128)S(1)}, u32[]{:S(2)}, u32[]{:S(2)}) collective-permute-start(s32[2]{0:T(128)S(1)} %copy-done.25), channel_id=1, source_target_pairs={{0,8},{8,0},{16,24},{24,16},{1,9},{9,1},{17,25},{25,17},{2,10},{10... | collective-permute-start | bytes 32 | tf_op jit(solution)/shard_map/ppermute | solution.py:380
  24.5 459.1 %reduce-scatter.5.cloned.1.call-start = ((), (), s32[]{:S(2)}) async-start(), calls=%async_computation.7 | async-start | bytes 9437184 | tf_op jit(solution)/shard_map/reduce_scatter | solution.py:454
  100.7 24.1 %collective-permute-start.7 = (bf16[512,512]{1,0:T(8,128)(2,1)}, bf16[512,512]{1,0:T(8,128)(2,1)S(1)}, u32[]{:S(2)}, u32[]{:S(2)}) collective-permute-start(bf16[512,512]{1,0:T(8,128)(2,1)} %get-tuple-element.102), channel_id=1, source_target_pairs={{0,8},{8,0},{16,24},{24,16},{1,9},{9,1},{17,25},{25,17},{2,10},{10... | collective-permute-start | bytes 1572872 | tf_op jit(solution)/shard_map/ppermute | solution.py:380
  101.3 23.5 %collective-permute-start.8 = (bf16[512,512]{1,0:T(8,128)(2,1)S(1)}, bf16[512,512]{1,0:T(8,128)(2,1)S(1)}, u32[]{:S(2)}, u32[]{:S(2)}) collective-permute-start(bf16[512,512]{1,0:T(8,128)(2,1)S(1)} %get-tuple-element.101), channel_id=1, source_target_pairs={{0,16},{8,24},{16,0},{24,8},{1,17},{9,25},{17,1},{25,9},{2,18},{10... | collective-permute-start | bytes 1572872 | tf_op jit(solution)/shard_map/ppermute | solution.py:383
  146.3 24.4 %collective-permute-start.11 = (bf16[256,2048]{1,0:T(8,128)(2,1)S(1)}, bf16[256,2048]{1,0:T(8,128)(2,1)S(1)}, u32[]{:S(2)}, u32[]{:S(2)}) collective-permute-start(bf16[256,2048]{1,0:T(8,128)(2,1)S(1)} %pad_maximum_fusion), channel_id=1, source_target_pairs={{0,8},{8,0},{16,24},{24,16},{1,9},{9,1},{17,25},{25,17},{2,10},{10... | collective-permute-start | bytes 3145736 | tf_op jit(solution)/shard_map/ppermute | solution.py:380
  148.6 24.1 %collective-permute-start.13 = (bf16[256,2048]{1,0:T(8,128)(2,1)S(1)}, bf16[256,2048]{1,0:T(8,128)(2,1)S(1)}, u32[]{:S(2)}, u32[]{:S(2)}) collective-permute-start(bf16[256,2048]{1,0:T(8,128)(2,1)S(1)} %pad_maximum_fusion.1), channel_id=1, source_target_pairs={{0,16},{8,24},{16,0},{24,8},{1,17},{9,25},{17,1},{25,9},{2,18},{10... | collective-permute-start | bytes 3145736 | tf_op jit(solution)/shard_map/ppermute | solution.py:383
  175.2 23.2 %collective-permute-start.15 = (bf16[256,2048]{1,0:T(8,128)(2,1)S(1)}, bf16[256,2048]{1,0:T(8,128)(2,1)S(1)}, u32[]{:S(2)}, u32[]{:S(2)}) collective-permute-start(bf16[256,2048]{1,0:T(8,128)(2,1)S(1)} %get-tuple-element.93), channel_id=1, source_target_pairs={{0,16},{8,24},{16,0},{24,8},{1,17},{9,25},{17,1},{25,9},{2,18},{10... | collective-permute-start | bytes 3145736 | tf_op jit(solution)/shard_map/ppermute | solution.py:383
  176.4 24.1 %collective-permute-start.14 = (bf16[256,2048]{1,0:T(8,128)(2,1)S(1)}, bf16[256,2048]{1,0:T(8,128)(2,1)S(1)}, u32[]{:S(2)}, u32[]{:S(2)}) collective-permute-start(bf16[256,2048]{1,0:T(8,128)(2,1)S(1)} %get-tuple-element.93), channel_id=1, source_target_pairs={{0,8},{8,0},{16,24},{24,16},{1,9},{9,1},{17,25},{25,17},{2,10},{10... | collective-permute-start | bytes 3145736 | tf_op jit(solution)/shard_map/ppermute | solution.py:380
  213.6 23.6 %collective-permute-start.18 = (bf16[1024,512]{1,0:T(8,128)(2,1)S(1)}, bf16[1024,512]{1,0:T(8,128)(2,1)S(1)}, u32[]{:S(2)}, u32[]{:S(2)}) collective-permute-start(bf16[1024,512]{1,0:T(8,128)(2,1)S(1)} %copy-done), channel_id=1, source_target_pairs={{0,8},{8,0},{16,24},{24,16},{1,9},{9,1},{17,25},{25,17},{2,10},{10... | collective-permute-start | bytes 3145736 | tf_op jit(solution)/shard_map/ppermute | solution.py:380
  281.3 26.0 %collective-permute-start.23 = (bf16[256,2048]{1,0:T(8,128)(2,1)S(1)}, bf16[256,2048]{1,0:T(8,128)(2,1)S(1)}, u32[]{:S(2)}, u32[]{:S(2)}) collective-permute-start(bf16[256,2048]{1,0:T(8,128)(2,1)S(1)} %pad_maximum_fusion.2), channel_id=1, source_target_pairs={{0,8},{8,0},{16,24},{24,16},{1,9},{9,1},{17,25},{25,17},{2,10},{10... | collective-permute-start | bytes 3145736 | tf_op jit(solution)/shard_map/ppermute | solution.py:380
  286.0 23.2 %collective-permute-start.25 = (bf16[256,2048]{1,0:T(8,128)(2,1)S(1)}, bf16[256,2048]{1,0:T(8,128)(2,1)S(1)}, u32[]{:S(2)}, u32[]{:S(2)}) collective-permute-start(bf16[256,2048]{1,0:T(8,128)(2,1)S(1)} %pad_maximum_fusion.3), channel_id=1, source_target_pairs={{0,16},{8,24},{16,0},{24,8},{1,17},{9,25},{17,1},{25,9},{2,18},{10... | collective-permute-start | bytes 3145736 | tf_op jit(solution)/shard_map/ppermute | solution.py:383
  313.9 24.6 %collective-permute-start.26 = (bf16[256,2048]{1,0:T(8,128)(2,1)S(1)}, bf16[256,2048]{1,0:T(8,128)(2,1)S(1)}, u32[]{:S(2)}, u32[]{:S(2)}) collective-permute-start(bf16[256,2048]{1,0:T(8,128)(2,1)S(1)} %get-tuple-element.85), channel_id=1, source_target_pairs={{0,8},{8,0},{16,24},{24,16},{1,9},{9,1},{17,25},{25,17},{2,10},{10... | collective-permute-start | bytes 3145736 | tf_op jit(solution)/shard_map/ppermute | solution.py:380
  361.3 192.2 %reduce-scatter.9.cloned.1.call-start = ((), (), s32[]{:S(2)}) async-start(), calls=%async_computation.9 | async-start | bytes 9437184 | tf_op jit(solution)/shard_map/reduce_scatter | solution.py:454
  417.9 192.4 %reduce-scatter.7.cloned.1.call-start = ((), (), s32[]{:S(2)}) async-start(), calls=%async_computation.8 | async-start | bytes 7077888 | tf_op jit(solution)/shard_map/reduce_scatter | solution.py:454
  449.8 23.6 %collective-permute-start.34 = (bf16[256,2048]{1,0:T(8,128)(2,1)S(1)}, bf16[256,2048]{1,0:T(8,128)(2,1)S(1)}, u32[]{:S(2)}, u32[]{:S(2)}) collective-permute-start(bf16[256,2048]{1,0:T(8,128)(2,1)S(1)} %get-tuple-element.87), channel_id=1, source_target_pairs={{0,8},{8,0},{16,24},{24,16},{1,9},{9,1},{17,25},{25,17},{2,10},{10... | collective-permute-start | bytes 3145736 | tf_op jit(solution)/shard_map/ppermute | solution.py:380
  518.1 128.9 %reduce-scatter.11.cloned.1.call-start = ((), (), s32[]{:S(2)}) async-start(), calls=%async_computation.10 | async-start | bytes 2506752 | tf_op jit(solution)/shard_map/reduce_scatter | solution.py:454
  554.0 23.2 %collective-permute-start.46 = (bf16[256,2048]{1,0:T(8,128)(2,1)}, bf16[256,2048]{1,0:T(8,128)(2,1)S(1)}, u32[]{:S(2)}, u32[]{:S(2)}) collective-permute-start(bf16[256,2048]{1,0:T(8,128)(2,1)} %reduce-scatter.9.cloned.1.call-done.refs_1_), channel_id=1, source_target_pairs={{0,8},{8,0},{16,24},{24,16},{1,9},{9,1},{17,25},{25,17},{2,10},{10... | collective-permute-start | bytes 3145736 | tf_op jit(solution)/shard_map/ppermute | solution.py:380
  581.0 52.1 %collective-permute-start.44 = (bf16[256,2048]{1,0:T(8,128)(2,1)}, bf16[256,2048]{1,0:T(8,128)(2,1)}, u32[]{:S(2)}, u32[]{:S(2)}) collective-permute-start(bf16[256,2048]{1,0:T(8,128)(2,1)} %pad_maximum_fusion.6), channel_id=1, source_target_pairs={{0,8},{8,0},{16,24},{24,16},{1,9},{9,1},{17,25},{25,17},{2,10},{10... | collective-permute-start | bytes 3145736 | tf_op jit(solution)/shard_map/ppermute | solution.py:380
  581.8 51.3 %collective-permute-start.45 = (bf16[256,2048]{1,0:T(8,128)(2,1)}, bf16[256,2048]{1,0:T(8,128)(2,1)}, u32[]{:S(2)}, u32[]{:S(2)}) collective-permute-start(bf16[256,2048]{1,0:T(8,128)(2,1)} %pad_maximum_fusion.7), channel_id=1, source_target_pairs={{0,16},{8,24},{16,0},{24,8},{1,17},{9,25},{17,1},{25,9},{2,18},{10... | collective-permute-start | bytes 3145736 | tf_op jit(solution)/shard_map/ppermute | solution.py:383
  (78 other events, 903.4 us)
Sparse Core Ops, SparseCore 0:
  10.4 85.0 all-gather.4
  97.7 80.6 all-gather.6
  180.0 80.5 all-gather.8
  361.4 87.1 reduce-scatter.4
  451.3 87.9 reduce-scatter.8
  542.0 68.1 reduce-scatter.6
  612.6 34.3 reduce-scatter.10

commit v4 on v3

--- a/solution.py
+++ b/solution.py
@@ -449,6 +449,16 @@
 
     def own_total(self, a):
         return lax.dynamic_index_in_dim(lax.psum(a, ("rep", "fsdp")), lax.axis_index("fsdp"), 0, False)
+
+    def scatter_paired(self, g):
+        shards = self.shards
+        core = lax.axis_index("fsdp") % 2
+        g = g.reshape(shards // 2, 2, g.shape[0] // shards, g.shape[1])
+        take = lambda i: lax.dynamic_index_in_dim(g, i, 1, False)
+        got = lax.ppermute(take(1 - core), "fsdp", [(i, i ^ 1) for i in range(shards)])
+        both = (take(core).astype(F32) + got.astype(F32)).astype(BF).reshape(-1, g.shape[3])
+        lines = [list(range(0, shards, 2)), list(range(1, shards, 2))]
+        return lax.psum_scatter(both, "fsdp", scatter_dimension=0, axis_index_groups=lines, tiled=True)
 
     def scatter_weight(self, g):
         return lax.psum_scatter(g, "fsdp", scatter_dimension=0, tiled=True)
@@ -598,7 +608,8 @@
 
     kept = []
     input_grad = dr1 + mv.scatter_sum(dqkv, w_qkv, mm_nt, True, late_grads, down_pieces if fast else ())
-    d_wout = mv.scatter_weight((kept or late_grads())[0])
+    d_wout = (kept or late_grads())[0]
+    d_wout = mv.scatter_paired(d_wout) if fast else mv.scatter_weight(d_wout)
     input_grad = input_grad.reshape(slots, seq, D)
 
     if fast:
@@ -607,8 +618,8 @@
         d_wup = place_cols(r, up_pieces, shards)
         qkv_near = mv.gather_near(after(d_wqkv, *up_pieces))
         qkv_pieces = mv.gather_far(after(qkv_near, d_wup))
+        out_pieces = mv.gather_direct(after(d_wout, d_wdown, input_grad, *qkv_pieces))
         d_wqkv = place_cols(r, qkv_pieces, 3)
-        out_pieces = mv.gather_direct(after(d_wout, input_grad, d_wdown, d_wqkv))
         d_wout = place_cols(r, out_pieces, 1)
         below = [p[wrows:] for p in out_pieces[:3]] + [out_pieces[4][wrows - out_pieces[3].shape[0] :]]
         packed = sum(p.astype(F32) for p in below).reshape(-1)[: sum(sizes)]

time: 680 us -> 679 us (level)
    ppermute x27, waiting for transfers between devices: 123 us -> 132 us  [over_x(): return lax.ppermute(a, 'rep', self.xs)]
    reduce_scatter x4 -> x3, waiting for transfers between devices: 18 us -> 13.5 us  [scatter_weight(): return lax.psum_scatter(g, 'fsdp', scatter_dimension=0, tiled=True)]
    unnamed x114 -> x120, local copies, waits for them, and re-layouts: 20.8 us -> 19.2 us
  transfers between devices with their start and end apart: 64 -> 65, of which waited for: 46 -> 46; matrix products, arithmetic and copies ran while one was open for 21% -> 21% of each run, Pallas kernels for 9% -> 9%
where the time goes in v4:
time: 679 us; the launch traced here: 675 us
  waiting for transfers between devices  335 us (49%)
  matrix products  112 us (16%)
  starting transfers between devices  66.9 us (10%)
  Pallas kernels  66.6 us (10%)
  local copies, waits for them, and re-layouts  38.1 us (6%)
  other arithmetic  25.8 us (4%)
  between operations  15.6 us (2%)
  blocking collectives  14.7 us (2%)
    ppermute x27, waiting for transfers between devices, over_y(): return lax.ppermute(a, 'rep', self.ys)  148 us
    ppermute x27, waiting for transfers between devices, over_x(): return lax.ppermute(a, 'rep', self.xs)  132 us
    dot_general x10, matrix products, mm(): return jnp.dot(a, b, preferred_element_type=F32)  49.6 us
    all_gather x3, waiting for transfers between devices, gather_weight(): return lax.all_gather(w, 'fsdp', axis=0, tiled=True)  38.1 us
    dot_general x3, matrix products, mm_tn(): lax.dot_general(a, b, (((0,), (0,)), ((), ())), preferred_element_type=F32)  34.3 us
    ppermute x27, starting transfers between devices, over_x(): return lax.ppermute(a, 'rep', self.xs)  31.1 us
    ppermute x27, starting transfers between devices, over_y(): return lax.ppermute(a, 'rep', self.ys)  29.2 us
    dot_general x3, matrix products, mm_nt(): lax.dot_general(a, b, (((1,), (1,)), ((), ())), preferred_element_type=F32)  28.3 us
  transfers between devices with their start and end apart: 65, of which 46 were waited for; matrix products, arithmetic and copies ran while one was open for 21% of the time, Pallas kernels for 9%

profile of v4, /device:TPU:0, one launch (start us, length us, event | category | flops | bytes accessed | tf_op | source)
XLA Modules:
  0.0 674.6 jit_solution(1198232402469159998)
XLA Ops:
  26.3 14.7 %all-gather = bf16[24576]{0:T(1024)(128)(2,1)S(1)} all-gather(bf16[3072]{0:T(1024)(128)(2,1)S(1)} %dynamic-update-slice.30), channel_id=2, replica_groups=mesh['rep'=4,'fsdp'=8] {'fsdp'}, dimensions={0}, use_global_device_ids=true | all-gather | bytes 55296 | tf_op jit(solution)/shard_map/all_gather | solution.py:497
  58.6 36.9 %all-gather.5.cloned.1.call-done = bf16[2048,2048]{1,0:T(8,128)(2,1)} async-done(((bf16[256,2048]{1,0:T(8,128)(2,1)}), bf16[2048,2048]{1,0:T(8,128)(2,1)}) %all-gather.5.cloned.1.call-update) | async-done | bytes 8388624 | tf_op jit(solution)/shard_map/all_gather | solution.py:448
  101.7 11.9 %add_convert_fusion.refs_1_ = bf16[1024,1536]{1,0:T(8,128)(2,1)} fusion(bf16[1024,2048]{1,0:T(8,128)(2,1)} %constant_dynamic-update-slice_fusion, bf16[2048,2048]{1,0:T(8,128)(2,1)} %all-gather.5.cloned.1.call-done, f32[1536]{0:T(1024)S(1)} %pad_maximum_fusion.8), kind=kOutput, calls=%fused_computation.13 | convolution fusion | flops 6445596672 | bytes 13637632 | tf_op jit(solution)/shard_map/dot_general | solution.py:18
  136.9 9.2 %collective-permute-done.10 = bf16[128,2048]{1,0:T(8,128)(2,1)S(1)} collective-permute-done((bf16[128,2048]{1,0:T(8,128)(2,1)S(1)}, bf16[128,2048]{1,0:T(8,128)(2,1)S(1)}, u32[]{:S(2)}, u32[]{:S(2)}) %collective-permute-start.10) | collective-permute-done | bytes 524320 | tf_op jit(solution)/shard_map/ppermute | solution.py:383
  149.8 20.9 %collective-permute-done.11 = bf16[256,2048]{1,0:T(8,128)(2,1)S(1)} collective-permute-done((bf16[256,2048]{1,0:T(8,128)(2,1)S(1)}, bf16[256,2048]{1,0:T(8,128)(2,1)S(1)}, u32[]{:S(2)}, u32[]{:S(2)}) %collective-permute-start.11) | collective-permute-done | bytes 1048608 | tf_op jit(solution)/shard_map/ppermute | solution.py:380
  177.0 21.4 %collective-permute-done.15 = bf16[256,2048]{1,0:T(8,128)(2,1)S(1)} collective-permute-done((bf16[256,2048]{1,0:T(8,128)(2,1)S(1)}, bf16[256,2048]{1,0:T(8,128)(2,1)S(1)}, u32[]{:S(2)}, u32[]{:S(2)}) %collective-permute-start.15) | collective-permute-done | bytes 1048608 | tf_op jit(solution)/shard_map/ppermute | solution.py:383
  200.9 9.9 %collective-permute-done.16 = bf16[128,2048]{1,0:T(8,128)(2,1)S(1)} collective-permute-done((bf16[128,2048]{1,0:T(8,128)(2,1)S(1)}, bf16[128,2048]{1,0:T(8,128)(2,1)S(1)}, u32[]{:S(2)}, u32[]{:S(2)}) %collective-permute-start.16) | collective-permute-done | bytes 524320 | tf_op jit(solution)/shard_map/ppermute | solution.py:380
  215.3 20.3 %collective-permute-done.19.ay = bf16[1024,512]{1,0:T(8,128)(2,1)S(1)} collective-permute-done((bf16[1024,512]{1,0:T(8,128)(2,1)S(1)}, bf16[1024,512]{1,0:T(8,128)(2,1)S(1)}, u32[]{:S(2)}, u32[]{:S(2)}) %collective-permute-start.19) | collective-permute-done | bytes 1048608 | tf_op jit(solution)/shard_map/ppermute | solution.py:383
  239.9 19.5 %fusion.6 = (bf16[1024,2048]{1,0:T(8,128)(2,1)}, bf16[1024,2048]{1,0:T(8,128)(2,1)}) fusion(f32[2048]{0:T(1024)S(1)} %bitcast.115, bf16[1024,2048]{1,0:T(8,128)(2,1)} %copy-done.24, bf16[2048,2048]{1,0:T(8,128)(2,1)} %all-gather.7.cloned.1.call-done), kind=kOutput, calls=%fused_computation.8 | convolution fusion | flops 8633974784 | bytes 20979712 | tf_op jit(solution)/shard_map/dot_general | solution.py:18
  289.8 17.4 %collective-permute-done.23 = bf16[256,2048]{1,0:T(8,128)(2,1)S(1)} collective-permute-done((bf16[256,2048]{1,0:T(8,128)(2,1)S(1)}, bf16[256,2048]{1,0:T(8,128)(2,1)S(1)}, u32[]{:S(2)}, u32[]{:S(2)}) %collective-permute-start.23) | collective-permute-done | bytes 1048608 | tf_op jit(solution)/shard_map/ppermute | solution.py:380
  315.3 19.7 %collective-permute-done.27 = bf16[256,2048]{1,0:T(8,128)(2,1)S(1)} collective-permute-done((bf16[256,2048]{1,0:T(8,128)(2,1)S(1)}, bf16[256,2048]{1,0:T(8,128)(2,1)S(1)}, u32[]{:S(2)}, u32[]{:S(2)}) %collective-permute-start.27) | collective-permute-done | bytes 1048608 | tf_op jit(solution)/shard_map/ppermute | solution.py:383
  338.7 9.0 %collective-permute-done.28 = bf16[128,2048]{1,0:T(8,128)(2,1)S(1)} collective-permute-done((bf16[128,2048]{1,0:T(8,128)(2,1)S(1)}, bf16[128,2048]{1,0:T(8,128)(2,1)S(1)}, u32[]{:S(2)}, u32[]{:S(2)}) %collective-permute-start.28) | collective-permute-done | bytes 524320 | tf_op jit(solution)/shard_map/ppermute | solution.py:380
  349.8 11.4 %convolution_convert_fusion.2 = bf16[2048,2048]{1,0:T(8,128)(2,1)} fusion(bf16[1024,2048]{1,0:T(8,128)(2,1)S(1)} %copy-done.38, bf16[1024,2048]{1,0:T(8,128)(2,1)S(1)} %constant_dynamic-update-slice_fusion.10.df_ref), kind=kOutput, calls=%fused_computation.12 | convolution fusion | flops 8594128896 | bytes 16777216 | tf_op jit(solution)/shard_map/dot_general | solution.py:26
  361.3 15.2 %shard_map.258 = (bf16[1024,2048]{1,0:T(8,128)(2,1)}, f32[1,2048]{1,0:T(1,128)}) custom-call(bf16[1024,2048]{1,0:T(8,128)(2,1)} %copy-done.23, bf16[2048,2048]{1,0:T(8,128)(2,1)} %all-gather.9.cloned.1.call-done.w_ref, bf16[1024,2048]{1,0:T(8,128)(2,1)} %get-tuple-element.92.slope_ref), custom_call_target="tpu_custom_call" | custom-call | flops 8589934592 | bytes 20971520 | tf_op jit(solution)/shard_map/pallas_call | solution.py:142
  376.5 12.6 %fusion.55 = f32[1024,2048]{1,0:T(8,128)S(1)} fusion(bf16[1024,2048]{1,0:T(8,128)(2,1)} %get-tuple-element.52, bf16[2048,2048]{1,0:T(8,128)(2,1)} %all-gather.7.cloned.1.call-done), kind=kOutput, calls=%fused_computation.157 | convolution fusion | flops 8589934592 | bytes 20971520 | tf_op jit(solution)/shard_map/dot_general | solution.py:22
  392.3 9.6 %collective-permute-done.30 = bf16[128,2048]{1,0:T(8,128)(2,1)S(1)} collective-permute-done((bf16[128,2048]{1,0:T(8,128)(2,1)S(1)}, bf16[128,2048]{1,0:T(8,128)(2,1)S(1)}, u32[]{:S(2)}, u32[]{:S(2)}) %collective-permute-start.30) | collective-permute-done | bytes 524320 | tf_op jit(solution)/shard_map/ppermute | solution.py:383
  406.4 11.4 %convolution_convert_fusion.1 = bf16[2048,2048]{1,0:T(8,128)(2,1)} fusion(bf16[1024,2048]{1,0:T(8,128)(2,1)S(1)} %copy-done.25, bf16[1024,2048]{1,0:T(8,128)(2,1)S(1)} %copy-done.39), kind=kOutput, calls=%fused_computation.11 | convolution fusion | flops 8594128896 | bytes 16777216 | tf_op jit(solution)/shard_map/dot_general | solution.py:26
  421.2 19.2 %collective-permute-done.32 = bf16[256,2048]{1,0:T(8,128)(2,1)S(1)} collective-permute-done((bf16[256,2048]{1,0:T(8,128)(2,1)}, bf16[256,2048]{1,0:T(8,128)(2,1)S(1)}, u32[]{:S(2)}, u32[]{:S(2)}) %collective-permute-start.32) | collective-permute-done | bytes 1048608 | tf_op jit(solution)/shard_map/ppermute | solution.py:380
  450.1 19.5 %collective-permute-done.35 = bf16[256,2048]{1,0:T(8,128)(2,1)S(1)} collective-permute-done((bf16[256,2048]{1,0:T(8,128)(2,1)S(1)}, bf16[256,2048]{1,0:T(8,128)(2,1)S(1)}, u32[]{:S(2)}, u32[]{:S(2)}) %collective-permute-start.35) | collective-permute-done | bytes 1048608 | tf_op jit(solution)/shard_map/ppermute | solution.py:383
  506.5 11.5 %convolution_convert_fusion = bf16[2048,1536]{1,0:T(8,128)(2,1)} fusion(bf16[1024,2048]{1,0:T(8,128)(2,1)} %constant_dynamic-update-slice_fusion, bf16[1024,1536]{1,0:T(8,128)(2,1)} %get-tuple-element.58), kind=kOutput, calls=%fused_computation.10 | convolution fusion | flops 6445596672 | bytes 13631488 | tf_op jit(solution)/shard_map/dot_general | solution.py:26
  522.6 10.0 %fusion.7 = f32[1024,2048]{1,0:T(8,128)S(1)} fusion(bf16[1024,1536]{1,0:T(8,128)(2,1)} %get-tuple-element.58, bf16[2048,2048]{1,0:T(8,128)(2,1)} %all-gather.5.cloned.1.call-done), kind=kOutput, calls=%fused_computation.14 | convolution fusion | flops 6442450944 | bytes 17825792 | tf_op jit(solution)/shard_map/dot_general | solution.py:22
  559.2 20.1 %collective-permute-done.47.refs_3_ = bf16[256,2048]{1,0:T(8,128)(2,1)S(1)} collective-permute-done((bf16[256,2048]{1,0:T(8,128)(2,1)}, bf16[256,2048]{1,0:T(8,128)(2,1)S(1)}, u32[]{:S(2)}, u32[]{:S(2)}) %collective-permute-start.47) | collective-permute-done | bytes 1048608 | tf_op jit(solution)/shard_map/ppermute | solution.py:383
  584.7 9.7 %collective-permute-done.48.refs_4_ = bf16[128,2048]{1,0:T(8,128)(2,1)} collective-permute-done((bf16[128,2048]{1,0:T(8,128)(2,1)S(1)}, bf16[128,2048]{1,0:T(8,128)(2,1)}, u32[]{:S(2)}, u32[]{:S(2)}) %collective-permute-start.48) | collective-permute-done | bytes 524320 | tf_op jit(solution)/shard_map/ppermute | solution.py:380
  596.7 13.5 %reduce-scatter.7.cloned.1.call-done.refs_1_ = bf16[256,1536]{1,0:T(8,128)(2,1)} async-done(((bf16[2048,1536]{1,0:T(8,128)(2,1)}), bf16[256,1536]{1,0:T(8,128)(2,1)}) %reduce-scatter.7.cloned.1.call-update) | async-done | bytes 786448 | tf_op jit(solution)/shard_map/reduce_scatter | solution.py:464
  (362 shorter events, 284.5 us)
Async XLA Ops:
  7.2 88.4 %all-gather.5.cloned.1.call-start = ((), (), s32[]{:S(2)}) async-start(), calls=%async_computation.4 | async-start | bytes 9437184 | tf_op jit(solution)/shard_map/all_gather | solution.py:448
  10.3 229.6 %all-gather.7.cloned.1.call-start = ((), (), s32[]{:S(2)}) async-start(), calls=%async_computation.5 | async-start | bytes 9437184 | tf_op jit(solution)/shard_map/all_gather | solution.py:448
  16.4 244.3 %all-gather.9.cloned.1.call-start = ((), (), s32[]{:S(2)}) async-start(), calls=%async_computation.6 | async-start | bytes 9437184 | tf_op jit(solution)/shard_map/all_gather | solution.py:448
  16.4 26.2 %collective-permute-start.4 = (bf16[256,2048]{1,0:T(8,128)(2,1)S(1)}, bf16[256,2048]{1,0:T(8,128)(2,1)S(1)}, u32[]{:S(2)}, u32[]{:S(2)}) collective-permute-start(bf16[256,2048]{1,0:T(8,128)(2,1)S(1)} %bitcast.91), channel_id=1, source_target_pairs={{0,16},{8,24},{16,0},{24,8},{1,17},{9,25},{17,1},{25,9},{2,18},{10... | collective-permute-start | bytes 3145736 | tf_op jit(solution)/shard_map/ppermute | solution.py:383
  19.5 25.6 %collective-permute-start.3 = (bf16[256,2048]{1,0:T(8,128)(2,1)S(1)}, bf16[256,2048]{1,0:T(8,128)(2,1)S(1)}, u32[]{:S(2)}, u32[]{:S(2)}) collective-permute-start(bf16[256,2048]{1,0:T(8,128)(2,1)S(1)} %bitcast.92), channel_id=1, source_target_pairs={{0,8},{8,0},{16,24},{24,16},{1,9},{9,1},{17,25},{25,17},{2,10},{10... | collective-permute-start | bytes 3145736 | tf_op jit(solution)/shard_map/ppermute | solution.py:380
  20.9 23.5 %collective-permute-start = (s32[2]{0:T(128)S(1)}, s32[2]{0:T(128)S(1)}, u32[]{:S(2)}, u32[]{:S(2)}) collective-permute-start(s32[2]{0:T(128)S(1)} %copy-done.28), channel_id=1, source_target_pairs={{0,8},{8,0},{16,24},{24,16},{1,9},{9,1},{17,25},{25,17},{2,10},{10... | collective-permute-start | bytes 32 | tf_op jit(solution)/shard_map/ppermute | solution.py:380
  24.5 459.0 %reduce-scatter.5.cloned.1.call-start = ((), (), s32[]{:S(2)}) async-start(), calls=%async_computation.7 | async-start | bytes 9437184 | tf_op jit(solution)/shard_map/reduce_scatter | solution.py:464
  100.8 24.1 %collective-permute-start.7 = (bf16[512,512]{1,0:T(8,128)(2,1)}, bf16[512,512]{1,0:T(8,128)(2,1)S(1)}, u32[]{:S(2)}, u32[]{:S(2)}) collective-permute-start(bf16[512,512]{1,0:T(8,128)(2,1)} %get-tuple-element.100), channel_id=1, source_target_pairs={{0,8},{8,0},{16,24},{24,16},{1,9},{9,1},{17,25},{25,17},{2,10},{10... | collective-permute-start | bytes 1572872 | tf_op jit(solution)/shard_map/ppermute | solution.py:380
  101.3 23.5 %collective-permute-start.8 = (bf16[512,512]{1,0:T(8,128)(2,1)S(1)}, bf16[512,512]{1,0:T(8,128)(2,1)S(1)}, u32[]{:S(2)}, u32[]{:S(2)}) collective-permute-start(bf16[512,512]{1,0:T(8,128)(2,1)S(1)} %get-tuple-element.99), channel_id=1, source_target_pairs={{0,16},{8,24},{16,0},{24,8},{1,17},{9,25},{17,1},{25,9},{2,18},{10... | collective-permute-start | bytes 1572872 | tf_op jit(solution)/shard_map/ppermute | solution.py:383
  146.3 24.4 %collective-permute-start.11 = (bf16[256,2048]{1,0:T(8,128)(2,1)S(1)}, bf16[256,2048]{1,0:T(8,128)(2,1)S(1)}, u32[]{:S(2)}, u32[]{:S(2)}) collective-permute-start(bf16[256,2048]{1,0:T(8,128)(2,1)S(1)} %pad_maximum_fusion), channel_id=1, source_target_pairs={{0,8},{8,0},{16,24},{24,16},{1,9},{9,1},{17,25},{25,17},{2,10},{10... | collective-permute-start | bytes 3145736 | tf_op jit(solution)/shard_map/ppermute | solution.py:380
  148.6 24.1 %collective-permute-start.13 = (bf16[256,2048]{1,0:T(8,128)(2,1)S(1)}, bf16[256,2048]{1,0:T(8,128)(2,1)S(1)}, u32[]{:S(2)}, u32[]{:S(2)}) collective-permute-start(bf16[256,2048]{1,0:T(8,128)(2,1)S(1)} %pad_maximum_fusion.1), channel_id=1, source_target_pairs={{0,16},{8,24},{16,0},{24,8},{1,17},{9,25},{17,1},{25,9},{2,18},{10... | collective-permute-start | bytes 3145736 | tf_op jit(solution)/shard_map/ppermute | solution.py:383
  176.5 24.1 %collective-permute-start.14 = (bf16[256,2048]{1,0:T(8,128)(2,1)S(1)}, bf16[256,2048]{1,0:T(8,128)(2,1)S(1)}, u32[]{:S(2)}, u32[]{:S(2)}) collective-permute-start(bf16[256,2048]{1,0:T(8,128)(2,1)S(1)} %get-tuple-element.91), channel_id=1, source_target_pairs={{0,8},{8,0},{16,24},{24,16},{1,9},{9,1},{17,25},{25,17},{2,10},{10... | collective-permute-start | bytes 3145736 | tf_op jit(solution)/shard_map/ppermute | solution.py:380
  213.6 23.7 %collective-permute-start.18 = (bf16[1024,512]{1,0:T(8,128)(2,1)S(1)}, bf16[1024,512]{1,0:T(8,128)(2,1)S(1)}, u32[]{:S(2)}, u32[]{:S(2)}) collective-permute-start(bf16[1024,512]{1,0:T(8,128)(2,1)S(1)} %copy-done), channel_id=1, source_target_pairs={{0,8},{8,0},{16,24},{24,16},{1,9},{9,1},{17,25},{25,17},{2,10},{10... | collective-permute-start | bytes 3145736 | tf_op jit(solution)/shard_map/ppermute | solution.py:380
  281.2 25.9 %collective-permute-start.23 = (bf16[256,2048]{1,0:T(8,128)(2,1)S(1)}, bf16[256,2048]{1,0:T(8,128)(2,1)S(1)}, u32[]{:S(2)}, u32[]{:S(2)}) collective-permute-start(bf16[256,2048]{1,0:T(8,128)(2,1)S(1)} %pad_maximum_fusion.2), channel_id=1, source_target_pairs={{0,8},{8,0},{16,24},{24,16},{1,9},{9,1},{17,25},{25,17},{2,10},{10... | collective-permute-start | bytes 3145736 | tf_op jit(solution)/shard_map/ppermute | solution.py:380
  285.9 23.2 %collective-permute-start.25 = (bf16[256,2048]{1,0:T(8,128)(2,1)S(1)}, bf16[256,2048]{1,0:T(8,128)(2,1)S(1)}, u32[]{:S(2)}, u32[]{:S(2)}) collective-permute-start(bf16[256,2048]{1,0:T(8,128)(2,1)S(1)} %pad_maximum_fusion.3), channel_id=1, source_target_pairs={{0,16},{8,24},{16,0},{24,8},{1,17},{9,25},{17,1},{25,9},{2,18},{10... | collective-permute-start | bytes 3145736 | tf_op jit(solution)/shard_map/ppermute | solution.py:383
  313.9 24.6 %collective-permute-start.26 = (bf16[256,2048]{1,0:T(8,128)(2,1)S(1)}, bf16[256,2048]{1,0:T(8,128)(2,1)S(1)}, u32[]{:S(2)}, u32[]{:S(2)}) collective-permute-start(bf16[256,2048]{1,0:T(8,128)(2,1)S(1)} %get-tuple-element.83), channel_id=1, source_target_pairs={{0,8},{8,0},{16,24},{24,16},{1,9},{9,1},{17,25},{25,17},{2,10},{10... | collective-permute-start | bytes 3145736 | tf_op jit(solution)/shard_map/ppermute | solution.py:380
  361.2 192.3 %reduce-scatter.9.cloned.1.call-start = ((), (), s32[]{:S(2)}) async-start(), calls=%async_computation.9 | async-start | bytes 9437184 | tf_op jit(solution)/shard_map/reduce_scatter | solution.py:464
  417.8 192.4 %reduce-scatter.7.cloned.1.call-start = ((), (), s32[]{:S(2)}) async-start(), calls=%async_computation.8 | async-start | bytes 7077888 | tf_op jit(solution)/shard_map/reduce_scatter | solution.py:464
  449.7 23.6 %collective-permute-start.34 = (bf16[256,2048]{1,0:T(8,128)(2,1)S(1)}, bf16[256,2048]{1,0:T(8,128)(2,1)S(1)}, u32[]{:S(2)}, u32[]{:S(2)}) collective-permute-start(bf16[256,2048]{1,0:T(8,128)(2,1)S(1)} %get-tuple-element.85), channel_id=1, source_target_pairs={{0,8},{8,0},{16,24},{24,16},{1,9},{9,1},{17,25},{25,17},{2,10},{10... | collective-permute-start | bytes 3145736 | tf_op jit(solution)/shard_map/ppermute | solution.py:380
  518.0 125.1 %reduce-scatter.11.cloned.1.call-start = ((), (), s32[]{:S(2)}) async-start(), calls=%async_computation.10 | async-start | bytes 1392640 | tf_op jit(solution)/shard_map/reduce_scatter | solution.py:461
  553.5 25.8 %collective-permute-start.47 = (bf16[256,2048]{1,0:T(8,128)(2,1)}, bf16[256,2048]{1,0:T(8,128)(2,1)S(1)}, u32[]{:S(2)}, u32[]{:S(2)}) collective-permute-start(bf16[256,2048]{1,0:T(8,128)(2,1)} %reduce-scatter.9.cloned.1.call-done.refs_1_), channel_id=1, source_target_pairs={{0,16},{8,24},{16,0},{24,8},{1,17},{9,25},{17,1},{25,9},{2,18},{10... | collective-permute-start | bytes 3145736 | tf_op jit(solution)/shard_map/ppermute | solution.py:383
  554.0 26.6 %collective-permute-start.46 = (bf16[256,2048]{1,0:T(8,128)(2,1)}, bf16[256,2048]{1,0:T(8,128)(2,1)}, u32[]{:S(2)}, u32[]{:S(2)}) collective-permute-start(bf16[256,2048]{1,0:T(8,128)(2,1)} %reduce-scatter.9.cloned.1.call-done.refs_1_), channel_id=1, source_target_pairs={{0,8},{8,0},{16,24},{24,16},{1,9},{9,1},{17,25},{25,17},{2,10},{10... | collective-permute-start | bytes 3145736 | tf_op jit(solution)/shard_map/ppermute | solution.py:380
  582.3 56.6 %collective-permute-start.43 = (bf16[256,2048]{1,0:T(8,128)(2,1)}, bf16[256,2048]{1,0:T(8,128)(2,1)}, u32[]{:S(2)}, u32[]{:S(2)}) collective-permute-start(bf16[256,2048]{1,0:T(8,128)(2,1)} %pad_maximum_fusion.6), channel_id=1, source_target_pairs={{0,8},{8,0},{16,24},{24,16},{1,9},{9,1},{17,25},{25,17},{2,10},{10... | collective-permute-start | bytes 3145736 | tf_op jit(solution)/shard_map/ppermute | solution.py:380
  583.4 55.5 %collective-permute-start.45 = (bf16[256,2048]{1,0:T(8,128)(2,1)}, bf16[256,2048]{1,0:T(8,128)(2,1)}, u32[]{:S(2)}, u32[]{:S(2)}) collective-permute-start(bf16[256,2048]{1,0:T(8,128)(2,1)} %pad_maximum_fusion.7), channel_id=1, source_target_pairs={{0,16},{8,24},{16,0},{24,8},{1,17},{9,25},{17,1},{25,9},{2,18},{10... | collective-permute-start | bytes 3145736 | tf_op jit(solution)/shard_map/ppermute | solution.py:383
  (83 other events, 991.4 us)
Sparse Core Ops, SparseCore 0:
  10.4 85.0 all-gather.4
  97.7 80.6 all-gather.6
  180.0 80.5 all-gather.8
  361.4 87.1 reduce-scatter.4
  451.3 87.9 reduce-scatter.8
  542.0 68.1 reduce-scatter.6
  613.1 26.5 reduce-scatter.10
